TPU v7x, 32 devices: a whole 2x2x4 slice. The times are simulated.
32 devices in a mesh: section: 4 (over y, x), dp: 2 (over core), mp: 4 (over z).
Axes of the slice: x: 2, y: 2, z: 4, core: 2. Of those that a mesh axis runs over, the one named last changes fastest.
Arguments:
- enc_hidden: bfloat16 [2, 128, 4096], P('dp', None, ('section', 'mp')), may hold values from -32 to 32
- enc_gain: float32 [4096], replicated, may hold values from 0.1 to 1.9
- key_weight: bfloat16 [4, 4096, 2048], P('section', None, 'mp'), may hold values from -0.09375 to 0.09375
- value_weight: bfloat16 [4, 4096, 2048], P('section', None, 'mp'), may hold values from -0.25 to 0.25
- queries: bfloat16 [2, 4, 256, 2048], P('dp', 'section', None, 'mp'), may hold values from -256 to 256
- out_grad: bfloat16 [2, 4, 256, 2048], P('dp', 'section', None, 'mp'), may hold values from -4 to 4
Outputs:
- attended: bfloat16 [2, 4, 256, 2048], P('dp', 'section', None, 'mp')
- query_grad: bfloat16 [2, 4, 256, 2048], P('dp', 'section', None, 'mp')
- hidden_grad: float32 [2, 128, 4096], P('dp', None, ('section', 'mp'))
- gain_grad: float32 [4096], P(('section', 'mp'))
All inputs are finite; a program needn't handle non-finite values.
Results may differ from a plain program's by a relative error of at most 0.02.
The roundings to bfloat16 on the way count: a program that leaves them out, or rounds other values in their place, can miss the bound.
Values may be sent and summed in bfloat16 or wider, within the bound.
No kernel may reach another device: no remote copies, remote signals or barrier semaphores. Data moves between devices by JAX's collectives and lax.ppermute only.
A program may use at most 64 MiB of HBM per device.

v0:
```python
import jax
import jax.numpy as jnp
from jax import lax
from jax.sharding import PartitionSpec as P

DH = 64


epsilon = 1e-06


def attend(key_value, queries, out_grad, columns):
    batch, source_length, _ = key_value.shape
    head_count = columns // DH
    factor = DH ** (-0.5)
    keys = key_value[..., :columns].reshape(batch, source_length, head_count, DH)
    values = key_value[..., columns:].reshape(batch, source_length, head_count, DH)
    asked = queries[:, 0].reshape(batch, -1, head_count, DH)
    upstream = out_grad[:, 0].reshape(batch, -1, head_count, DH)
    target_length = asked.shape[1]
    scores = jnp.einsum("sqhd,skhd->shqk", asked, keys, preferred_element_type=jnp.float32) * factor
    highest = jnp.max(scores, axis=-1, keepdims=True)
    raised = jnp.exp(scores - highest)
    shares = raised / jnp.sum(raised, axis=-1, keepdims=True)
    shares_low = shares.astype(jnp.bfloat16)
    attended = jnp.einsum(
        "shqk,skhd->sqhd", shares_low, values, preferred_element_type=jnp.float32
    ).astype(jnp.bfloat16)
    share_grad = jnp.einsum("sqhd,skhd->shqk", upstream, values, preferred_element_type=jnp.float32)
    value_grad = jnp.einsum(
        "shqk,sqhd->skhd", shares_low, upstream, preferred_element_type=jnp.float32
    ).astype(jnp.bfloat16)
    score_grad = (
        shares * (share_grad - jnp.sum(shares * share_grad, axis=-1, keepdims=True)) * factor
    )
    score_low = score_grad.astype(jnp.bfloat16)
    query_grad = jnp.einsum(
        "shqk,skhd->sqhd", score_low, keys, preferred_element_type=jnp.float32
    ).astype(jnp.bfloat16)
    key_grad = jnp.einsum(
        "shqk,sqhd->skhd", score_low, asked, preferred_element_type=jnp.float32
    ).astype(jnp.bfloat16)
    return (
        attended.reshape(batch, 1, target_length, columns),
        query_grad.reshape(batch, 1, target_length, columns),
        key_grad.reshape(batch, source_length, columns),
        value_grad.reshape(batch, source_length, columns),
    )


def per_device(enc_hidden, enc_gain, key_weight, value_weight, queries, out_grad):
    batch, source_length, own_columns = enc_hidden.shape
    width = key_weight.shape[1]
    columns = key_weight.shape[2]
    key_matrix = key_weight[0]
    value_matrix = value_weight[0]
    replicas = batch * lax.axis_size("dp")
    sections = lax.axis_size("section")
    groups = lax.axis_size("mp")
    first_column = lax.axis_index(("section", "mp")) * own_columns
    gain_own = lax.dynamic_slice_in_dim(enc_gain, first_column, own_columns, 0)
    widened = enc_hidden.astype(jnp.float32)
    squares = lax.psum(jnp.sum(widened * widened, axis=-1, keepdims=True), ("section", "mp"))
    inverse = lax.rsqrt(squares / width + epsilon)
    normed = widened * inverse
    own_memory = (normed * gain_own).astype(jnp.bfloat16)
    memory = lax.all_gather(own_memory, ("section", "mp"), axis=2, tiled=True)
    flat = memory.reshape(-1, width)
    keys = jnp.dot(flat, key_matrix, preferred_element_type=jnp.float32).astype(jnp.bfloat16)
    values = jnp.dot(flat, value_matrix, preferred_element_type=jnp.float32).astype(jnp.bfloat16)
    key_value = jnp.concatenate((keys, values), axis=-1).reshape(batch, source_length, 2 * columns)
    attended, query_grad, key_grad, value_grad = attend(key_value, queries, out_grad, columns)
    total = jnp.einsum("skc,dc->skd", key_grad, key_matrix, preferred_element_type=jnp.float32)
    head_part = (
        total
        + jnp.einsum("skc,dc->skd", value_grad, value_matrix, preferred_element_type=jnp.float32)
    ).reshape(batch, source_length, sections, groups, own_columns)
    layer_part = lax.psum_scatter(
        head_part.astype(jnp.bfloat16), "mp", scatter_dimension=3, tiled=True
    )
    own_grad = (
        lax.psum_scatter(layer_part, "section", scatter_dimension=2, tiled=True)
        .astype(jnp.float32)
        .reshape(batch, source_length, own_columns)
    )
    scaled = own_grad * gain_own
    mean_total = lax.psum(jnp.sum(scaled * normed, axis=-1, keepdims=True), ("section", "mp"))
    gain_total = lax.psum(jnp.sum(own_grad * normed, axis=(0, 1)), "dp")
    hidden_grad = inverse * (scaled - normed * (mean_total / width))
    gain_grad = gain_total / replicas
    return (attended, query_grad, hidden_grad, gain_grad)


def solution(mesh):
    in_specs = (
        P("dp", None, ("section", "mp")),
        P(),
        P("section", None, "mp"),
        P("section", None, "mp"),
        P("dp", "section", None, "mp"),
        P("dp", "section", None, "mp"),
    )
    out_specs = (
        P("dp", "section", None, "mp"),
        P("dp", "section", None, "mp"),
        P("dp", None, ("section", "mp")),
        P(("section", "mp")),
    )
    return jax.shard_map(
        per_device, mesh=mesh, in_specs=in_specs, out_specs=out_specs, check_vma=False
    )
```

profile of v0, /device:TPU:0, one launch (start us, length us, event | category | flops | bytes accessed | tf_op | source)
XLA Modules:
  0.0 253.4 jit_solution(6738457621057778831)
XLA Ops:
  7.2 0.9 fusion.40
  8.2 43.7 %psum.21 = f32[1,128,1]{1,2,0:T(1,128)S(1)} all-reduce(f32[1,128,1]{1,2,0:T(1,128)S(1)} %bitcast.127), channel_id=1, replica_groups=mesh['section'=4,'dp'=2,'mp'=4] {'section','mp'}, use_global_device_ids=true, to_apply=%region_1.0 | all-reduce | flops 128 | bytes 1024 | tf_op jit(solution)/shard_map/psum | solution.py:63
  51.9 0.8 dynamic_slice.3
  52.7 1.6 fusion.38
  54.3 1.1 copy.38
  55.4 1.1 copy.40
  56.5 49.2 %all-gather.2.cloned.1.call-done = bf16[1,128,4096]{2,1,0:T(8,128)(2,1)} async-done(((bf16[1,128,256]{2,1,0:T(8,128)(2,1)}), bf16[1,128,4096]{2,1,0:T(8,128)(2,1)}) %all-gather.2.cloned.1.call-update) | async-done | bytes 1048592 | tf_op jit(solution)/shard_map/all_gather | solution.py:67
  105.7 3.4 %fusion.20 = bf16[128,512]{1,0:T(8,128)(2,1)S(1)} fusion(bf16[1,4096,512]{2,1,0:T(8,128)(2,1)} %param.9, bf16[1,128,4096]{2,1,0:T(8,128)(2,1)} %all-gather.2.cloned.1.call-done), kind=kOutput, calls=%fused_computation.23 | convolution fusion | flops 536936448 | bytes 5373952 | tf_op jit(solution)/shard_map/dot_general | solution.py:70
  109.1 0.4 copy-done.1
  109.4 0.3 copy-done.2
  109.7 0.8 fusion.17
  110.8 1.5 fusion.49
  112.3 0.3 convolution_bitcast_fusion
  112.7 0.7 convolution_convert_fusion.2
  113.4 2.0 convolution_convert_fusion.3
  115.4 3.8 %fusion.6 = f32[128,4096]{1,0:T(8,128)S(1)} fusion(bf16[128,512]{0,1:T(8,128)(2,1)S(1)} %bitcast.121, bf16[1,4096,512]{2,1,0:T(8,128)(2,1)} %param.8), kind=kOutput, calls=%fused_computation.7 | convolution fusion | flops 536870912 | bytes 6422528 | tf_op jit(solution)/shard_map/skc,dc->skd/dot_general | solution.py:73
  119.3 1.5 fusion.2
  120.8 0.8 convert_element_type.98
  121.6 1.3 copy.44
  123.0 0.6 dynamic-slice
  123.6 50.1 %all-reduce.4.cloned.1.call-done = bf16[1,128,4,4,256]{4,1,3,2,0:T(8,128)(2,1)} async-done(((bf16[1,128,4,4,256]{4,1,3,2,0:T(8,128)(2,1)}), bf16[1,128,4,4,256]{4,1,3,2,0:T(8,128)(2,1)}) %all-reduce.4.cloned.1.call-update) | async-done | bytes 1048592
  173.7 2.3 constant_dynamic-slice_fusion
  176.1 1.6 convolution_convert_fusion.1
  177.7 0.8 copy.45
  178.6 2.0 convolution_convert_fusion
  180.6 0.8 copy.46
  181.4 18.8 %reduce-scatter.10.cloned.1.call-done = bf16[1,128,1,1,256]{4,1,3,2,0:T(8,128)(2,1)} async-done(((bf16[1,128,4,1,256]{4,1,3,2,0:T(8,128)(2,1)}), bf16[1,128,1,1,256]{4,1,3,2,0:T(8,128)(2,1)}) %reduce-scatter.10.cloned.1.call-update) | async-done | bytes 65552
  200.2 1.0 fusion.41
  201.3 41.0 %psum.22 = f32[1,128,1]{1,2,0:T(1,128)S(1)} all-reduce(f32[1,128,1]{1,2,0:T(1,128)S(1)} %bitcast.126), channel_id=1, replica_groups=mesh['section'=4,'dp'=2,'mp'=4] {'section','mp'}, use_global_device_ids=true, to_apply=%region_8.0 | all-reduce | flops 128 | bytes 1024 | tf_op jit(solution)/shard_map/psum | solution.py:87
  242.2 2.5 psum.23
  244.7 0.6 broadcast_multiply_fusion
  245.3 1.6 fusion.37
  (28 shorter events, 0.5 us)
Async XLA Ops:
  7.2 98.5 %all-gather.2.cloned.1.call-start = ((), (), s32[]{:S(2)}) async-start(), calls=%async_computation.1 | async-start | bytes 1114112 | tf_op jit(solution)/shard_map/all_gather | solution.py:67
  54.2 119.5 %all-reduce.4.cloned.1.call-start = ((), (), s32[]{:S(2)}) async-start(), calls=%async_computation.2 | async-start | bytes 2097152
  105.7 3.7 %copy-start.1 = (bf16[1,4096,512]{2,1,0:T(8,128)(2,1)S(1)}, bf16[1,4096,512]{2,1,0:T(8,128)(2,1)}, u32[]{:S(2)}) copy-start(bf16[1,4096,512]{2,1,0:T(8,128)(2,1)} %param.8) | copy-start | bytes 12582916
  105.7 4.0 %copy-start.2 = (bf16[1,128,4096]{2,1,0:T(8,128)(2,1)S(1)}, bf16[1,128,4096]{2,1,0:T(8,128)(2,1)}, u32[]{:S(2)}) copy-start(bf16[1,128,4096]{2,1,0:T(8,128)(2,1)} %all-gather.2.cloned.1.call-done) | copy-start | bytes 3145732
  110.8 4.5 %copy-start.4 = (bf16[1,128,512]{1,2,0:T(8,128)(2,1)}, bf16[1,128,512]{1,2,0:T(8,128)(2,1)S(1)}, u32[]{:S(2)}) copy-start(bf16[1,128,512]{1,2,0:T(8,128)(2,1)S(1)} %copy.37) | copy-start | bytes 393220
  112.3 3.1 %copy-start.7 = (f32[8,256]{1,0:T(8,128)}, f32[8,256]{1,0:T(8,128)S(1)}, u32[]{:S(2)}) copy-start(f32[8,256]{1,0:T(8,128)S(1)} %get-tuple-element.20) | copy-start | bytes 24580
  115.4 3.8 %copy-start = (bf16[1,4096,512]{2,1,0:T(8,128)(2,1)S(1)}, bf16[1,4096,512]{2,1,0:T(8,128)(2,1)}, u32[]{:S(2)}) copy-start(bf16[1,4096,512]{2,1,0:T(8,128)(2,1)} %param.9) | copy-start | bytes 12582916
  120.8 2.3 copy-start.6
  121.6 57.0 %copy-start.5 = (bf16[1,128,512]{1,2,0:T(8,128)(2,1)S(1)}, bf16[1,128,512]{1,2,0:T(8,128)(2,1)}, u32[]{:S(2)}) copy-start(bf16[1,128,512]{1,2,0:T(8,128)(2,1)} %copy-done.4) | copy-start | bytes 393220
  121.6 57.0 %copy-start.8 = (f32[8,256]{1,0:T(8,128)S(1)}, f32[8,256]{1,0:T(8,128)}, u32[]{:S(2)}) copy-start(f32[8,256]{1,0:T(8,128)} %copy-done.7) | copy-start | bytes 24580
  122.9 77.3 %reduce-scatter.10.cloned.1.call-start = ((), (), s32[]{:S(2)}) async-start(), calls=%async_computation.3 | async-start | bytes 327680
  177.7 22.5 %copy-start.3 = (bf16[1,128,256]{2,1,0:T(8,128)(2,1)S(1)}, bf16[1,128,256]{2,1,0:T(8,128)(2,1)}, u32[]{:S(2)}) copy-start(bf16[1,128,256]{2,1,0:T(8,128)(2,1)} %param.6) | copy-start | bytes 196612
Sparse Core Ops, SparseCore 0:
  54.4 51.2 all-gather.1
  123.1 50.6 all-reduce.3
  176.7 23.4 reduce-scatter.9
where the time goes:
time: 254 us; the launch traced here: 253 us
  waiting for transfers between devices  118 us (46%)
  blocking collectives  87.1 us (34%)
  matrix products  17.6 us (7%)
  between operations  14 us (6%)
  local copies, waits for them, and re-layouts  10.6 us (4%)
  other arithmetic  5.72 us (2%)
    unnamed x5, waiting for transfers between devices  69 us
    all_gather x1, waiting for transfers between devices, per_device(): memory = lax.all_gather(own_memory, ('section', 'mp'), axis=2, tiled=True)  49.2 us
    psum x1, blocking collectives, per_device(): lax.psum(jnp.sum(widened * widened, axis=-1, keepdims=True), ('section',...  43.7 us
    psum x1, blocking collectives, per_device(): lax.psum(jnp.sum(scaled * normed, axis=-1, keepdims=True), ('section', 'm...  41 us
    unnamed x24, local copies, waits for them, and re-layouts  7.49 us
  transfers between devices with their start and end apart: 3, of which 3 were waited for; matrix products, arithmetic and copies ran while one was open for 3% of the time, Pallas kernels for 0%

commit v1 on v0

v1 whole, which is shorter than its diff:
```python
import jax
import jax.numpy as jnp
from jax import lax
from jax.experimental import pallas as pl
from jax.experimental.pallas import tpu as pltpu
from jax.sharding import PartitionSpec as P

DH = 64
EPSILON = 1e-06
BLOCK = 256
EXTRA = 16
EXTRA_WIDTH = 256
F32 = jnp.float32
BF16 = jnp.bfloat16
VMEM = pl.BlockSpec(memory_space=pltpu.VMEM)
SMEM = pl.BlockSpec(memory_space=pltpu.SMEM)
HBM = pl.BlockSpec(memory_space=pltpu.HBM)

NN = (((1,), (0,)), ((), ()))
NT = (((1,), (1,)), ((), ()))


def dot(a, b, dims=NN):
    return lax.dot_general(a, b, dims, preferred_element_type=F32)


def split_rows(row):
    high = row.astype(BF16)
    low = (row - high.astype(F32)).astype(BF16)
    return high, low


def in_vmem(array):
    return pltpu.with_memory_space_constraint(array, pltpu.VMEM)


def in_hbm(array):
    return pltpu.with_memory_space_constraint(array, pltpu.HBM)


def load_weights(place, wk, wv, gain, sections, slots):
    width, columns = wk.shape
    blocks = sections * slots
    block = width // blocks

    def kernel(place_ref, wk_ref, wv_ref, gain_ref, wk_out, wv_out, gain_out, sems):
        copies = []
        for j in range(sections):
            for i in range(slots):
                n = j * slots + i
                b = lax.bitwise_xor(place_ref[0], j) * slots + lax.bitwise_xor(place_ref[1], i)
                source = pl.ds(pl.multiple_of(b * block, block), block)
                copies += [
                    pltpu.make_async_copy(wk_ref.at[source, :], wk_out.at[n], sems.at[0, n]),
                    pltpu.make_async_copy(wv_ref.at[source, :], wv_out.at[n], sems.at[1, n]),
                ]
                gain_out[n] = gain_ref[b]
        for copy in copies:
            copy.start()
        for copy in copies:
            copy.wait()

    return pl.pallas_call(
        kernel,
        out_shape=(
            pltpu.VMEM((blocks, block, columns), BF16),
            pltpu.VMEM((blocks, block, columns), BF16),
            pltpu.VMEM((blocks, 1, block), F32),
        ),
        in_specs=[SMEM, HBM, HBM, VMEM],
        out_specs=(VMEM, VMEM, VMEM),
        scratch_shapes=[pltpu.SemaphoreType.DMA((2, blocks))],
        compiler_params=pltpu.CompilerParams(vmem_limit_bytes=4 << 20),
        cost_estimate=pl.CostEstimate(
            flops=0, bytes_accessed=8 * width * columns, transcendentals=0
        ),
        name="load_weights",
    )(place, in_hbm(wk), in_hbm(wv), gain)


def attend(x, gain, wk, wv, q, g):
    sections = len(x)
    slots, rows, block = x[0].shape
    length, columns = q.shape
    width = sections * slots * block
    pair = 2 * DH
    pairs = columns // pair
    factor = DH ** (-0.5)

    def kernel(*refs):
        x_refs = refs[:sections]
        (gain_ref, wk_ref, wv_ref, q_ref, g_ref, low_ref, grad_low_ref, keys_ref, values_ref,
         kg_ref, vg_ref, inverse_ref, extra_ref, memory_buf) = refs[sections:]

        squares = jnp.zeros((rows, block), F32)
        for x_ref in x_refs:
            for i in range(slots):
                wide = x_ref[i].astype(F32)
                squares += wide * wide
        inverse = lax.rsqrt(jnp.sum(squares, axis=-1, keepdims=True) / width + EPSILON)
        inverse_ref[...] = jnp.broadcast_to(inverse, inverse_ref.shape)

        keys = jnp.zeros((rows, columns), F32)
        values = jnp.zeros((rows, columns), F32)
        for j in range(sections):
            for i in range(slots):
                memory = x_refs[j][i].astype(F32) * inverse * gain_ref[j * slots + i]
                memory_buf[:, i * block:(i + 1) * block] = memory.astype(BF16)
            span = slice(j * slots, (j + 1) * slots)
            keys += dot(memory_buf[...], wk_ref[span].reshape(slots * block, columns))
            values += dot(memory_buf[...], wv_ref[span].reshape(slots * block, columns))
        keys_ref[...] = keys.astype(BF16)
        values_ref[...] = values.astype(BF16)

        first = lax.broadcasted_iota(jnp.int32, (rows, pair), 1) < DH
        zero = jnp.zeros((rows, pair), BF16)
        c_sum = jnp.zeros((rows, pair), F32)
        for p in range(pairs):
            at = slice(p * pair, (p + 1) * pair)
            k, v = keys_ref[:, at], values_ref[:, at]
            q, g = q_ref[:, at], g_ref[:, at]
            k_two = jnp.concatenate((jnp.where(first, k, zero), jnp.where(first, zero, k)), axis=0)
            v_two = jnp.concatenate((jnp.where(first, v, zero), jnp.where(first, zero, v)), axis=0)
            scores = dot(k_two, q, NT)
            share_grad = dot(v_two, g, NT)
            for h in range(2):
                half = slice(h * rows, (h + 1) * rows)
                score = scores[half]
                raised = jnp.exp((score - jnp.max(score, axis=0, keepdims=True)) * factor)
                shares = raised * (1.0 / jnp.sum(raised, axis=0, keepdims=True))
                low_ref[p, half, :] = shares.astype(BF16)
                grads = share_grad[half]
                mean = jnp.sum(shares * grads, axis=0, keepdims=True)
                grad_low_ref[p, half, :] = (shares * (grads - mean) * factor).astype(BF16)
            vg = dot(low_ref[p], g)
            kg = dot(grad_low_ref[p], q)
            vg = jnp.where(first, vg[:rows], vg[rows:]).astype(BF16)
            kg = jnp.where(first, kg[:rows], kg[rows:]).astype(BF16)
            vg_ref[:, at] = vg
            kg_ref[:, at] = kg
            c_sum += kg.astype(F32) * k.astype(F32) + vg.astype(F32) * v.astype(F32)

        row = jnp.sum(c_sum.T, axis=0, keepdims=True)
        row = jnp.concatenate((row, jnp.zeros((1, EXTRA_WIDTH - rows), F32)), axis=1)
        high, low = split_rows(row)
        blank = jnp.zeros((EXTRA - 2, EXTRA_WIDTH), BF16)
        extra_ref[...] = jnp.concatenate((high, low, blank), axis=0)

    return pl.pallas_call(
        kernel,
        out_shape=(
            pltpu.VMEM((pairs, 2 * rows, length), BF16),
            pltpu.VMEM((pairs, 2 * rows, length), BF16),
            pltpu.VMEM((rows, columns), BF16),
            pltpu.VMEM((rows, columns), BF16),
            pltpu.VMEM((rows, columns), BF16),
            pltpu.VMEM((rows, columns), BF16),
            pltpu.VMEM((rows, 128), F32),
            pltpu.VMEM((EXTRA, EXTRA_WIDTH), BF16),
        ),
        in_specs=[VMEM] * (sections + 5),
        out_specs=(VMEM,) * 8,
        scratch_shapes=[pltpu.VMEM((rows, slots * block), BF16)],
        compiler_params=pltpu.CompilerParams(vmem_limit_bytes=16 << 20),
        cost_estimate=pl.CostEstimate(
            flops=4 * rows * width * columns + 16 * length * rows * columns,
            bytes_accessed=8 * width * columns,
            transcendentals=length * rows * columns // DH,
        ),
        name="attend",
    )(*x, gain, in_vmem(wk), in_vmem(wv), q, g)


def outputs(low, grad_low, keys, values):
    pairs, both, length = low.shape
    rows, columns = keys.shape
    pair = columns // pairs

    def kernel(low_ref, grad_low_ref, keys_ref, values_ref, attended_ref, query_grad_ref):
        first = lax.broadcasted_iota(jnp.int32, (rows, pair), 1) < DH
        zero = jnp.zeros((rows, pair), BF16)
        for p in range(pairs):
            at = slice(p * pair, (p + 1) * pair)
            for part, weight, out in (
                (low_ref, values_ref, attended_ref), (grad_low_ref, keys_ref, query_grad_ref)
            ):
                w = weight[:, at]
                two = jnp.concatenate((jnp.where(first, w, zero), jnp.where(first, zero, w)), axis=0)
                out[:, at] = dot(two.T, part[p]).T.astype(BF16)

    return pl.pallas_call(
        kernel,
        out_shape=(jax.ShapeDtypeStruct((length, columns), BF16),) * 2,
        in_specs=[VMEM] * 4,
        out_specs=(VMEM, VMEM),
        compiler_params=pltpu.CompilerParams(vmem_limit_bytes=8 << 20),
        cost_estimate=pl.CostEstimate(
            flops=8 * length * rows * columns,
            bytes_accessed=4 * length * columns + 4 * pairs * both * length,
            transcendentals=0,
        ),
        name="outputs",
    )(in_vmem(low), in_vmem(grad_low), in_vmem(keys), in_vmem(values))


def project(kg, vg, extra, wk, wv, j, slots):
    rows, columns = kg.shape
    block = wk.shape[1]

    def kernel(kg_ref, vg_ref, extra_ref, wk_ref, wv_ref, out_ref):
        kg, vg = kg_ref[...], vg_ref[...]
        for i in range(slots):
            n = j * slots + i
            part = dot(kg, wk_ref[n], NT) + dot(vg, wv_ref[n], NT)
            out_ref[i * rows:(i + 1) * rows, :] = part.astype(BF16)
        out_ref[slots * rows:, :] = extra_ref[...]

    return pl.pallas_call(
        kernel,
        out_shape=jax.ShapeDtypeStruct((slots * rows + EXTRA, block), BF16),
        in_specs=[VMEM] * 5,
        out_specs=VMEM,
        compiler_params=pltpu.CompilerParams(vmem_limit_bytes=4 << 20),
        cost_estimate=pl.CostEstimate(
            flops=4 * rows * columns * slots * block,
            bytes_accessed=4 * slots * block * columns,
            transcendentals=0,
        ),
        name="project",
    )(in_vmem(kg), in_vmem(vg), in_vmem(extra), in_vmem(wk), in_vmem(wv))


def sum_sections(chunks, slots, rows, c_rows):
    count = len(chunks)
    block = chunks[0].shape[1]

    def kernel(*refs):
        parts, outs = refs[:count], refs[count:]

        def total(start, size):
            acc = parts[0][start:start + size, :].astype(F32)
            for part in parts[1:]:
                acc += part[start:start + size, :].astype(F32)
            return acc

        extra = total(slots * rows, EXTRA)
        high, low = split_rows(extra[:c_rows] + extra[c_rows:2 * c_rows])
        blank = jnp.zeros((EXTRA - 2 * c_rows, block), BF16)
        tail = jnp.concatenate((high, low, blank), axis=0)
        for i in range(slots):
            outs[i][:rows, :] = total(i * rows, rows).astype(BF16)
            outs[i][rows:, :] = tail

    return pl.pallas_call(
        kernel,
        out_shape=(jax.ShapeDtypeStruct((rows + EXTRA, block), BF16),) * slots,
        in_specs=[VMEM] * count,
        out_specs=(VMEM,) * slots,
        compiler_params=pltpu.CompilerParams(vmem_limit_bytes=8 << 20),
        name="sum_sections",
    )(*chunks)


def finish(parts, hidden, gain, inverse, width, c_rows):
    count = len(parts)
    rows, block = hidden.shape

    def kernel(hidden_ref, gain_ref, inverse_ref, *refs):
        parts, (grad_ref, gain_grad_ref) = refs[:count], refs[count:]
        total = parts[0][...].astype(F32)
        for part in parts[1:]:
            total += part[...].astype(F32)
        extra = total[rows:]
        c = extra[:c_rows] + extra[c_rows:2 * c_rows]
        c = jnp.concatenate([c[n:n + 1] for n in range(c_rows)], axis=1)[:, :rows]
        mean = (jnp.broadcast_to(c, (rows, rows)) / width).T[:, 0:1]
        total = total[:rows]
        inverse = inverse_ref[:, 0:1]
        normed = hidden_ref[...].astype(F32) * inverse
        gain_grad_ref[...] = jnp.sum(total * normed, axis=0, keepdims=True)
        grad_ref[...] = inverse * (total * gain_ref[0] - normed * mean)

    return pl.pallas_call(
        kernel,
        out_shape=(
            jax.ShapeDtypeStruct((rows, block), F32),
            jax.ShapeDtypeStruct((1, block), F32),
        ),
        in_specs=[VMEM] * (count + 3),
        out_specs=(VMEM, VMEM),
        compiler_params=pltpu.CompilerParams(vmem_limit_bytes=8 << 20),
        name="finish",
    )(hidden, gain, in_vmem(inverse), *parts)


def partners(axis, array_of, size):
    order = sorted(range(1, size), key=lambda j: -bin(j).count("1"))
    got = {}
    for j in order:
        got[j] = lax.ppermute(array_of(j), axis, [(d, d ^ j) for d in range(size)])
    return [got[j] for j in range(1, size)]


def swapped(array, axis, mine):
    return jnp.stack(
        [
            lax.dynamic_index_in_dim(array, jnp.bitwise_xor(mine, i), axis, False)
            for i in range(array.shape[axis])
        ],
        axis,
    )


def per_device(enc_hidden, enc_gain, key_weight, value_weight, queries, out_grad):
    own = enc_hidden[0]
    rows, own_columns = own.shape
    wk, wv = key_weight[0], value_weight[0]
    width, columns = wk.shape
    sections = lax.axis_size("section")
    groups = lax.axis_size("mp")
    replicas = lax.axis_size("dp")
    section = lax.axis_index("section")
    mp = lax.axis_index("mp")
    direct = own_columns == BLOCK
    c_rows = max(rows // own_columns, 1)

    stack = jnp.stack([own] + partners("mp", lambda j: own, groups))
    gain = enc_gain.reshape(width // BLOCK, 1, BLOCK)
    if direct:
        slots = groups
        x = [stack] + partners("section", lambda j: stack, sections)
        place = jnp.stack((section, mp))
    else:
        slots = 4
        x = lax.all_gather(stack, "section", axis=0)
        x = swapped(x, 1, mp).transpose(2, 0, 1, 3).reshape(rows, -1, slots, BLOCK)
        x = list(x.transpose(1, 2, 0, 3))
        place = jnp.zeros(2, jnp.int32)
    wk, wv, gain = load_weights(place, wk, wv, gain, len(x), slots)
    low, grad_low, keys, values, kg, vg, inverse, extra = attend(
        x, gain, wk, wv, queries[0, 0], out_grad[0, 0]
    )

    if direct:
        def chunk(j):
            return project(kg, vg, extra, wk, wv, j, slots)
    else:
        whole = [project(kg, vg, extra, wk, wv, n, slots)[:-EXTRA] for n in range(len(x))]
        whole = jnp.stack(whole).reshape(-1, rows, BLOCK).transpose(1, 0, 2)
        whole = whole.reshape(rows, sections, groups, own_columns).transpose(1, 2, 0, 3)
        whole = swapped(whole, 1, mp).reshape(sections, groups * rows, own_columns)
        tail = extra[:2, : c_rows * own_columns].reshape(2 * c_rows, own_columns)
        tail = jnp.concatenate((tail, jnp.zeros((EXTRA - 2 * c_rows, own_columns), BF16)))
        gain = lax.dynamic_slice_in_dim(
            enc_gain, (section * groups + mp) * own_columns, own_columns, 0
        ).reshape(1, 1, own_columns)

        def chunk(j):
            body = lax.dynamic_index_in_dim(whole, jnp.bitwise_xor(section, j), 0, False)
            return jnp.concatenate((body, tail))

    got = partners("section", chunk, sections)
    summed = sum_sections([chunk(0)] + got, groups, rows, c_rows)
    attended, query_grad = outputs(low, grad_low, keys, values)
    got = partners("mp", lambda j: summed[j], groups)
    hidden_grad, gain_part = finish([summed[0]] + got, own, gain, inverse, width, c_rows)
    if replicas == 2:
        gain_total = gain_part + lax.ppermute(gain_part, "dp", [(0, 1), (1, 0)])
    else:
        gain_total = lax.psum(gain_part, "dp")
    return (
        attended[None, None],
        query_grad[None, None],
        hidden_grad[None],
        gain_total[0] / replicas,
    )


def solution(mesh):
    in_specs = (
        P("dp", None, ("section", "mp")),
        P(),
        P("section", None, "mp"),
        P("section", None, "mp"),
        P("dp", "section", None, "mp"),
        P("dp", "section", None, "mp"),
    )
    out_specs = (
        P("dp", "section", None, "mp"),
        P("dp", "section", None, "mp"),
        P("dp", None, ("section", "mp")),
        P(("section", "mp")),
    )
    return jax.shard_map(
        per_device, mesh=mesh, in_specs=in_specs, out_specs=out_specs, check_vma=False
    )
```

time: 254 us -> 59.3 us (0.23)
  waiting for transfers between devices: 118 us -> 26.3 us
  blocking collectives: 87.1 us -> 0 us
  matrix products: 17.6 us -> 0 us
  starting transfers between devices: 0.12 us -> 17.3 us
  between operations: 14 us -> 0.72 us
  Pallas kernels: 0 us -> 12.5 us
  local copies, waits for them, and re-layouts: 10.6 us -> 0.73 us
  other arithmetic: 5.72 us -> 1.52 us
    psum x3 -> x0, blocking collectives: 87.1 us -> none  [the longest x1 43.7 us: per_device(): lax.psum(jnp.sum(widened * widened, axis=-1, keepdims=True), ('section',...]
    unnamed x5 -> x0, waiting for transfers between devices: 69 us -> none
    all_gather x1 -> x0, waiting for transfers between devices: 49.2 us -> none  [per_device(): memory = lax.all_gather(own_memory, ('section', 'mp'), axis=2, tiled=True)]
    ppermute x0 -> x13, waiting for transfers between devices: none -> 26.3 us  [the longest x12 26.3 us: partners(): got[j] = lax.ppermute(array_of(j), axis, [(d, d ^ j) for d in range(size)])]
    ppermute x0 -> x13, starting transfers between devices: none -> 17.3 us  [the longest x12 17.3 us: partners(): got[j] = lax.ppermute(array_of(j), axis, [(d, d ^ j) for d in range(size)])]
    dot_general x9 -> x0, matrix products: 16.1 us -> none  [the longest x1 3.83 us: per_device(): jnp.einsum('skc,dc->skd', key_grad, key_matrix, preferred_element_type=jn...]
    pallas_call x0 -> x9, Pallas kernels: none -> 12.5 us  [the longest x1 4.19 us: load_weights(): pl.pallas_call(kernel, out_shape=(pltpu.VMEM((blocks, block, columns), BF...]
    unnamed x24 -> x8, local copies, waits for them, and re-layouts: 7.49 us -> 0.73 us
  transfers between devices with their start and end apart: 3 -> 13, of which waited for: 3 -> 9; matrix products, arithmetic and copies ran while one was open for 3% -> 0% of each run, Pallas kernels for 0% -> 11%
where the time goes in v1:
time: 59.3 us; the launch traced here: 59 us
  waiting for transfers between devices  26.3 us (44%)
  starting transfers between devices  17.3 us (29%)
  Pallas kernels  12.5 us (21%)
  other arithmetic  1.52 us (3%)
  local copies, waits for them, and re-layouts  0.73 us (1%)
  between operations  0.72 us (1%)
    ppermute x12, waiting for transfers between devices, partners(): got[j] = lax.ppermute(array_of(j), axis, [(d, d ^ j) for d in range(size)])  26.3 us
    ppermute x12, starting transfers between devices, partners(): got[j] = lax.ppermute(array_of(j), axis, [(d, d ^ j) for d in range(size)])  17.3 us
    pallas_call x1, Pallas kernels, load_weights(): pl.pallas_call(kernel, out_shape=(pltpu.VMEM((blocks, block, columns), BF...  4.19 us
    pallas_call x4, Pallas kernels, project(): pl.pallas_call(kernel, out_shape=jax.ShapeDtypeStruct((slots * rows + EXT...  3.21 us
    pallas_call x1, Pallas kernels, attend(): pl.pallas_call(kernel, out_shape=(pltpu.VMEM((pairs, 2 * rows, length), B...  2.82 us
    pallas_call x1, Pallas kernels, outputs(): pl.pallas_call(kernel, out_shape=(jax.ShapeDtypeStruct((length, columns),...  1.27 us
  transfers between devices with their start and end apart: 13, of which 9 were waited for; matrix products, arithmetic and copies ran while one was open for 0% of the time, Pallas kernels for 11%

profile of v1, /device:TPU:0, one launch (start us, length us, event | category | flops | bytes accessed | tf_op | source)
XLA Modules:
  0.0 59.0 jit_solution(8281734054325788946)
XLA Ops:
  0.6 5.1 %collective-permute-start.2 = (bf16[128,256]{1,0:T(8,128)(2,1)}, bf16[128,256]{1,0:T(8,128)(2,1)S(1)}, u32[]{:S(2)}, u32[]{:S(2)}) collective-permute-start(bf16[128,256]{1,0:T(8,128)(2,1)} %bitcast.17), channel_id=1, source_target_pairs={{0,3},{1,2},{2,1},{3,0},{4,7},{5,6},{6,5},{7,4},{8,11},{9,10},{10,... | collective-permute-start | bytes 196616 | tf_op jit(solution)/shard_map/ppermute | solution.py:300
  5.7 0.6 %collective-permute-start = (bf16[128,256]{1,0:T(8,128)(2,1)}, bf16[128,256]{1,0:T(8,128)(2,1)S(1)}, u32[]{:S(2)}, u32[]{:S(2)}) collective-permute-start(bf16[128,256]{1,0:T(8,128)(2,1)} %bitcast.19), channel_id=1, source_target_pairs={{0,1},{1,0},{2,3},{3,2},{4,5},{5,4},{6,7},{7,6},{8,9},{9,8},{10,11... | collective-permute-start | bytes 196616 | tf_op jit(solution)/shard_map/ppermute | solution.py:300
  6.4 2.2 %collective-permute-done.2 = bf16[128,256]{1,0:T(8,128)(2,1)S(1)} collective-permute-done((bf16[128,256]{1,0:T(8,128)(2,1)}, bf16[128,256]{1,0:T(8,128)(2,1)S(1)}, u32[]{:S(2)}, u32[]{:S(2)}) %collective-permute-start.2) | collective-permute-done | bytes 65568 | tf_op jit(solution)/shard_map/ppermute | solution.py:300
  8.6 3.0 %collective-permute-done.1 = bf16[128,256]{1,0:T(8,128)(2,1)S(1)} collective-permute-done((bf16[128,256]{1,0:T(8,128)(2,1)}, bf16[128,256]{1,0:T(8,128)(2,1)S(1)}, u32[]{:S(2)}, u32[]{:S(2)}) %collective-permute-start.1) | collective-permute-done | bytes 65568 | tf_op jit(solution)/shard_map/ppermute | solution.py:300
  11.6 0.9 %pad_maximum_fusion.refs_0_ = bf16[4,128,256]{2,1,0:T(8,128)(2,1)S(1)} fusion(bf16[1,128,256]{2,1,0:T(8,128)(2,1)S(1)} %bitcast.24, bf16[1,128,256]{2,1,0:T(8,128)(2,1)S(1)} %bitcast.25, bf16[1,128,256]{2,1,0:T(8,128)(2,1)S(1)} %bitcast.26, bf16[1,128,256]{2,1,0:T(8,128)(2,1)} %param.6), kind=kLoop, calls=%fused_computation | loop fusion | flops 393216 | bytes 524288 | tf_op jit(solution)/shard_map/stack | solution.py:327
  12.4 2.5 %collective-permute-start.5 = (bf16[4,128,256]{2,1,0:T(8,128)(2,1)S(1)}, bf16[4,128,256]{2,1,0:T(8,128)(2,1)S(1)}, u32[]{:S(2)}, u32[]{:S(2)}) collective-permute-start(bf16[4,128,256]{2,1,0:T(8,128)(2,1)S(1)} %pad_maximum_fusion.refs_0_), channel_id=1, source_target_pairs={{0,24},{8,16},{16,8},{24,0},{1,25},{9,17},{17,9},{25,1},{2,26},{10... | collective-permute-start | bytes 786440 | tf_op jit(solution)/shard_map/ppermute | solution.py:300
  15.0 0.5 collective-permute-start.4
  15.5 0.5 collective-permute-start.3
  16.0 0.1 pad_add_fusion.place_ref
  16.1 0.7 %copy-done.3 = f32[4096]{0:T(1024)S(1)} copy-done((f32[4096]{0:T(1024)S(1)}, f32[4096]{0:T(1024)}, u32[]{:S(2)}) %copy-start.3) | copy-done | bytes 16408
  16.8 4.2 %load_weights.1 = (bf16[16,256,512]{2,1,0:T(8,128)(2,1)S(1)}, bf16[16,256,512]{2,1,0:T(8,128)(2,1)S(1)}, f32[16,1,256]{2,1,0:T(1,128)S(1)}) custom-call(s32[2]{0:T(128)S(1)} %pad_add_fusion.place_ref, bf16[4096,512]{1,0:T(8,128)(2,1)} %bitcast.22, bf16[4096,512]{1,0:T(8,128)(2,1)} %bitcast.23, f32[16,1,256]{2,1,0:T(1,128)S(1)} %bitcast.21), custom_call_target="tpu_custom_call" | custom-call | bytes 16777216 | tf_op jit(solution)/shard_map/load_weights/pallas_call | solution.py:63
  21.0 1.7 %collective-permute-done.5.refs_3_ = bf16[4,128,256]{2,1,0:T(8,128)(2,1)S(1)} collective-permute-done((bf16[4,128,256]{2,1,0:T(8,128)(2,1)S(1)}, bf16[4,128,256]{2,1,0:T(8,128)(2,1)S(1)}, u32[]{:S(2)}, u32[]{:S(2)}) %collective-permute-start.5) | collective-permute-done | bytes 262176 | tf_op jit(solution)/shard_map/ppermute | solution.py:300
  22.7 4.2 %collective-permute-done.4.refs_2_ = bf16[4,128,256]{2,1,0:T(8,128)(2,1)S(1)} collective-permute-done((bf16[4,128,256]{2,1,0:T(8,128)(2,1)S(1)}, bf16[4,128,256]{2,1,0:T(8,128)(2,1)S(1)}, u32[]{:S(2)}, u32[]{:S(2)}) %collective-permute-start.4) | collective-permute-done | bytes 262176 | tf_op jit(solution)/shard_map/ppermute | solution.py:300
  26.9 0.3 collective-permute-done.3.refs_1_
  27.2 2.8 %attend.1 = (bf16[4,256,256]{2,1,0:T(8,128)(2,1)S(1)}, bf16[4,256,256]{2,1,0:T(8,128)(2,1)S(1)}, bf16[128,512]{1,0:T(8,128)(2,1)S(1)}, bf16[128,512]{1,0:T(8,128...) custom-call(bf16[4,128,256]{2,1,0:T(8,128)(2,1)S(1)} %pad_maximum_fu, ...), custom_call_target="tpu_custom_call" | custom-call | flops 1342177280 | bytes 16777216 | tf_op jit(solution)/shard_map/attend/pallas_call | solution.py:149
  30.0 0.8 %project.7 = bf16[528,256]{1,0:T(8,128)(2,1)S(1)} custom-call(bf16[128,512]{1,0:T(8,128)(2,1)S(1)} %get-tuple-element.33.kg_ref, bf16[128,512]{1,0:T(8,128)(2,1)S(1)} %get-tuple-element.34.vg_ref, bf16[16,256]{1,0:T(8,128)(2,1)S(1)} %get-tuple-element.35.extra_ref, bf16[16,256,512]{2,1,0:T(8,128)(2,1)S(1)} %get-tuple-element.24.refs_5_.wk_ref, ...), custom_call_target="tpu_custom_call" | custom-call | flops 268435456 | bytes 2097152 | tf_op jit(solution)/shard_map/project/pallas_call | solution.py:218
  30.8 0.8 %project.6 = bf16[528,256]{1,0:T(8,128)(2,1)S(1)} custom-call(bf16[128,512]{1,0:T(8,128)(2,1)S(1)} %get-tuple-element.33.kg_ref, bf16[128,512]{1,0:T(8,128)(2,1)S(1)} %get-tuple-element.34.vg_ref, bf16[16,256]{1,0:T(8,128)(2,1)S(1)} %get-tuple-element.35.extra_ref, bf16[16,256,512]{2,1,0:T(8,128)(2,1)S(1)} %get-tuple-element.24.refs_5_.wk_ref, ...), custom_call_target="tpu_custom_call" | custom-call | flops 268435456 | bytes 2097152 | tf_op jit(solution)/shard_map/project/pallas_call | solution.py:218
  31.6 0.8 %project.5 = bf16[528,256]{1,0:T(8,128)(2,1)S(1)} custom-call(bf16[128,512]{1,0:T(8,128)(2,1)S(1)} %get-tuple-element.33.kg_ref, bf16[128,512]{1,0:T(8,128)(2,1)S(1)} %get-tuple-element.34.vg_ref, bf16[16,256]{1,0:T(8,128)(2,1)S(1)} %get-tuple-element.35.extra_ref, bf16[16,256,512]{2,1,0:T(8,128)(2,1)S(1)} %get-tuple-element.24.refs_5_.wk_ref, ...), custom_call_target="tpu_custom_call" | custom-call | flops 268435456 | bytes 2097152 | tf_op jit(solution)/shard_map/project/pallas_call | solution.py:218
  32.5 1.5 %collective-permute-start.6 = (bf16[528,256]{1,0:T(8,128)(2,1)S(1)}, bf16[528,256]{1,0:T(8,128)(2,1)S(1)}, u32[]{:S(2)}, u32[]{:S(2)}) collective-permute-start(bf16[528,256]{1,0:T(8,128)(2,1)S(1)} %project.5), channel_id=1, source_target_pairs={{0,8},{8,0},{16,24},{24,16},{1,9},{9,1},{17,25},{25,17},{2,10},{10... | collective-permute-start | bytes 811016 | tf_op jit(solution)/shard_map/ppermute | solution.py:300
  34.0 0.6 %collective-permute-start.7 = (bf16[528,256]{1,0:T(8,128)(2,1)S(1)}, bf16[528,256]{1,0:T(8,128)(2,1)S(1)}, u32[]{:S(2)}, u32[]{:S(2)}) collective-permute-start(bf16[528,256]{1,0:T(8,128)(2,1)S(1)} %project.6), channel_id=1, source_target_pairs={{0,16},{8,24},{16,0},{24,8},{1,17},{9,25},{17,1},{25,9},{2,18},{10... | collective-permute-start | bytes 811016 | tf_op jit(solution)/shard_map/ppermute | solution.py:300
  34.6 1.4 %collective-permute-start.8 = (bf16[528,256]{1,0:T(8,128)(2,1)S(1)}, bf16[528,256]{1,0:T(8,128)(2,1)S(1)}, u32[]{:S(2)}, u32[]{:S(2)}) collective-permute-start(bf16[528,256]{1,0:T(8,128)(2,1)S(1)} %project.7), channel_id=1, source_target_pairs={{0,24},{8,16},{16,8},{24,0},{1,25},{9,17},{17,9},{25,1},{2,26},{10... | collective-permute-start | bytes 811016 | tf_op jit(solution)/shard_map/ppermute | solution.py:300
  36.0 0.8 %project.4.refs_0_ = bf16[528,256]{1,0:T(8,128)(2,1)S(1)} custom-call(bf16[128,512]{1,0:T(8,128)(2,1)S(1)} %get-tuple-element.33.kg_ref, bf16[128,512]{1,0:T(8,128)(2,1)S(1)} %get-tuple-element.34.vg_ref, bf16[16,256]{1,0:T(8,128)(2,1)S(1)} %get-tuple-element.35.extra_ref, bf16[16,256,512]{2,1,0:T(8,128)(2,1)S(1)} %get-tuple-element.24.refs_5_.wk_ref, ...), custom_call_target="tpu_custom_call" | custom-call | flops 268435456 | bytes 2097152 | tf_op jit(solution)/shard_map/project/pallas_call | solution.py:218
  36.8 5.1 %collective-permute-done.6.refs_1_ = bf16[528,256]{1,0:T(8,128)(2,1)S(1)} collective-permute-done((bf16[528,256]{1,0:T(8,128)(2,1)S(1)}, bf16[528,256]{1,0:T(8,128)(2,1)S(1)}, u32[]{:S(2)}, u32[]{:S(2)}) %collective-permute-start.6) | collective-permute-done | bytes 270368 | tf_op jit(solution)/shard_map/ppermute | solution.py:300
  41.9 5.9 %collective-permute-done.7.refs_2_ = bf16[528,256]{1,0:T(8,128)(2,1)S(1)} collective-permute-done((bf16[528,256]{1,0:T(8,128)(2,1)S(1)}, bf16[528,256]{1,0:T(8,128)(2,1)S(1)}, u32[]{:S(2)}, u32[]{:S(2)}) %collective-permute-start.7) | collective-permute-done | bytes 270368 | tf_op jit(solution)/shard_map/ppermute | solution.py:300
  47.8 0.1 sum_sections.1
  48.1 2.0 %collective-permute-start.10 = (bf16[144,256]{1,0:T(8,128)(2,1)S(1)}, bf16[144,256]{1,0:T(8,128)(2,1)S(1)}, u32[]{:S(2)}, u32[]{:S(2)}) collective-permute-start(bf16[144,256]{1,0:T(8,128)(2,1)S(1)} %get-tuple-element.38), channel_id=1, source_target_pairs={{0,2},{1,3},{2,0},{3,1},{4,6},{5,7},{6,4},{7,5},{8,10},{9,11},{10,... | collective-permute-start | bytes 221192 | tf_op jit(solution)/shard_map/ppermute | solution.py:300
  50.1 2.4 %collective-permute-start.11 = (bf16[144,256]{1,0:T(8,128)(2,1)S(1)}, bf16[144,256]{1,0:T(8,128)(2,1)S(1)}, u32[]{:S(2)}, u32[]{:S(2)}) collective-permute-start(bf16[144,256]{1,0:T(8,128)(2,1)S(1)} %get-tuple-element.39), channel_id=1, source_target_pairs={{0,3},{1,2},{2,1},{3,0},{4,7},{5,6},{6,5},{7,4},{8,11},{9,10},{10,... | collective-permute-start | bytes 221192 | tf_op jit(solution)/shard_map/ppermute | solution.py:300
  52.4 2.9 %collective-permute-done.10.refs_2_ = bf16[144,256]{1,0:T(8,128)(2,1)S(1)} collective-permute-done((bf16[144,256]{1,0:T(8,128)(2,1)S(1)}, bf16[144,256]{1,0:T(8,128)(2,1)S(1)}, u32[]{:S(2)}, u32[]{:S(2)}) %collective-permute-start.10) | collective-permute-done | bytes 73760 | tf_op jit(solution)/shard_map/ppermute | solution.py:300
  55.4 1.0 %collective-permute-done.11.refs_3_ = bf16[144,256]{1,0:T(8,128)(2,1)S(1)} collective-permute-done((bf16[144,256]{1,0:T(8,128)(2,1)S(1)}, bf16[144,256]{1,0:T(8,128)(2,1)S(1)}, u32[]{:S(2)}, u32[]{:S(2)}) %collective-permute-start.11) | collective-permute-done | bytes 73760 | tf_op jit(solution)/shard_map/ppermute | solution.py:300
  56.3 0.8 %finish.1 = (f32[128,256]{1,0:T(8,128)}, f32[1,256]{1,0:T(1,128)S(1)}) custom-call(bf16[128,256]{1,0:T(8,128)(2,1)S(1)} %bitcast.20, f32[16,1,256]{2,1,0:T(1,128)S(1)} %get-tuple-element.23.refs_4_.gain_ref, f32[128,128]{1,0:T(8,128)S(1)} %get-tuple-element.32.inverse_ref, bf16[144,256]{1,0:T(8,128)(2,1)S(1)} %get-tuple-element.36.refs_0_, ...), custom_call_target="tpu_custom_call" | custom-call | tf_op jit(solution)/shard_map/finish/pallas_call | solution.py:283
  57.2 1.3 %outputs.1 = (bf16[256,512]{1,0:T(8,128)(2,1)}, bf16[256,512]{1,0:T(8,128)(2,1)}) custom-call(bf16[4,256,256]{2,1,0:T(8,128)(2,1)S(1)} %get-tuple-element.26.low_ref, bf16[4,256,256]{2,1,0:T(8,128)(2,1)S(1)} %get-tuple-element.27.grad_low_ref, bf16[128,512]{1,0:T(8,128)(2,1)S(1)} %get-tuple-element.28.keys_ref, bf16[128,512]{1,0:T(8,128)(2,1)S(1)} %get-tuple-element.29.values_ref), custom_call_target="tpu_custom_call" | custom-call | flops 134217728 | bytes 1572864 | tf_op jit(solution)/shard_map/outputs/pallas_call | solution.py:191
  58.4 0.6 add_multiply_fusion
  (14 shorter events, 0.1 us)
Async XLA Ops:
  0.6 7.9 %collective-permute-start.2 = (bf16[128,256]{1,0:T(8,128)(2,1)}, bf16[128,256]{1,0:T(8,128)(2,1)S(1)}, u32[]{:S(2)}, u32[]{:S(2)}) collective-permute-start(bf16[128,256]{1,0:T(8,128)(2,1)} %bitcast.17), channel_id=1, source_target_pairs={{0,3},{1,2},{2,1},{3,0},{4,7},{5,6},{6,5},{7,4},{8,11},{9,10},{10,... | collective-permute-start | bytes 196616 | tf_op jit(solution)/shard_map/ppermute | solution.py:300
  5.7 5.8 %collective-permute-start.1 = (bf16[128,256]{1,0:T(8,128)(2,1)}, bf16[128,256]{1,0:T(8,128)(2,1)S(1)}, u32[]{:S(2)}, u32[]{:S(2)}) collective-permute-start(bf16[128,256]{1,0:T(8,128)(2,1)} %bitcast.18), channel_id=1, source_target_pairs={{0,2},{1,3},{2,0},{3,1},{4,6},{5,7},{6,4},{7,5},{8,10},{9,11},{10,... | collective-permute-start | bytes 196616 | tf_op jit(solution)/shard_map/ppermute | solution.py:300
  5.7 5.8 %collective-permute-start = (bf16[128,256]{1,0:T(8,128)(2,1)}, bf16[128,256]{1,0:T(8,128)(2,1)S(1)}, u32[]{:S(2)}, u32[]{:S(2)}) collective-permute-start(bf16[128,256]{1,0:T(8,128)(2,1)} %bitcast.19), channel_id=1, source_target_pairs={{0,1},{1,0},{2,3},{3,2},{4,5},{5,4},{6,7},{7,6},{8,9},{9,8},{10,11... | collective-permute-start | bytes 196616 | tf_op jit(solution)/shard_map/ppermute | solution.py:300
  12.4 10.2 %collective-permute-start.5 = (bf16[4,128,256]{2,1,0:T(8,128)(2,1)S(1)}, bf16[4,128,256]{2,1,0:T(8,128)(2,1)S(1)}, u32[]{:S(2)}, u32[]{:S(2)}) collective-permute-start(bf16[4,128,256]{2,1,0:T(8,128)(2,1)S(1)} %pad_maximum_fusion.refs_0_), channel_id=1, source_target_pairs={{0,24},{8,16},{16,8},{24,0},{1,25},{9,17},{17,9},{25,1},{2,26},{10... | collective-permute-start | bytes 786440 | tf_op jit(solution)/shard_map/ppermute | solution.py:300
  15.0 11.9 %collective-permute-start.4 = (bf16[4,128,256]{2,1,0:T(8,128)(2,1)S(1)}, bf16[4,128,256]{2,1,0:T(8,128)(2,1)S(1)}, u32[]{:S(2)}, u32[]{:S(2)}) collective-permute-start(bf16[4,128,256]{2,1,0:T(8,128)(2,1)S(1)} %pad_maximum_fusion.refs_0_), channel_id=1, source_target_pairs={{0,16},{8,24},{16,0},{24,8},{1,17},{9,25},{17,1},{25,9},{2,18},{10... | collective-permute-start | bytes 786440 | tf_op jit(solution)/shard_map/ppermute | solution.py:300
  15.5 11.7 %collective-permute-start.3 = (bf16[4,128,256]{2,1,0:T(8,128)(2,1)S(1)}, bf16[4,128,256]{2,1,0:T(8,128)(2,1)S(1)}, u32[]{:S(2)}, u32[]{:S(2)}) collective-permute-start(bf16[4,128,256]{2,1,0:T(8,128)(2,1)S(1)} %pad_maximum_fusion.refs_0_), channel_id=1, source_target_pairs={{0,8},{8,0},{16,24},{24,16},{1,9},{9,1},{17,25},{25,17},{2,10},{10... | collective-permute-start | bytes 786440 | tf_op jit(solution)/shard_map/ppermute | solution.py:300
  16.1 0.7 %copy-start.3 = (f32[4096]{0:T(1024)S(1)}, f32[4096]{0:T(1024)}, u32[]{:S(2)}) copy-start(f32[4096]{0:T(1024)} %param.7) | copy-start | bytes 49156
  16.8 10.4 %copy-start = (bf16[1,1,256,512]{3,2,1,0:T(8,128)(2,1)S(1)}, bf16[1,1,256,512]{3,2,1,0:T(8,128)(2,1)}, u32[]{:S(2)}) copy-start(bf16[1,1,256,512]{3,2,1,0:T(8,128)(2,1)} %param.10) | copy-start | bytes 786436
  16.8 10.4 %copy-start.1 = (bf16[1,1,256,512]{3,2,1,0:T(8,128)(2,1)S(1)}, bf16[1,1,256,512]{3,2,1,0:T(8,128)(2,1)}, u32[]{:S(2)}) copy-start(bf16[1,1,256,512]{3,2,1,0:T(8,128)(2,1)} %param.11) | copy-start | bytes 786436
  32.5 23.9 %copy-start.2 = (bf16[1,128,256]{2,1,0:T(8,128)(2,1)S(1)}, bf16[1,128,256]{2,1,0:T(8,128)(2,1)}, u32[]{:S(2)}) copy-start(bf16[1,128,256]{2,1,0:T(8,128)(2,1)} %param.6) | copy-start | bytes 196612
  32.5 9.4 %collective-permute-start.6 = (bf16[528,256]{1,0:T(8,128)(2,1)S(1)}, bf16[528,256]{1,0:T(8,128)(2,1)S(1)}, u32[]{:S(2)}, u32[]{:S(2)}) collective-permute-start(bf16[528,256]{1,0:T(8,128)(2,1)S(1)} %project.5), channel_id=1, source_target_pairs={{0,8},{8,0},{16,24},{24,16},{1,9},{9,1},{17,25},{25,17},{2,10},{10... | collective-permute-start | bytes 811016 | tf_op jit(solution)/shard_map/ppermute | solution.py:300
  34.0 13.8 %collective-permute-start.7 = (bf16[528,256]{1,0:T(8,128)(2,1)S(1)}, bf16[528,256]{1,0:T(8,128)(2,1)S(1)}, u32[]{:S(2)}, u32[]{:S(2)}) collective-permute-start(bf16[528,256]{1,0:T(8,128)(2,1)S(1)} %project.6), channel_id=1, source_target_pairs={{0,16},{8,24},{16,0},{24,8},{1,17},{9,25},{17,1},{25,9},{2,18},{10... | collective-permute-start | bytes 811016 | tf_op jit(solution)/shard_map/ppermute | solution.py:300
  34.6 13.2 %collective-permute-start.8 = (bf16[528,256]{1,0:T(8,128)(2,1)S(1)}, bf16[528,256]{1,0:T(8,128)(2,1)S(1)}, u32[]{:S(2)}, u32[]{:S(2)}) collective-permute-start(bf16[528,256]{1,0:T(8,128)(2,1)S(1)} %project.7), channel_id=1, source_target_pairs={{0,24},{8,16},{16,8},{24,0},{1,25},{9,17},{17,9},{25,1},{2,26},{10... | collective-permute-start | bytes 811016 | tf_op jit(solution)/shard_map/ppermute | solution.py:300
  48.0 4.5 %collective-permute-start.9 = (bf16[144,256]{1,0:T(8,128)(2,1)S(1)}, bf16[144,256]{1,0:T(8,128)(2,1)S(1)}, u32[]{:S(2)}, u32[]{:S(2)}) collective-permute-start(bf16[144,256]{1,0:T(8,128)(2,1)S(1)} %get-tuple-element.37), channel_id=1, source_target_pairs={{0,1},{1,0},{2,3},{3,2},{4,5},{5,4},{6,7},{7,6},{8,9},{9,8},{10,11... | collective-permute-start | bytes 221192 | tf_op jit(solution)/shard_map/ppermute | solution.py:300
  48.1 7.3 %collective-permute-start.10 = (bf16[144,256]{1,0:T(8,128)(2,1)S(1)}, bf16[144,256]{1,0:T(8,128)(2,1)S(1)}, u32[]{:S(2)}, u32[]{:S(2)}) collective-permute-start(bf16[144,256]{1,0:T(8,128)(2,1)S(1)} %get-tuple-element.38), channel_id=1, source_target_pairs={{0,2},{1,3},{2,0},{3,1},{4,6},{5,7},{6,4},{7,5},{8,10},{9,11},{10,... | collective-permute-start | bytes 221192 | tf_op jit(solution)/shard_map/ppermute | solution.py:300
  50.1 6.3 %collective-permute-start.11 = (bf16[144,256]{1,0:T(8,128)(2,1)S(1)}, bf16[144,256]{1,0:T(8,128)(2,1)S(1)}, u32[]{:S(2)}, u32[]{:S(2)}) collective-permute-start(bf16[144,256]{1,0:T(8,128)(2,1)S(1)} %get-tuple-element.39), channel_id=1, source_target_pairs={{0,3},{1,2},{2,1},{3,0},{4,7},{5,6},{6,5},{7,4},{8,11},{9,10},{10,... | collective-permute-start | bytes 221192 | tf_op jit(solution)/shard_map/ppermute | solution.py:300
  57.2 1.3 %collective-permute-start.12 = (f32[1,256]{1,0:T(1,128)S(1)}, f32[1,256]{1,0:T(1,128)S(1)}, u32[]{:S(2)}, u32[]{:S(2)}) collective-permute-start(f32[1,256]{1,0:T(1,128)S(1)} %get-tuple-element.41), channel_id=1, source_target_pairs={{0,4},{4,0},{1,5},{5,1},{2,6},{6,2},{3,7},{7,3},{8,12},{12,8},{9,1... | collective-permute-start | bytes 3080 | tf_op jit(solution)/shard_map/ppermute | solution.py:368

commit v2 on v1

v2 whole, which is shorter than its diff:
```python
import jax
import jax.numpy as jnp
from jax import lax
from jax.experimental import pallas as pl
from jax.experimental.pallas import tpu as pltpu
from jax.sharding import PartitionSpec as P

DH = 64
EPSILON = 1e-06
BLOCK = 256
EXTRA = 16
EXTRA_WIDTH = 256
F32 = jnp.float32
BF16 = jnp.bfloat16
VMEM = pl.BlockSpec(memory_space=pltpu.VMEM)
SMEM = pl.BlockSpec(memory_space=pltpu.SMEM)
HBM = pl.BlockSpec(memory_space=pltpu.HBM)

NN = (((1,), (0,)), ((), ()))
NT = (((1,), (1,)), ((), ()))


def dot(a, b, dims=NN):
    return lax.dot_general(a, b, dims, preferred_element_type=F32)


def split_rows(row):
    high = row.astype(BF16)
    low = (row - high.astype(F32)).astype(BF16)
    return high, low


def in_vmem(array):
    return pltpu.with_memory_space_constraint(array, pltpu.VMEM)


def cost(flops, size):
    return pl.CostEstimate(flops=flops, bytes_accessed=size, transcendentals=0)


def in_hbm(array):
    return pltpu.with_memory_space_constraint(array, pltpu.HBM)


def fetch(own, gain):
    def kernel(own_ref, gain_ref, own_out, gain_out, sems):
        copies = (
            pltpu.make_async_copy(own_ref, own_out.at[0], sems.at[0]),
            pltpu.make_async_copy(gain_ref, gain_out, sems.at[1]),
        )
        for copy in copies:
            copy.start()
        for copy in copies:
            copy.wait()

    return pl.pallas_call(
        kernel,
        out_shape=(pltpu.VMEM((1, *own.shape), BF16), pltpu.VMEM(gain.shape, F32)),
        in_specs=[HBM, HBM],
        out_specs=(VMEM, VMEM),
        scratch_shapes=[pltpu.SemaphoreType.DMA((2,))],
        compiler_params=pltpu.CompilerParams(vmem_limit_bytes=1 << 20),
        cost_estimate=cost(0, 1 << 20),
        name="fetch",
    )(in_hbm(own), in_hbm(gain))


def load_weights(place, wk, wv, gain, sections, slots):
    width, columns = wk.shape
    block = gain.shape[2]

    def kernel(place_ref, wk_ref, wv_ref, gain_ref, *refs):
        outs, sems = refs[:-1], refs[-1]
        copies = []
        for j in range(sections):
            gain_out, wk_out, wv_out = outs[j::sections]
            for i in range(slots):
                b = lax.bitwise_xor(place_ref[0], j) * slots + lax.bitwise_xor(place_ref[1], i)
                source = pl.ds(pl.multiple_of(b * block, block), block)
                n = j * slots + i
                copies += [
                    pltpu.make_async_copy(wk_ref.at[source, :], wk_out.at[i], sems.at[0, n]),
                    pltpu.make_async_copy(wv_ref.at[source, :], wv_out.at[i], sems.at[1, n]),
                ]
                gain_out[i] = gain_ref[b]
        for copy in copies:
            copy.start()
        for copy in copies:
            copy.wait()

    outs = pl.pallas_call(
        kernel,
        out_shape=(pltpu.VMEM((slots, 1, block), F32),) * sections
        + (pltpu.VMEM((slots, block, columns), BF16),) * (2 * sections),
        in_specs=[SMEM, HBM, HBM, VMEM],
        out_specs=(VMEM,) * (3 * sections),
        scratch_shapes=[pltpu.SemaphoreType.DMA((2, sections * slots))],
        compiler_params=pltpu.CompilerParams(vmem_limit_bytes=1 << 20),
        cost_estimate=cost(0, 8 * width * columns),
        name="load_weights",
    )(place, in_hbm(wk), in_hbm(wv), in_vmem(gain))
    return [outs[n * sections:(n + 1) * sections] for n in range(3)]


def attend(x, gain, wk, wv, q, g):
    sections = len(x)
    flat = [array for arrays in x for array in arrays]
    _, rows, block = flat[0].shape
    slots = sum(array.shape[0] for array in x[0])
    length, columns = q.shape
    width = sections * slots * block
    pair = 2 * DH
    pairs = columns // pair
    factor = DH ** (-0.5)

    def kernel(*refs):
        x_refs, refs = refs[:len(flat)], refs[len(flat):]
        gain_refs, wk_refs, wv_refs = (refs[n * sections:(n + 1) * sections] for n in range(3))
        (q_ref, g_ref, low_ref, grad_low_ref, keys_ref, values_ref, kg_ref, vg_ref, inverse_ref,
         extra_ref, memory_buf) = refs[3 * sections:]
        places = [(ref, i) for ref in x_refs for i in range(ref.shape[0])]

        def wide(j, i):
            ref, n = places[j * slots + i]
            return ref[n].astype(F32)

        squares = jnp.zeros((rows, block), F32)
        for j in range(sections):
            for i in range(slots):
                squares += wide(j, i) * wide(j, i)
        inverse = lax.rsqrt(jnp.sum(squares, axis=-1, keepdims=True) / width + EPSILON)
        inverse_ref[...] = jnp.broadcast_to(inverse, inverse_ref.shape)

        keys = jnp.zeros((rows, columns), F32)
        values = jnp.zeros((rows, columns), F32)
        for j in range(sections):
            for i in range(slots):
                memory = wide(j, i) * inverse * gain_refs[j][i]
                memory_buf[:, i * block:(i + 1) * block] = memory.astype(BF16)
            keys += dot(memory_buf[...], wk_refs[j][...].reshape(slots * block, columns))
            values += dot(memory_buf[...], wv_refs[j][...].reshape(slots * block, columns))
        keys_ref[...] = keys.astype(BF16)
        values_ref[...] = values.astype(BF16)

        first = lax.broadcasted_iota(jnp.int32, (rows, pair), 1) < DH
        zero = jnp.zeros((rows, pair), BF16)
        c_sum = jnp.zeros((rows, pair), F32)
        for p in range(pairs):
            at = slice(p * pair, (p + 1) * pair)
            k, v = keys_ref[:, at], values_ref[:, at]
            q, g = q_ref[:, at], g_ref[:, at]
            k_two = jnp.concatenate((jnp.where(first, k, zero), jnp.where(first, zero, k)), axis=0)
            v_two = jnp.concatenate((jnp.where(first, v, zero), jnp.where(first, zero, v)), axis=0)
            scores = dot(k_two, q, NT)
            share_grad = dot(v_two, g, NT)
            for h in range(2):
                head = slice(h * rows, (h + 1) * rows)
                score = scores[head]
                raised = jnp.exp((score - jnp.max(score, axis=0, keepdims=True)) * factor)
                shares = raised * (1.0 / jnp.sum(raised, axis=0, keepdims=True))
                low_ref[p, head, :] = shares.astype(BF16)
                grads = share_grad[head]
                mean = jnp.sum(shares * grads, axis=0, keepdims=True)
                grad_low_ref[p, head, :] = (shares * (grads - mean) * factor).astype(BF16)
            vg = dot(low_ref[p], g)
            kg = dot(grad_low_ref[p], q)
            vg = jnp.where(first, vg[:rows], vg[rows:]).astype(BF16)
            kg = jnp.where(first, kg[:rows], kg[rows:]).astype(BF16)
            vg_ref[:, at] = vg
            kg_ref[:, at] = kg
            c_sum += kg.astype(F32) * k.astype(F32) + vg.astype(F32) * v.astype(F32)

        row = jnp.sum(c_sum.T, axis=0, keepdims=True)
        row = jnp.concatenate((row, jnp.zeros((1, EXTRA_WIDTH - rows), F32)), axis=1)
        high, low = split_rows(row)
        blank = jnp.zeros((EXTRA - 2, EXTRA_WIDTH), BF16)
        extra_ref[...] = jnp.concatenate((high, low, blank), axis=0)

    return pl.pallas_call(
        kernel,
        out_shape=(
            pltpu.VMEM((pairs, 2 * rows, length), BF16),
            pltpu.VMEM((pairs, 2 * rows, length), BF16),
            pltpu.VMEM((rows, columns), BF16),
            pltpu.VMEM((rows, columns), BF16),
            pltpu.VMEM((rows, columns), BF16),
            pltpu.VMEM((rows, columns), BF16),
            pltpu.VMEM((rows, 128), F32),
            pltpu.VMEM((EXTRA, EXTRA_WIDTH), BF16),
        ),
        in_specs=[VMEM] * (len(flat) + 3 * sections + 2),
        out_specs=(VMEM,) * 8,
        scratch_shapes=[pltpu.VMEM((rows, slots * block), BF16)],
        compiler_params=pltpu.CompilerParams(vmem_limit_bytes=16 << 20),
        cost_estimate=pl.CostEstimate(
            flops=4 * rows * width * columns + 16 * length * rows * columns,
            bytes_accessed=8 * width * columns,
            transcendentals=length * rows * columns // DH,
        ),
        name="attend",
    )(*flat, *map(in_vmem, gain), *map(in_vmem, wk), *map(in_vmem, wv), q, g)


def mix(shares, weights):
    pairs, both, length = shares.shape
    rows, columns = weights.shape
    pair = columns // pairs

    def kernel(shares_ref, weights_ref, out_ref):
        first = lax.broadcasted_iota(jnp.int32, (rows, pair), 1) < DH
        zero = jnp.zeros((rows, pair), BF16)
        for p in range(pairs):
            at = slice(p * pair, (p + 1) * pair)
            w = weights_ref[:, at]
            two = jnp.concatenate((jnp.where(first, w, zero), jnp.where(first, zero, w)), axis=0)
            out_ref[:, at] = dot(two.T, shares_ref[p]).T.astype(BF16)

    return pl.pallas_call(
        kernel,
        out_shape=jax.ShapeDtypeStruct((length, columns), BF16),
        in_specs=[VMEM] * 2,
        out_specs=VMEM,
        compiler_params=pltpu.CompilerParams(vmem_limit_bytes=4 << 20),
        cost_estimate=cost(1, 1),
        name="mix",
    )(in_vmem(shares), in_vmem(weights))


def project(kg, vg, wk, wv, start, count, extra=None):
    rows, columns = kg.shape
    block = wk.shape[1]
    tail = [] if extra is None else [in_vmem(extra)]
    more = 0 if extra is None else extra.shape[0]

    def kernel(kg_ref, vg_ref, wk_ref, wv_ref, *refs):
        kg, vg, out_ref = kg_ref[...], vg_ref[...], refs[-1]
        for i in range(count):
            n = start + i
            part = dot(kg, wk_ref[n], NT) + dot(vg, wv_ref[n], NT)
            out_ref[i * rows:(i + 1) * rows, :] = part.astype(BF16)
        if tail:
            out_ref[count * rows:, :] = refs[0][...]

    return pl.pallas_call(
        kernel,
        out_shape=pltpu.VMEM((count * rows + more, block), BF16),
        in_specs=[VMEM] * (4 + len(tail)),
        out_specs=VMEM,
        compiler_params=pltpu.CompilerParams(vmem_limit_bytes=4 << 20),
        cost_estimate=cost(1, 1),
        name="project",
    )(in_vmem(kg), in_vmem(vg), in_vmem(wk), in_vmem(wv), *tail)


def join(first, second):
    count = first.shape[0]

    def kernel(first_ref, second_ref, out_ref):
        out_ref[:count] = first_ref[...]
        out_ref[count:] = second_ref[...]

    return pl.pallas_call(
        kernel,
        out_shape=pltpu.VMEM((count + second.shape[0], *first.shape[1:]), BF16),
        in_specs=[VMEM, VMEM],
        out_specs=VMEM,
        compiler_params=pltpu.CompilerParams(vmem_limit_bytes=2 << 20),
        name="join",
    )(in_vmem(first), second)


def total_of(refs, start, size):
    total = refs[0][start:start + size, :].astype(F32)
    for ref in refs[1:]:
        total += ref[start:start + size, :].astype(F32)
    return total


def sum_c(extra, c_rows):
    return extra[:c_rows] + extra[c_rows:2 * c_rows]


def c_tail(c):
    high, low = split_rows(c)
    blank = jnp.zeros((EXTRA - 2 * c.shape[0], c.shape[1]), BF16)
    return jnp.concatenate((high, low, blank), axis=0)


def sum_far(chunks, rows, c_rows):
    size, block = chunks[0].shape

    def kernel(*refs):
        parts, out = refs[:-1], refs[-1]
        for start in range(0, size - EXTRA, rows):
            out[start:start + rows, :] = total_of(parts, start, rows).astype(BF16)
        out[size - EXTRA:, :] = c_tail(sum_c(total_of(parts, size - EXTRA, EXTRA), c_rows))

    return pl.pallas_call(
        kernel,
        out_shape=pltpu.VMEM((size, block), BF16),
        in_specs=[VMEM] * len(chunks),
        out_specs=VMEM,
        compiler_params=pltpu.CompilerParams(vmem_limit_bytes=4 << 20),
        name="sum_far",
    )(*chunks)


def sum_near(chunks, mine, theirs, rows, c_rows):
    block = mine.shape[1]
    size = mine.shape[0] - EXTRA

    def kernel(mine_ref, theirs_ref, *refs):
        parts, (own_ref, out) = refs[:-2], refs[-2:]
        extra = mine_ref[size:, :].astype(F32) + theirs_ref[size:, :].astype(F32)
        out[size - rows:, :] = c_tail(sum_c(extra, c_rows))
        parts = (theirs_ref, *parts)
        own_ref[...] = total_of(parts, 0, rows)
        for start in range(rows, size, rows):
            out[start - rows:start, :] = total_of(parts, start, rows).astype(BF16)

    return pl.pallas_call(
        kernel,
        out_shape=(
            pltpu.VMEM((rows, block), F32), pltpu.VMEM((size - rows + EXTRA, block), BF16)
        ),
        in_specs=[VMEM] * (2 + len(chunks)),
        out_specs=(VMEM, VMEM),
        compiler_params=pltpu.CompilerParams(vmem_limit_bytes=4 << 20),
        name="sum_near",
    )(in_vmem(mine), theirs, *chunks)


def gain_part(own_total, part, hidden, inverse):
    rows, block = own_total.shape

    def kernel(hidden_ref, inverse_ref, own_ref, part_ref, out_ref):
        total = own_ref[...] + part_ref[:rows, :].astype(F32)
        normed = hidden_ref[0].astype(F32) * inverse_ref[:, 0:1]
        out_ref[...] = jnp.sum(total * normed, axis=0, keepdims=True)

    return pl.pallas_call(
        kernel,
        out_shape=pltpu.VMEM((1, block), F32),
        in_specs=[VMEM] * 4,
        out_specs=VMEM,
        compiler_params=pltpu.CompilerParams(vmem_limit_bytes=4 << 20),
        name="gain_part",
    )(in_vmem(hidden), in_vmem(inverse), in_vmem(own_total), part)


def finish(own_total, mine, part, hidden, gain, inverse, width, c_rows):
    rows, block = own_total.shape

    def kernel(hidden_ref, gain_ref, inverse_ref, own_ref, mine_ref, part_ref, out_ref):
        extra = mine_ref[...].astype(F32) + part_ref[rows:, :].astype(F32)
        c = sum_c(extra, c_rows)
        c = jnp.concatenate([c[n:n + 1] for n in range(c_rows)], axis=1)[:, :rows]
        mean = (jnp.broadcast_to(c, (rows, rows)) / width).T[:, 0:1]
        total = own_ref[...] + part_ref[:rows, :].astype(F32)
        inverse = inverse_ref[:, 0:1]
        normed = hidden_ref[0].astype(F32) * inverse
        out_ref[...] = inverse * (total * gain_ref[0] - normed * mean)

    return pl.pallas_call(
        kernel,
        out_shape=jax.ShapeDtypeStruct((rows, block), F32),
        in_specs=[VMEM] * 6,
        out_specs=VMEM,
        compiler_params=pltpu.CompilerParams(vmem_limit_bytes=4 << 20),
        cost_estimate=cost(0, 64 << 10),
        name="finish",
    )(in_vmem(hidden), gain, in_vmem(inverse), in_vmem(own_total), in_vmem(mine), part)


def add_gain(mine, theirs, replicas):
    def kernel(mine_ref, theirs_ref, out_ref):
        out_ref[...] = (mine_ref[...] + theirs_ref[...]) / replicas

    return pl.pallas_call(
        kernel,
        out_shape=jax.ShapeDtypeStruct(mine.shape, F32),
        in_specs=[VMEM, VMEM],
        out_specs=VMEM,
        compiler_params=pltpu.CompilerParams(vmem_limit_bytes=1 << 20),
        name="add_gain",
    )(in_vmem(mine), theirs)


def to_partner(array, axis, j):
    return lax.ppermute(array, axis, [(d, d ^ j) for d in range(lax.axis_size(axis))])


def swapped(array, axis, mine):
    return jnp.stack(
        [
            lax.dynamic_index_in_dim(array, jnp.bitwise_xor(mine, i), axis, False)
            for i in range(array.shape[axis])
        ],
        axis,
    )


def per_device(enc_hidden, enc_gain, key_weight, value_weight, queries, out_grad):
    own = enc_hidden[0]
    rows, own_columns = own.shape
    wk, wv = key_weight[0], value_weight[0]
    width, columns = wk.shape
    sections = lax.axis_size("section")
    groups = lax.axis_size("mp")
    replicas = lax.axis_size("dp")
    section = lax.axis_index("section")
    mp = lax.axis_index("mp")
    direct = own_columns == BLOCK
    c_rows = max(rows // own_columns, 1)

    half = groups // 2
    far_first = sorted(range(1, sections), key=lambda j: -bin(j).count("1"))
    place = jnp.stack((section, mp)) if direct else jnp.zeros(2, jnp.int32)
    slots = groups if direct else 4

    hidden, gain = fetch(own, enc_gain.reshape(width // BLOCK, 1, BLOCK))
    near, step = hidden, 1
    while step < half:
        near = join(near, to_partner(own[None] if step == 1 else near, "mp", step))
        step *= 2
    far = to_partner(near, "mp", half)
    if direct:
        x = [(near, far)]
        for j in range(1, sections):
            x.append((to_partner(near, "section", j), to_partner(far, "section", j)))
    else:
        x = lax.all_gather(jnp.concatenate((near, far)), "section", axis=0)
        x = swapped(x, 1, mp).transpose(2, 0, 1, 3).reshape(rows, -1, slots, BLOCK)
        x = [(part,) for part in x.transpose(1, 2, 0, 3)]
    gain, wk, wv = load_weights(place, wk, wv, gain, len(x), slots)
    low, grad_low, keys, values, kg, vg, inverse, extra = attend(
        x, gain, wk, wv, queries[0, 0], out_grad[0, 0]
    )

    if direct:
        own_gain = gain[0]
        pad = jnp.zeros((32, BLOCK), BF16)
        far = [
            project(kg, vg, wk[j], wv[j], half, slots - half, extra) for j in range(sections)
        ]
        far[1:], low = lax.optimization_barrier((far[1:], low))
    attended = mix(low, values)
    if direct:
        kg, attended = lax.optimization_barrier((kg, attended))
        near = [project(kg, vg, wk[j], wv[j], 0, half, pad) for j in range(sections)]
    else:
        whole = [
            project(kg, vg, wk[n // slots], wv[n // slots], n % slots, 1)
            for n in range(width // BLOCK)
        ]
        whole = jnp.stack(whole).transpose(1, 0, 2)
        whole = whole.reshape(rows, sections, groups, own_columns).transpose(1, 2, 0, 3)
        whole = swapped(swapped(whole, 1, mp), 0, section)
        tail = extra[:2, : c_rows * own_columns].reshape(2 * c_rows, own_columns)
        tail = jnp.concatenate((tail, jnp.zeros((EXTRA - 2 * c_rows, own_columns), BF16)))
        near = list(whole[:, :half].reshape(sections, half * rows, own_columns))
        far = whole[:, half:].reshape(sections, (groups - half) * rows, own_columns)
        far = [jnp.concatenate((part, tail)) for part in far]
        own_gain = lax.dynamic_slice_in_dim(
            enc_gain, (section * groups + mp) * own_columns, own_columns, 0
        ).reshape(1, 1, own_columns)

    far = far[:1] + [to_partner(far[j], "section", j) for j in far_first]
    near = near[:1] + [to_partner(near[j], "section", j) for j in far_first]
    mine = sum_far(far, rows, c_rows)
    theirs = to_partner(mine, "mp", half)
    mine, grad_low = lax.optimization_barrier((mine, grad_low))
    query_grad = mix(grad_low, keys)
    mine, query_grad = lax.optimization_barrier((mine, query_grad))
    own_total, part = sum_near(near, mine, theirs, rows, c_rows)
    mine = part[-EXTRA:]
    part = to_partner(part, "mp", 1)
    gain_own = gain_part(own_total, part, hidden, inverse)
    if replicas == 2:
        gain_other = lax.ppermute(gain_own, "dp", [(0, 1), (1, 0)])
    else:
        gain_other = lax.psum(gain_own, "dp")
        gain_own = jnp.zeros_like(gain_own)
    hidden_grad = finish(own_total, mine, part, hidden, own_gain, inverse, width, c_rows)
    gain_total = add_gain(gain_own, gain_other, replicas)
    return (
        attended[None, None],
        query_grad[None, None],
        hidden_grad[None],
        gain_total[0],
    )


def solution(mesh):
    in_specs = (
        P("dp", None, ("section", "mp")),
        P(),
        P("section", None, "mp"),
        P("section", None, "mp"),
        P("dp", "section", None, "mp"),
        P("dp", "section", None, "mp"),
    )
    out_specs = (
        P("dp", "section", None, "mp"),
        P("dp", "section", None, "mp"),
        P("dp", None, ("section", "mp")),
        P(("section", "mp")),
    )
    return jax.shard_map(
        per_device, mesh=mesh, in_specs=in_specs, out_specs=out_specs, check_vma=False
    )
```

time: 59.3 us -> 52.7 us (0.89)
  waiting for transfers between devices: 26.3 us -> 15.1 us
  starting transfers between devices: 17.3 us -> 21 us
  Pallas kernels: 12.5 us -> 15.5 us
  other arithmetic: 1.52 us -> 0.07 us
  local copies, waits for them, and re-layouts: 0.73 us -> 0.01 us
    ppermute x13 -> x17, waiting for transfers between devices: 26.3 us -> 15.1 us  [the longest x16 14.9 us: to_partner(): lax.ppermute(array, axis, [(d, d ^ j) for d in range(lax.axis_size(axis))])]
    ppermute x13 -> x17, starting transfers between devices: 17.3 us -> 21 us  [the longest x16 21 us: to_partner(): lax.ppermute(array, axis, [(d, d ^ j) for d in range(lax.axis_size(axis))])]
    pallas_call x8 -> x18, Pallas kernels: 9.65 us -> 12.7 us  [the longest x1 4.19 us: load_weights(): pl.pallas_call(kernel, out_shape=(pltpu.VMEM((slots, 1, block), F32),) *...]
    another operation x2 -> x1, other arithmetic: 0.95 us -> 0.07 us  [per_device(): place = jnp.stack((section, mp)) if direct else jnp.zeros(2, jnp.int32)]
    unnamed x8 -> x4, local copies, waits for them, and re-layouts: 0.73 us -> 0.01 us
  transfers between devices with their start and end apart: 13 -> 17, of which waited for: 9 -> 9; matrix products, arithmetic and copies ran while one was open for 0% -> 0% of each run, Pallas kernels for 11% -> 20%
where the time goes in v2:
time: 52.7 us; the launch traced here: 52.5 us
  starting transfers between devices  21 us (40%)
  Pallas kernels  15.5 us (29%)
  waiting for transfers between devices  15.1 us (29%)
  between operations  0.8 us (2%)
    ppermute x16, starting transfers between devices, to_partner(): lax.ppermute(array, axis, [(d, d ^ j) for d in range(lax.axis_size(axis))])  21 us
    ppermute x16, waiting for transfers between devices, to_partner(): lax.ppermute(array, axis, [(d, d ^ j) for d in range(lax.axis_size(axis))])  14.9 us
    pallas_call x1, Pallas kernels, load_weights(): pl.pallas_call(kernel, out_shape=(pltpu.VMEM((slots, 1, block), F32),) *...  4.19 us
    pallas_call x8, Pallas kernels, project(): pl.pallas_call(kernel, out_shape=pltpu.VMEM((count * rows + more, block),...  3.79 us
    pallas_call x1, Pallas kernels, attend(): pl.pallas_call(kernel, out_shape=(pltpu.VMEM((pairs, 2 * rows, length), B...  2.84 us
    pallas_call x2, Pallas kernels, mix(): pl.pallas_call(kernel, out_shape=jax.ShapeDtypeStruct((length, columns),...  2.1 us
  transfers between devices with their start and end apart: 17, of which 9 were waited for; matrix products, arithmetic and copies ran while one was open for 0% of the time, Pallas kernels for 20%

profile of v2, /device:TPU:0, one launch (start us, length us, event | category | flops | bytes accessed | tf_op | source)
XLA Modules:
  0.0 52.5 jit_solution(7762545910836943145)
XLA Ops:
  0.6 3.1 %collective-permute-start = (bf16[1,128,256]{2,1,0:T(8,128)(2,1)}, bf16[1,128,256]{2,1,0:T(8,128)(2,1)S(1)}, u32[]{:S(2)}, u32[]{:S(2)}) collective-permute-start(bf16[1,128,256]{2,1,0:T(8,128)(2,1)} %param.6), channel_id=1, source_target_pairs={{0,1},{1,0},{2,3},{3,2},{4,5},{5,4},{6,7},{7,6},{8,9},{9,8},{10,11... | collective-permute-start | bytes 196616 | tf_op jit(solution)/shard_map/ppermute | solution.py:390
  3.7 0.9 %fetch.1 = (bf16[1,128,256]{2,1,0:T(8,128)(2,1)S(1)}, f32[16,1,256]{2,1,0:T(1,128)S(1)}) custom-call(bf16[128,256]{1,0:T(8,128)(2,1)} %bitcast.19, f32[16,1,256]{2,1,0:T(1,128)} %bitcast.20), custom_call_target="tpu_custom_call" | custom-call | bytes 1048576 | tf_op jit(solution)/shard_map/fetch/pallas_call | solution.py:56
  4.6 1.6 %collective-permute-done.second_ref = bf16[1,128,256]{2,1,0:T(8,128)(2,1)S(1)} collective-permute-done((bf16[1,128,256]{2,1,0:T(8,128)(2,1)}, bf16[1,128,256]{2,1,0:T(8,128)(2,1)S(1)}, u32[]{:S(2)}, u32[]{:S(2)}) %collective-permute-start) | collective-permute-done | bytes 65568 | tf_op jit(solution)/shard_map/ppermute | solution.py:390
  6.2 3.1 %collective-permute-start.1 = (bf16[2,128,256]{2,1,0:T(8,128)(2,1)S(1)}, bf16[2,128,256]{2,1,0:T(8,128)(2,1)S(1)}, u32[]{:S(2)}, u32[]{:S(2)}) collective-permute-start(bf16[2,128,256]{2,1,0:T(8,128)(2,1)S(1)} %join.1.refs_0_), channel_id=1, source_target_pairs={{0,2},{1,3},{2,0},{3,1},{4,6},{5,7},{6,4},{7,5},{8,10},{9,11},{10,... | collective-permute-start | bytes 393224 | tf_op jit(solution)/shard_map/ppermute | solution.py:390
  9.3 1.5 %collective-permute-start.2 = (bf16[2,128,256]{2,1,0:T(8,128)(2,1)S(1)}, bf16[2,128,256]{2,1,0:T(8,128)(2,1)S(1)}, u32[]{:S(2)}, u32[]{:S(2)}) collective-permute-start(bf16[2,128,256]{2,1,0:T(8,128)(2,1)S(1)} %join.1.refs_0_), channel_id=1, source_target_pairs={{0,8},{8,0},{16,24},{24,16},{1,9},{9,1},{17,25},{25,17},{2,10},{10... | collective-permute-start | bytes 393224 | tf_op jit(solution)/shard_map/ppermute | solution.py:390
  10.8 1.5 %collective-permute-start.4 = (bf16[2,128,256]{2,1,0:T(8,128)(2,1)S(1)}, bf16[2,128,256]{2,1,0:T(8,128)(2,1)S(1)}, u32[]{:S(2)}, u32[]{:S(2)}) collective-permute-start(bf16[2,128,256]{2,1,0:T(8,128)(2,1)S(1)} %join.1.refs_0_), channel_id=1, source_target_pairs={{0,16},{8,24},{16,0},{24,8},{1,17},{9,25},{17,1},{25,9},{2,18},{10... | collective-permute-start | bytes 393224 | tf_op jit(solution)/shard_map/ppermute | solution.py:390
  12.3 0.5 collective-permute-start.6
  12.8 1.7 %collective-permute-done.1.refs_1_ = bf16[2,128,256]{2,1,0:T(8,128)(2,1)S(1)} collective-permute-done((bf16[2,128,256]{2,1,0:T(8,128)(2,1)S(1)}, bf16[2,128,256]{2,1,0:T(8,128)(2,1)S(1)}, u32[]{:S(2)}, u32[]{:S(2)}) %collective-permute-start.1) | collective-permute-done | bytes 131104 | tf_op jit(solution)/shard_map/ppermute | solution.py:390
  14.4 1.5 %collective-permute-start.3 = (bf16[2,128,256]{2,1,0:T(8,128)(2,1)S(1)}, bf16[2,128,256]{2,1,0:T(8,128)(2,1)S(1)}, u32[]{:S(2)}, u32[]{:S(2)}) collective-permute-start(bf16[2,128,256]{2,1,0:T(8,128)(2,1)S(1)} %collective-permute-done.1.refs_1_), channel_id=1, source_target_pairs={{0,8},{8,0},{16,24},{24,16},{1,9},{9,1},{17,25},{25,17},{2,10},{10... | collective-permute-start | bytes 393224 | tf_op jit(solution)/shard_map/ppermute | solution.py:390
  16.0 1.5 %collective-permute-start.5 = (bf16[2,128,256]{2,1,0:T(8,128)(2,1)S(1)}, bf16[2,128,256]{2,1,0:T(8,128)(2,1)S(1)}, u32[]{:S(2)}, u32[]{:S(2)}) collective-permute-start(bf16[2,128,256]{2,1,0:T(8,128)(2,1)S(1)} %collective-permute-done.1.refs_1_), channel_id=1, source_target_pairs={{0,16},{8,24},{16,0},{24,8},{1,17},{9,25},{17,1},{25,9},{2,18},{10... | collective-permute-start | bytes 393224 | tf_op jit(solution)/shard_map/ppermute | solution.py:390
  18.0 4.2 %load_weights.1 = (f32[4,1,256]{2,1,0:T(1,128)S(1)}, f32[4,1,256]{2,1,0:T(1,128)S(1)}, f32[4,1,256]{2,1,0:T(1,128)S(1)}, f32[4,1,256]{2,1,0:T(1,128)S(1)}, bf16[...) custom-call(s32[2]{0:T(128)S(1)} %pad_add_fusion.place_ref, ...), custom_call_target="tpu_custom_call" | custom-call | bytes 16777216 | tf_op jit(solution)/shard_map/load_weights/pallas_call | solution.py:91
  22.2 1.5 %collective-permute-done.5.refs_5_ = bf16[2,128,256]{2,1,0:T(8,128)(2,1)S(1)} collective-permute-done((bf16[2,128,256]{2,1,0:T(8,128)(2,1)S(1)}, bf16[2,128,256]{2,1,0:T(8,128)(2,1)S(1)}, u32[]{:S(2)}, u32[]{:S(2)}) %collective-permute-start.5) | collective-permute-done | bytes 131104 | tf_op jit(solution)/shard_map/ppermute | solution.py:390
  23.7 2.8 %attend.1 = (bf16[4,256,256]{2,1,0:T(8,128)(2,1)S(1)}, bf16[4,256,256]{2,1,0:T(8,128)(2,1)S(1)}, bf16[128,512]{1,0:T(8,128)(2,1)S(1)}, bf16[128,512]{1,0:T(8,128...) custom-call(bf16[2,128,256]{2,1,0:T(8,128)(2,1)S(1)} %join.1.refs_0_, ...), custom_call_target="tpu_custom_call" | custom-call | flops 1342177280 | bytes 16777216 | tf_op jit(solution)/shard_map/attend/pallas_call | solution.py:179
  26.6 0.5 project.10
  27.1 0.5 project.9
  27.6 0.5 project.8
  28.0 1.1 %collective-permute-start.10 = (bf16[272,256]{1,0:T(8,128)(2,1)S(1)}, bf16[272,256]{1,0:T(8,128)(2,1)S(1)}, u32[]{:S(2)}, u32[]{:S(2)}) collective-permute-start(bf16[272,256]{1,0:T(8,128)(2,1)S(1)} %project.9), channel_id=1, source_target_pairs={{0,16},{8,24},{16,0},{24,8},{1,17},{9,25},{17,1},{25,9},{2,18},{10... | collective-permute-start | bytes 417800 | tf_op jit(solution)/shard_map/ppermute | solution.py:390
  29.1 0.8 %collective-permute-start.8 = (bf16[272,256]{1,0:T(8,128)(2,1)S(1)}, bf16[272,256]{1,0:T(8,128)(2,1)S(1)}, u32[]{:S(2)}, u32[]{:S(2)}) collective-permute-start(bf16[272,256]{1,0:T(8,128)(2,1)S(1)} %project.10), channel_id=1, source_target_pairs={{0,24},{8,16},{16,8},{24,0},{1,25},{9,17},{17,9},{25,1},{2,26},{10... | collective-permute-start | bytes 417800 | tf_op jit(solution)/shard_map/ppermute | solution.py:390
  29.9 1.7 %collective-permute-start.9 = (bf16[272,256]{1,0:T(8,128)(2,1)S(1)}, bf16[272,256]{1,0:T(8,128)(2,1)S(1)}, u32[]{:S(2)}, u32[]{:S(2)}) collective-permute-start(bf16[272,256]{1,0:T(8,128)(2,1)S(1)} %project.8), channel_id=1, source_target_pairs={{0,8},{8,0},{16,24},{24,16},{1,9},{9,1},{17,25},{25,17},{2,10},{10... | collective-permute-start | bytes 417800 | tf_op jit(solution)/shard_map/ppermute | solution.py:390
  31.6 1.1 %mix.2 = bf16[256,512]{1,0:T(8,128)(2,1)} custom-call(bf16[4,256,256]{2,1,0:T(8,128)(2,1)S(1)} %get-tuple-element.56.shares_ref, bf16[128,512]{1,0:T(8,128)(2,1)S(1)} %get-tuple-element.57.weights_ref), custom_call_target="tpu_custom_call" | custom-call | flops 1 | bytes 1 | tf_op jit(solution)/shard_map/mix/pallas_call | solution.py:218
  32.6 0.5 project.15
  33.6 1.1 %collective-permute-start.14 = (bf16[288,256]{1,0:T(8,128)(2,1)S(1)}, bf16[288,256]{1,0:T(8,128)(2,1)S(1)}, u32[]{:S(2)}, u32[]{:S(2)}) collective-permute-start(bf16[288,256]{1,0:T(8,128)(2,1)S(1)} %project.15), channel_id=1, source_target_pairs={{0,16},{8,24},{16,0},{24,8},{1,17},{9,25},{17,1},{25,9},{2,18},{10... | collective-permute-start | bytes 442376 | tf_op jit(solution)/shard_map/ppermute | solution.py:390
  34.7 0.6 %collective-permute-start.13 = (bf16[288,256]{1,0:T(8,128)(2,1)S(1)}, bf16[288,256]{1,0:T(8,128)(2,1)S(1)}, u32[]{:S(2)}, u32[]{:S(2)}) collective-permute-start(bf16[288,256]{1,0:T(8,128)(2,1)S(1)} %project.14), channel_id=1, source_target_pairs={{0,8},{8,0},{16,24},{24,16},{1,9},{9,1},{17,25},{25,17},{2,10},{10... | collective-permute-start | bytes 442376 | tf_op jit(solution)/shard_map/ppermute | solution.py:390
  35.3 0.5 project.13
  35.8 1.9 %collective-permute-start.12 = (bf16[288,256]{1,0:T(8,128)(2,1)S(1)}, bf16[288,256]{1,0:T(8,128)(2,1)S(1)}, u32[]{:S(2)}, u32[]{:S(2)}) collective-permute-start(bf16[288,256]{1,0:T(8,128)(2,1)S(1)} %project.13), channel_id=1, source_target_pairs={{0,24},{8,16},{16,8},{24,0},{1,25},{9,17},{17,9},{25,1},{2,26},{10... | collective-permute-start | bytes 442376 | tf_op jit(solution)/shard_map/ppermute | solution.py:390
  39.0 0.5 project.12.refs_0_
  39.5 1.1 %mix.3 = bf16[256,512]{1,0:T(8,128)(2,1)} custom-call(bf16[4,256,256]{2,1,0:T(8,128)(2,1)S(1)} %get-tuple-element.64.shares_ref, bf16[128,512]{1,0:T(8,128)(2,1)S(1)} %get-tuple-element.65.weights_ref), custom_call_target="tpu_custom_call" | custom-call | flops 1 | bytes 1 | tf_op jit(solution)/shard_map/mix/pallas_call | solution.py:218
  40.9 2.0 %collective-permute-done.12.refs_1_ = bf16[288,256]{1,0:T(8,128)(2,1)S(1)} collective-permute-done((bf16[288,256]{1,0:T(8,128)(2,1)S(1)}, bf16[288,256]{1,0:T(8,128)(2,1)S(1)}, u32[]{:S(2)}, u32[]{:S(2)}) %collective-permute-start.12) | collective-permute-done | bytes 147488 | tf_op jit(solution)/shard_map/ppermute | solution.py:390
  42.9 3.3 %collective-permute-done.11.theirs_ref = bf16[272,256]{1,0:T(8,128)(2,1)S(1)} collective-permute-done((bf16[272,256]{1,0:T(8,128)(2,1)S(1)}, bf16[272,256]{1,0:T(8,128)(2,1)S(1)}, u32[]{:S(2)}, u32[]{:S(2)}) %collective-permute-start.11) | collective-permute-done | bytes 139296 | tf_op jit(solution)/shard_map/ppermute | solution.py:390
  46.5 4.2 %collective-permute-done.15.part_ref = bf16[144,256]{1,0:T(8,128)(2,1)S(1)} collective-permute-done((bf16[144,256]{1,0:T(8,128)(2,1)S(1)}, bf16[144,256]{1,0:T(8,128)(2,1)S(1)}, u32[]{:S(2)}, u32[]{:S(2)}) %collective-permute-start.15) | collective-permute-done | bytes 73760 | tf_op jit(solution)/shard_map/ppermute | solution.py:390
  50.9 0.8 %finish.1 = f32[128,256]{1,0:T(8,128)} custom-call(bf16[1,128,256]{2,1,0:T(8,128)(2,1)S(1)} %get-tuple-element.38.first_ref.hidden_ref, f32[4,1,256]{2,1,0:T(1,128)S(1)} %get-tuple-element.40.refs_8_.gain_ref, f32[128,128]{1,0:T(8,128)S(1)} %get-tuple-element.67.inverse_ref, f32[128,256]{1,0:T(8,128)S(1)} %get-tuple-element.70.own_ref, ...), custom_call_target="tpu_custom_call" | custom-call | bytes 65536 | tf_op jit(solution)/shard_map/finish/pallas_call | solution.py:364
  52.0 0.6 %add_gain.1 = f32[1,256]{1,0:T(1,128)} custom-call(f32[1,256]{1,0:T(1,128)S(1)} %gain_part.1.mine_ref, f32[1,256]{1,0:T(1,128)S(1)} %collective-permute-done.16.theirs_ref), custom_call_target="tpu_custom_call" | custom-call | tf_op jit(solution)/shard_map/add_gain/pallas_call | solution.py:379
  (28 shorter events, 3.4 us)
Async XLA Ops:
  0.6 5.5 %collective-permute-start = (bf16[1,128,256]{2,1,0:T(8,128)(2,1)}, bf16[1,128,256]{2,1,0:T(8,128)(2,1)S(1)}, u32[]{:S(2)}, u32[]{:S(2)}) collective-permute-start(bf16[1,128,256]{2,1,0:T(8,128)(2,1)} %param.6), channel_id=1, source_target_pairs={{0,1},{1,0},{2,3},{3,2},{4,5},{5,4},{6,7},{7,6},{8,9},{9,8},{10,11... | collective-permute-start | bytes 196616 | tf_op jit(solution)/shard_map/ppermute | solution.py:390
  6.2 8.3 %collective-permute-start.1 = (bf16[2,128,256]{2,1,0:T(8,128)(2,1)S(1)}, bf16[2,128,256]{2,1,0:T(8,128)(2,1)S(1)}, u32[]{:S(2)}, u32[]{:S(2)}) collective-permute-start(bf16[2,128,256]{2,1,0:T(8,128)(2,1)S(1)} %join.1.refs_0_), channel_id=1, source_target_pairs={{0,2},{1,3},{2,0},{3,1},{4,6},{5,7},{6,4},{7,5},{8,10},{9,11},{10,... | collective-permute-start | bytes 393224 | tf_op jit(solution)/shard_map/ppermute | solution.py:390
  9.3 8.2 %collective-permute-start.2 = (bf16[2,128,256]{2,1,0:T(8,128)(2,1)S(1)}, bf16[2,128,256]{2,1,0:T(8,128)(2,1)S(1)}, u32[]{:S(2)}, u32[]{:S(2)}) collective-permute-start(bf16[2,128,256]{2,1,0:T(8,128)(2,1)S(1)} %join.1.refs_0_), channel_id=1, source_target_pairs={{0,8},{8,0},{16,24},{24,16},{1,9},{9,1},{17,25},{25,17},{2,10},{10... | collective-permute-start | bytes 393224 | tf_op jit(solution)/shard_map/ppermute | solution.py:390
  10.8 11.4 %collective-permute-start.4 = (bf16[2,128,256]{2,1,0:T(8,128)(2,1)S(1)}, bf16[2,128,256]{2,1,0:T(8,128)(2,1)S(1)}, u32[]{:S(2)}, u32[]{:S(2)}) collective-permute-start(bf16[2,128,256]{2,1,0:T(8,128)(2,1)S(1)} %join.1.refs_0_), channel_id=1, source_target_pairs={{0,16},{8,24},{16,0},{24,8},{1,17},{9,25},{17,1},{25,9},{2,18},{10... | collective-permute-start | bytes 393224 | tf_op jit(solution)/shard_map/ppermute | solution.py:390
  12.3 9.9 %collective-permute-start.6 = (bf16[2,128,256]{2,1,0:T(8,128)(2,1)S(1)}, bf16[2,128,256]{2,1,0:T(8,128)(2,1)S(1)}, u32[]{:S(2)}, u32[]{:S(2)}) collective-permute-start(bf16[2,128,256]{2,1,0:T(8,128)(2,1)S(1)} %join.1.refs_0_), channel_id=1, source_target_pairs={{0,24},{8,16},{16,8},{24,0},{1,25},{9,17},{17,9},{25,1},{2,26},{10... | collective-permute-start | bytes 393224 | tf_op jit(solution)/shard_map/ppermute | solution.py:390
  14.4 7.8 %collective-permute-start.3 = (bf16[2,128,256]{2,1,0:T(8,128)(2,1)S(1)}, bf16[2,128,256]{2,1,0:T(8,128)(2,1)S(1)}, u32[]{:S(2)}, u32[]{:S(2)}) collective-permute-start(bf16[2,128,256]{2,1,0:T(8,128)(2,1)S(1)} %collective-permute-done.1.refs_1_), channel_id=1, source_target_pairs={{0,8},{8,0},{16,24},{24,16},{1,9},{9,1},{17,25},{25,17},{2,10},{10... | collective-permute-start | bytes 393224 | tf_op jit(solution)/shard_map/ppermute | solution.py:390
  16.0 7.8 %collective-permute-start.5 = (bf16[2,128,256]{2,1,0:T(8,128)(2,1)S(1)}, bf16[2,128,256]{2,1,0:T(8,128)(2,1)S(1)}, u32[]{:S(2)}, u32[]{:S(2)}) collective-permute-start(bf16[2,128,256]{2,1,0:T(8,128)(2,1)S(1)} %collective-permute-done.1.refs_1_), channel_id=1, source_target_pairs={{0,16},{8,24},{16,0},{24,8},{1,17},{9,25},{17,1},{25,9},{2,18},{10... | collective-permute-start | bytes 393224 | tf_op jit(solution)/shard_map/ppermute | solution.py:390
  17.5 6.2 %collective-permute-start.7 = (bf16[2,128,256]{2,1,0:T(8,128)(2,1)S(1)}, bf16[2,128,256]{2,1,0:T(8,128)(2,1)S(1)}, u32[]{:S(2)}, u32[]{:S(2)}) collective-permute-start(bf16[2,128,256]{2,1,0:T(8,128)(2,1)S(1)} %collective-permute-done.1.refs_1_), channel_id=1, source_target_pairs={{0,24},{8,16},{16,8},{24,0},{1,25},{9,17},{17,9},{25,1},{2,26},{10... | collective-permute-start | bytes 393224 | tf_op jit(solution)/shard_map/ppermute | solution.py:390
  18.0 5.7 %copy-start = (bf16[1,1,256,512]{3,2,1,0:T(8,128)(2,1)S(1)}, bf16[1,1,256,512]{3,2,1,0:T(8,128)(2,1)}, u32[]{:S(2)}) copy-start(bf16[1,1,256,512]{3,2,1,0:T(8,128)(2,1)} %param.10) | copy-start | bytes 786436
  18.0 5.7 %copy-start.1 = (bf16[1,1,256,512]{3,2,1,0:T(8,128)(2,1)S(1)}, bf16[1,1,256,512]{3,2,1,0:T(8,128)(2,1)}, u32[]{:S(2)}) copy-start(bf16[1,1,256,512]{3,2,1,0:T(8,128)(2,1)} %param.11) | copy-start | bytes 786436
  28.0 7.7 %collective-permute-start.10 = (bf16[272,256]{1,0:T(8,128)(2,1)S(1)}, bf16[272,256]{1,0:T(8,128)(2,1)S(1)}, u32[]{:S(2)}, u32[]{:S(2)}) collective-permute-start(bf16[272,256]{1,0:T(8,128)(2,1)S(1)} %project.9), channel_id=1, source_target_pairs={{0,16},{8,24},{16,0},{24,8},{1,17},{9,25},{17,1},{25,9},{2,18},{10... | collective-permute-start | bytes 417800 | tf_op jit(solution)/shard_map/ppermute | solution.py:390
  29.1 9.1 %collective-permute-start.8 = (bf16[272,256]{1,0:T(8,128)(2,1)S(1)}, bf16[272,256]{1,0:T(8,128)(2,1)S(1)}, u32[]{:S(2)}, u32[]{:S(2)}) collective-permute-start(bf16[272,256]{1,0:T(8,128)(2,1)S(1)} %project.10), channel_id=1, source_target_pairs={{0,24},{8,16},{16,8},{24,0},{1,25},{9,17},{17,9},{25,1},{2,26},{10... | collective-permute-start | bytes 417800 | tf_op jit(solution)/shard_map/ppermute | solution.py:390
  29.9 8.7 %collective-permute-start.9 = (bf16[272,256]{1,0:T(8,128)(2,1)S(1)}, bf16[272,256]{1,0:T(8,128)(2,1)S(1)}, u32[]{:S(2)}, u32[]{:S(2)}) collective-permute-start(bf16[272,256]{1,0:T(8,128)(2,1)S(1)} %project.8), channel_id=1, source_target_pairs={{0,8},{8,0},{16,24},{24,16},{1,9},{9,1},{17,25},{25,17},{2,10},{10... | collective-permute-start | bytes 417800 | tf_op jit(solution)/shard_map/ppermute | solution.py:390
  33.6 7.0 %collective-permute-start.14 = (bf16[288,256]{1,0:T(8,128)(2,1)S(1)}, bf16[288,256]{1,0:T(8,128)(2,1)S(1)}, u32[]{:S(2)}, u32[]{:S(2)}) collective-permute-start(bf16[288,256]{1,0:T(8,128)(2,1)S(1)} %project.15), channel_id=1, source_target_pairs={{0,16},{8,24},{16,0},{24,8},{1,17},{9,25},{17,1},{25,9},{2,18},{10... | collective-permute-start | bytes 442376 | tf_op jit(solution)/shard_map/ppermute | solution.py:390
  34.7 6.2 %collective-permute-start.13 = (bf16[288,256]{1,0:T(8,128)(2,1)S(1)}, bf16[288,256]{1,0:T(8,128)(2,1)S(1)}, u32[]{:S(2)}, u32[]{:S(2)}) collective-permute-start(bf16[288,256]{1,0:T(8,128)(2,1)S(1)} %project.14), channel_id=1, source_target_pairs={{0,8},{8,0},{16,24},{24,16},{1,9},{9,1},{17,25},{25,17},{2,10},{10... | collective-permute-start | bytes 442376 | tf_op jit(solution)/shard_map/ppermute | solution.py:390
  35.8 7.1 %collective-permute-start.12 = (bf16[288,256]{1,0:T(8,128)(2,1)S(1)}, bf16[288,256]{1,0:T(8,128)(2,1)S(1)}, u32[]{:S(2)}, u32[]{:S(2)}) collective-permute-start(bf16[288,256]{1,0:T(8,128)(2,1)S(1)} %project.13), channel_id=1, source_target_pairs={{0,24},{8,16},{16,8},{24,0},{1,25},{9,17},{17,9},{25,1},{2,26},{10... | collective-permute-start | bytes 442376 | tf_op jit(solution)/shard_map/ppermute | solution.py:390
  38.7 7.5 %collective-permute-start.11 = (bf16[272,256]{1,0:T(8,128)(2,1)S(1)}, bf16[272,256]{1,0:T(8,128)(2,1)S(1)}, u32[]{:S(2)}, u32[]{:S(2)}) collective-permute-start(bf16[272,256]{1,0:T(8,128)(2,1)S(1)} %sum_far.1.mine_ref), channel_id=1, source_target_pairs={{0,2},{1,3},{2,0},{3,1},{4,6},{5,7},{6,4},{7,5},{8,10},{9,11},{10,... | collective-permute-start | bytes 417800 | tf_op jit(solution)/shard_map/ppermute | solution.py:390
  46.3 4.4 %collective-permute-start.15 = (bf16[144,256]{1,0:T(8,128)(2,1)S(1)}, bf16[144,256]{1,0:T(8,128)(2,1)S(1)}, u32[]{:S(2)}, u32[]{:S(2)}) collective-permute-start(bf16[144,256]{1,0:T(8,128)(2,1)S(1)} %get-tuple-element.71), channel_id=1, source_target_pairs={{0,1},{1,0},{2,3},{3,2},{4,5},{5,4},{6,7},{7,6},{8,9},{9,8},{10,11... | collective-permute-start | bytes 221192 | tf_op jit(solution)/shard_map/ppermute | solution.py:390
  50.8 1.2 %collective-permute-start.16 = (f32[1,256]{1,0:T(1,128)S(1)}, f32[1,256]{1,0:T(1,128)S(1)}, u32[]{:S(2)}, u32[]{:S(2)}) collective-permute-start(f32[1,256]{1,0:T(1,128)S(1)} %gain_part.1.mine_ref), channel_id=1, source_target_pairs={{0,4},{4,0},{1,5},{5,1},{2,6},{6,2},{3,7},{7,3},{8,12},{12,8},{9,1... | collective-permute-start | bytes 3080 | tf_op jit(solution)/shard_map/ppermute | solution.py:480

commit v3 on v2

v3 whole, which is shorter than its diff:
```python
import math

import jax
import jax.numpy as jnp
from jax import lax
from jax.experimental import pallas as pl
from jax.experimental.pallas import tpu as pltpu
from jax.sharding import PartitionSpec as P

DH = 64
EPSILON = 1e-06
BLOCK = 256
EXTRA = 16
EXTRA_WIDTH = 256
TURN_GATHER = True
TURN_SCATTER = True
REORDER = True
F32 = jnp.float32
BF16 = jnp.bfloat16
VMEM = pl.BlockSpec(memory_space=pltpu.VMEM)
SMEM = pl.BlockSpec(memory_space=pltpu.SMEM)
HBM = pl.BlockSpec(memory_space=pltpu.HBM)

NN = (((1,), (0,)), ((), ()))
NT = (((1,), (1,)), ((), ()))


def dot(a, b, dims=NN):
    return lax.dot_general(a, b, dims, preferred_element_type=F32)


def split_rows(row):
    high = row.astype(BF16)
    low = (row - high.astype(F32)).astype(BF16)
    return high, low


def in_vmem(array):
    return pltpu.with_memory_space_constraint(array, pltpu.VMEM)


def cost(flops, size):
    return pl.CostEstimate(flops=flops, bytes_accessed=size, transcendentals=0)


def in_hbm(array):
    return pltpu.with_memory_space_constraint(array, pltpu.HBM)


def fetch(*arrays):
    count = len(arrays)

    def kernel(*refs):
        sems = refs[-1]
        copies = [
            pltpu.make_async_copy(refs[n], refs[count + n], sems.at[n]) for n in range(count)
        ]
        for copy in copies:
            copy.start()
        for copy in copies:
            copy.wait()

    return pl.pallas_call(
        kernel,
        out_shape=tuple(pltpu.VMEM(array.shape, array.dtype) for array in arrays),
        in_specs=[HBM] * count,
        out_specs=(VMEM,) * count,
        scratch_shapes=[pltpu.SemaphoreType.DMA((count,))],
        compiler_params=pltpu.CompilerParams(vmem_limit_bytes=1 << 20),
        cost_estimate=cost(0, 2 * sum(a.size * a.dtype.itemsize for a in arrays)),
        name="fetch",
    )(*map(in_hbm, arrays))


def far_first(j):
    return j ^ (j & 1) * 2


def first_row(direct, j, i, slots, block, turned, reordered):
    if direct:
        section, mp, core = (lax.axis_index(name) for name in ("section", "mp", "dp"))
        odd = lax.rem(core, 2) if turned else 0
        label = far_first if reordered else lambda n: n
        section = lax.bitwise_xor(section, j + odd * (i - j))
        mp = lax.bitwise_xor(mp, label(i) + odd * (label(j) - label(i)))
    else:
        section, mp = j, i
    return pl.multiple_of((section * slots + mp) * block, block)


def attend(x, gain, wk, wv, q, g, direct):
    sections = len(x)
    flat = [array for arrays in x for array in arrays]
    _, rows, block = flat[0].shape
    slots = sum(array.shape[0] for array in x[0])
    length, columns = q.shape
    width = sections * slots * block
    pair = 2 * DH
    pairs = columns // pair
    factor = DH ** (-0.5)

    def kernel(*refs):
        x_refs, refs = refs[:len(flat)], refs[len(flat):]
        (gain_ref, wk_ref, wv_ref, q_ref, g_ref, low_ref, grad_low_ref, keys_ref, values_ref,
         kg_ref, vg_ref, inverse_ref, extra_ref, memory_buf) = refs
        places = [(ref, i) for ref in x_refs for i in range(ref.shape[0])]

        def wide(j, i):
            ref, n = places[j * slots + i]
            return ref[n].astype(F32)

        squares = jnp.zeros((rows, block), F32)
        for j in range(sections):
            for i in range(slots):
                squares += wide(j, i) * wide(j, i)
        inverse = lax.rsqrt(jnp.sum(squares, axis=-1, keepdims=True) / width + EPSILON)
        inverse_ref[...] = jnp.broadcast_to(inverse, inverse_ref.shape)

        keys = jnp.zeros((rows, columns), F32)
        values = jnp.zeros((rows, columns), F32)
        for j in range(sections):
            for i in range(slots):
                row = first_row(direct, j, i, slots, block, TURN_GATHER, False)
                memory = wide(j, i) * inverse * gain_ref[row // block]
                memory_buf[pl.ds(row // block, 1)] = memory.astype(BF16)[None]
        for j in range(sections):
            blocks = [memory_buf[j * slots + i] for i in range(slots)]
            memory = jnp.concatenate(blocks, axis=1)
            span = slice(j * slots * block, (j + 1) * slots * block)
            keys += dot(memory, wk_ref[span, :])
            values += dot(memory, wv_ref[span, :])
        keys_ref[...] = keys.astype(BF16)
        values_ref[...] = values.astype(BF16)

        first = lax.broadcasted_iota(jnp.int32, (rows, pair), 1) < DH
        zero = jnp.zeros((rows, pair), BF16)
        c_sum = jnp.zeros((rows, pair), F32)
        for p in range(pairs):
            at = slice(p * pair, (p + 1) * pair)
            k, v = keys_ref[:, at], values_ref[:, at]
            q, g = q_ref[:, at], g_ref[:, at]
            k_two = jnp.concatenate((jnp.where(first, k, zero), jnp.where(first, zero, k)), axis=0)
            v_two = jnp.concatenate((jnp.where(first, v, zero), jnp.where(first, zero, v)), axis=0)
            scores = dot(k_two, q, NT)
            share_grad = dot(v_two, g, NT)
            for h in range(2):
                head = slice(h * rows, (h + 1) * rows)
                score = scores[head]
                raised = jnp.exp((score - jnp.max(score, axis=0, keepdims=True)) * factor)
                shares = raised * (1.0 / jnp.sum(raised, axis=0, keepdims=True))
                low_ref[p, head, :] = shares.astype(BF16)
                grads = share_grad[head]
                mean = jnp.sum(shares * grads, axis=0, keepdims=True)
                grad_low_ref[p, head, :] = (shares * (grads - mean) * factor).astype(BF16)
            vg = dot(low_ref[p], g)
            kg = dot(grad_low_ref[p], q)
            vg = jnp.where(first, vg[:rows], vg[rows:]).astype(BF16)
            kg = jnp.where(first, kg[:rows], kg[rows:]).astype(BF16)
            vg_ref[:, at] = vg
            kg_ref[:, at] = kg
            c_sum += kg.astype(F32) * k.astype(F32) + vg.astype(F32) * v.astype(F32)

        row = jnp.sum(c_sum.T, axis=0, keepdims=True)
        row = jnp.concatenate((row, jnp.zeros((1, EXTRA_WIDTH - rows), F32)), axis=1)
        high, low = split_rows(row)
        blank = jnp.zeros((EXTRA - 2, EXTRA_WIDTH), BF16)
        extra_ref[...] = jnp.concatenate((high, low, blank), axis=0)

    return pl.pallas_call(
        kernel,
        out_shape=(
            pltpu.VMEM((pairs, 2 * rows, length), BF16),
            pltpu.VMEM((pairs, 2 * rows, length), BF16),
            pltpu.VMEM((rows, columns), BF16),
            pltpu.VMEM((rows, columns), BF16),
            pltpu.VMEM((rows, columns), BF16),
            pltpu.VMEM((rows, columns), BF16),
            pltpu.VMEM((rows, 128), F32),
            pltpu.VMEM((EXTRA, EXTRA_WIDTH), BF16),
        ),
        in_specs=[VMEM] * (len(flat) + 5),
        out_specs=(VMEM,) * 8,
        scratch_shapes=[pltpu.VMEM((sections * slots, rows, block), BF16)],
        compiler_params=pltpu.CompilerParams(vmem_limit_bytes=16 << 20),
        cost_estimate=pl.CostEstimate(
            flops=4 * rows * width * columns + 16 * length * rows * columns,
            bytes_accessed=8 * width * columns,
            transcendentals=length * rows * columns // DH,
        ),
        name="attend",
    )(*flat, in_vmem(gain), in_vmem(wk), in_vmem(wv), q, g)


def mix(shares, weights):
    pairs, both, length = shares.shape
    rows, columns = weights.shape
    pair = columns // pairs

    def kernel(shares_ref, weights_ref, out_ref):
        first = lax.broadcasted_iota(jnp.int32, (rows, pair), 1) < DH
        zero = jnp.zeros((rows, pair), BF16)
        for p in range(pairs):
            at = slice(p * pair, (p + 1) * pair)
            w = weights_ref[:, at]
            two = jnp.concatenate((jnp.where(first, w, zero), jnp.where(first, zero, w)), axis=0)
            out_ref[:, at] = dot(two.T, shares_ref[p]).T.astype(BF16)

    return pl.pallas_call(
        kernel,
        out_shape=jax.ShapeDtypeStruct((length, columns), BF16),
        in_specs=[VMEM] * 2,
        out_specs=VMEM,
        compiler_params=pltpu.CompilerParams(vmem_limit_bytes=4 << 20),
        cost_estimate=cost(1, 1),
        name="mix",
    )(in_vmem(shares), in_vmem(weights))


def project(kg, vg, wk, wv, direct, j, slots, start, count, extra=None):
    rows, columns = kg.shape
    block = BLOCK
    tail = [] if extra is None else [in_vmem(extra)]
    more = 0 if extra is None else extra.shape[0]

    def kernel(kg_ref, vg_ref, wk_ref, wv_ref, *refs):
        kg, vg, out_ref = kg_ref[...], vg_ref[...], refs[-1]
        for i in range(count):
            span = pl.ds(first_row(direct, j, start + i, slots, block, TURN_SCATTER, REORDER), block)
            part = dot(kg, wk_ref[span, :], NT) + dot(vg, wv_ref[span, :], NT)
            out_ref[i * rows:(i + 1) * rows, :] = part.astype(BF16)
        if tail:
            out_ref[count * rows:, :] = refs[0][...]

    return pl.pallas_call(
        kernel,
        out_shape=pltpu.VMEM((count * rows + more, block), BF16),
        in_specs=[VMEM] * (4 + len(tail)),
        out_specs=VMEM,
        compiler_params=pltpu.CompilerParams(vmem_limit_bytes=4 << 20),
        cost_estimate=cost(1, 1),
        name="project",
    )(in_vmem(kg), in_vmem(vg), in_vmem(wk), in_vmem(wv), *tail)


def join(parts):
    def kernel(*refs):
        for n, ref in enumerate(refs[:-1]):
            refs[-1][n] = ref[0]

    return pl.pallas_call(
        kernel,
        out_shape=pltpu.VMEM((len(parts), *parts[0].shape[1:]), BF16),
        in_specs=[VMEM] * len(parts),
        out_specs=VMEM,
        compiler_params=pltpu.CompilerParams(vmem_limit_bytes=2 << 20),
        name="join",
    )(in_vmem(parts[0]), *parts[1:])


def total_of(refs, start, size):
    total = refs[0][start:start + size, :].astype(F32)
    for ref in refs[1:]:
        total += ref[start:start + size, :].astype(F32)
    return total


def sum_c(extra, c_rows):
    return extra[:c_rows] + extra[c_rows:2 * c_rows]


def c_tail(c):
    high, low = split_rows(c)
    blank = jnp.zeros((EXTRA - 2 * c.shape[0], c.shape[1]), BF16)
    return jnp.concatenate((high, low, blank), axis=0)


def sum_chunks(chunks, rows, c_rows):
    size, block = chunks[0].shape
    count = (size - EXTRA) // rows

    def kernel(*refs):
        parts, outs = refs[:len(chunks)], refs[len(chunks):]
        tail = c_tail(sum_c(total_of(parts, size - EXTRA, EXTRA), c_rows))
        outs[-1][...] = tail
        outs[0][...] = total_of(parts, 0, rows)
        for i in range(1, count):
            outs[i][:rows, :] = total_of(parts, i * rows, rows).astype(BF16)
            outs[i][rows:, :] = tail

    return pl.pallas_call(
        kernel,
        out_shape=(pltpu.VMEM((rows, block), F32),)
        + (pltpu.VMEM((rows + EXTRA, block), BF16),) * (count - 1)
        + (pltpu.VMEM((EXTRA, block), BF16),),
        in_specs=[VMEM] * len(chunks),
        out_specs=(VMEM,) * (count + 1),
        compiler_params=pltpu.CompilerParams(vmem_limit_bytes=4 << 20),
        name="sum_chunks",
    )(*chunks)


def gain_part(own_total, parts, hidden, inverse):
    rows, block = own_total.shape

    def kernel(hidden_ref, inverse_ref, own_ref, *refs):
        part_refs, out_ref = refs[:-1], refs[-1]
        total = own_ref[...] + total_of(part_refs, 0, rows)
        normed = hidden_ref[0].astype(F32) * inverse_ref[:, 0:1]
        out_ref[...] = jnp.sum(total * normed, axis=0, keepdims=True)

    return pl.pallas_call(
        kernel,
        out_shape=pltpu.VMEM((1, block), F32),
        in_specs=[VMEM] * (3 + len(parts)),
        out_specs=VMEM,
        compiler_params=pltpu.CompilerParams(vmem_limit_bytes=4 << 20),
        name="gain_part",
    )(in_vmem(hidden), in_vmem(inverse), in_vmem(own_total), *parts)


def finish(own_total, tail, parts, hidden, gain, inverse, width, c_rows, direct, slots):
    rows, block = own_total.shape

    def kernel(hidden_ref, gain_ref, inverse_ref, own_ref, tail_ref, *refs):
        part_refs, out_ref = refs[:-1], refs[-1]
        extra = tail_ref[...].astype(F32) + total_of(part_refs, rows, EXTRA)
        c = sum_c(extra, c_rows)
        c = jnp.concatenate([c[n:n + 1] for n in range(c_rows)], axis=1)[:, :rows]
        mean = (jnp.broadcast_to(c, (rows, rows)) / width).T[:, 0:1]
        total = own_ref[...] + total_of(part_refs, 0, rows)
        inverse = inverse_ref[:, 0:1]
        normed = hidden_ref[0].astype(F32) * inverse
        out_ref[...] = inverse * (total * gain_ref[first_row(direct, 0, 0, slots, 1, False, False)] - normed * mean)

    return pl.pallas_call(
        kernel,
        out_shape=jax.ShapeDtypeStruct((rows, block), F32),
        in_specs=[VMEM] * (5 + len(parts)),
        out_specs=VMEM,
        compiler_params=pltpu.CompilerParams(vmem_limit_bytes=4 << 20),
        cost_estimate=cost(0, 64 << 10),
        name="finish",
    )(in_vmem(hidden), in_vmem(gain), in_vmem(inverse), in_vmem(own_total), in_vmem(tail), *parts)


def add_gain(mine, theirs, replicas):
    def kernel(mine_ref, theirs_ref, out_ref):
        out_ref[...] = (mine_ref[...] + theirs_ref[...]) / replicas

    return pl.pallas_call(
        kernel,
        out_shape=jax.ShapeDtypeStruct(mine.shape, F32),
        in_specs=[VMEM, VMEM],
        out_specs=VMEM,
        compiler_params=pltpu.CompilerParams(vmem_limit_bytes=1 << 20),
        name="add_gain",
    )(in_vmem(mine), theirs)


def exchange(array, step, j, turned, reordered):
    names = ("section", "dp", "mp")
    sizes = [lax.axis_size(name) for name in names]
    pairs = []
    for n in range(math.prod(sizes)):
        section, core, mp = n // (sizes[1] * sizes[2]), n // sizes[2] % sizes[1], n % sizes[2]
        if (step == 2) != (turned and core % 2 == 1):
            section ^= j
        else:
            mp ^= far_first(j) if reordered else j
        pairs.append((n, (section * sizes[1] + core) * sizes[2] + mp))
    return lax.ppermute(array, names, pairs)


def swapped(array, axis, mine):
    return jnp.stack(
        [
            lax.dynamic_index_in_dim(array, jnp.bitwise_xor(mine, i), axis, False)
            for i in range(array.shape[axis])
        ],
        axis,
    )


def per_device(enc_hidden, enc_gain, key_weight, value_weight, queries, out_grad):
    own = enc_hidden[0]
    rows, own_columns = own.shape
    wk, wv = key_weight[0], value_weight[0]
    width, columns = wk.shape
    sections = lax.axis_size("section")
    groups = lax.axis_size("mp")
    replicas = lax.axis_size("dp")
    section = lax.axis_index("section")
    mp = lax.axis_index("mp")
    direct = own_columns == BLOCK and sections == groups
    c_rows = max(rows // own_columns, 1)

    slots = groups if direct else 4
    longest = sorted(range(1, max(sections, groups)), key=lambda j: (-bin(j).count("1"), -j))
    order = {1: [j for j in longest if j < groups], 2: [j for j in longest if j < sections]}

    def swap(step, array_of, turned, reordered):
        got = {j: exchange(array_of(j), step, j, direct and turned, direct and reordered) for j in order[step]}
        return [got[j] for j in sorted(got)]

    hidden, gain, wk, wv = fetch(
        own[None], enc_gain.reshape(width // BLOCK, 1, BLOCK), wk, wv
    )
    x = join([hidden] + swap(1, lambda j: own[None], TURN_GATHER, False))
    if direct:
        x = [(x,)] + [(part,) for part in swap(2, lambda j: x, TURN_GATHER, False)]
    else:
        x = lax.all_gather(x, "section", axis=0)
        x = swapped(x, 1, mp).transpose(2, 0, 1, 3).reshape(rows, -1, slots, BLOCK)
        x = [(part,) for part in x.transpose(1, 2, 0, 3)]
    low, grad_low, keys, values, kg, vg, inverse, extra = attend(
        x, gain, wk, wv, queries[0, 0], out_grad[0, 0], direct
    )

    if direct:
        own_gain = gain
        chunks = [
            project(kg, vg, wk, wv, direct, j, slots, 0, slots, extra) for j in range(sections)
        ]
    else:
        whole = [
            project(kg, vg, wk, wv, direct, n // slots, slots, n % slots, 1)
            for n in range(width // BLOCK)
        ]
        whole = jnp.stack(whole).transpose(1, 0, 2)
        whole = whole.reshape(rows, sections, groups, own_columns).transpose(1, 2, 0, 3)
        whole = swapped(swapped(whole, 1, mp), 0, section)
        tail = extra[:2, : c_rows * own_columns].reshape(2 * c_rows, own_columns)
        tail = jnp.concatenate((tail, jnp.zeros((EXTRA - 2 * c_rows, own_columns), BF16)))
        chunks = whole.reshape(sections, groups * rows, own_columns)
        chunks = [jnp.concatenate((part, tail)) for part in chunks]
        own_gain = lax.dynamic_slice_in_dim(
            enc_gain, (section * groups + mp) * own_columns, own_columns, 0
        ).reshape(1, 1, own_columns)

    attended, query_grad = mix(low, values), mix(grad_low, keys)
    got = swap(2, lambda j: chunks[j], TURN_SCATTER, REORDER)
    first, attended, query_grad = lax.optimization_barrier((chunks[0], attended, query_grad))
    own_total, *parts, tail = sum_chunks([first] + got, rows, c_rows)
    parts = swap(1, lambda j: parts[j - 1], TURN_SCATTER, REORDER)
    gain_own = gain_part(own_total, parts, hidden, inverse)
    if replicas == 2:
        gain_other = lax.ppermute(gain_own, "dp", [(0, 1), (1, 0)])
    else:
        gain_other = lax.psum(gain_own, "dp")
        gain_own = jnp.zeros_like(gain_own)
    hidden_grad = finish(own_total, tail, parts, hidden, own_gain, inverse, width, c_rows, direct, slots)
    gain_total = add_gain(gain_own, gain_other, replicas)
    return (
        attended[None, None],
        query_grad[None, None],
        hidden_grad[None],
        gain_total[0],
    )


def solution(mesh):
    in_specs = (
        P("dp", None, ("section", "mp")),
        P(),
        P("section", None, "mp"),
        P("section", None, "mp"),
        P("dp", "section", None, "mp"),
        P("dp", "section", None, "mp"),
    )
    out_specs = (
        P("dp", "section", None, "mp"),
        P("dp", "section", None, "mp"),
        P("dp", None, ("section", "mp")),
        P(("section", "mp")),
    )
    return jax.shard_map(
        per_device, mesh=mesh, in_specs=in_specs, out_specs=out_specs, check_vma=False
    )
```

time: 52.7 us -> 50.5 us (0.958)
  Pallas kernels: 15.5 us -> 13.7 us
  starting transfers between devices: 21 us -> 19.7 us
  waiting for transfers between devices: 15.1 us -> 16.2 us
    ppermute x16 -> x12, starting transfers between devices: 21 us -> 17.3 us  [exchange(): return lax.ppermute(array, names, pairs)]
    ppermute x1, starting transfers between devices: 0.07 us -> 2.41 us  [per_device(): gain_other = lax.ppermute(gain_own, 'dp', [(0, 1), (1, 0)])]
    pallas_call x5 -> x3, Pallas kernels: 5.26 us -> 3.75 us  [the longest x1 3.6 us: fetch(): pl.pallas_call(kernel, out_shape=tuple((pltpu.VMEM(array.shape, array.dty...]
    ppermute x16 -> x12, waiting for transfers between devices: 14.9 us -> 16.2 us  [exchange(): return lax.ppermute(array, names, pairs)]
    pallas_call x8 -> x4, Pallas kernels: 3.79 us -> 3.26 us  [project(): pl.pallas_call(kernel, out_shape=pltpu.VMEM((count * rows + more, block),...]
  transfers between devices with their start and end apart: 17 -> 13, of which waited for: 9 -> 8; matrix products, arithmetic and copies ran while one was open for 0% -> 0% of each run, Pallas kernels for 20% -> 16%
where the time goes in v3:
time: 50.5 us; the launch traced here: 50.3 us
  starting transfers between devices  19.7 us (39%)
  waiting for transfers between devices  16.2 us (32%)
  Pallas kernels  13.7 us (27%)
  between operations  0.71 us (1%)
    ppermute x12, starting transfers between devices, exchange(): return lax.ppermute(array, names, pairs)  17.3 us
    ppermute x12, waiting for transfers between devices, exchange(): return lax.ppermute(array, names, pairs)  16.2 us
    pallas_call x1, Pallas kernels, fetch(): pl.pallas_call(kernel, out_shape=tuple((pltpu.VMEM(array.shape, array.dty...  3.6 us
    pallas_call x4, Pallas kernels, project(): pl.pallas_call(kernel, out_shape=pltpu.VMEM((count * rows + more, block),...  3.26 us
    pallas_call x1, Pallas kernels, attend(): pl.pallas_call(kernel, out_shape=(pltpu.VMEM((pairs, 2 * rows, length), B...  3.04 us
    ppermute x1, starting transfers between devices, per_device(): gain_other = lax.ppermute(gain_own, 'dp', [(0, 1), (1, 0)])  2.41 us
    pallas_call x2, Pallas kernels, mix(): pl.pallas_call(kernel, out_shape=jax.ShapeDtypeStruct((length, columns),...  2.1 us
  transfers between devices with their start and end apart: 13, of which 8 were waited for; matrix products, arithmetic and copies ran while one was open for 0% of the time, Pallas kernels for 16%

profile of v3, /device:TPU:0, one launch (start us, length us, event | category | flops | bytes accessed | tf_op | source)
XLA Modules:
  0.0 50.3 jit_solution(1195613219182033522)
XLA Ops:
  0.6 3.1 %collective-permute-start = (bf16[1,128,256]{2,1,0:T(8,128)(2,1)}, bf16[1,128,256]{2,1,0:T(8,128)(2,1)S(1)}, u32[]{:S(2)}, u32[]{:S(2)}) collective-permute-start(bf16[1,128,256]{2,1,0:T(8,128)(2,1)} %refs_0_.1), channel_id=1, source_target_pairs={{0,1},{1,0},{2,3},{3,2},{4,12},{5,13},{6,14},{7,15},{8,9},{9,8},{1... | collective-permute-start | bytes 196616 | tf_op jit(solution)/shard_map/ppermute | solution.py:371
  3.7 2.5 %collective-permute-start.2 = (bf16[1,128,256]{2,1,0:T(8,128)(2,1)}, bf16[1,128,256]{2,1,0:T(8,128)(2,1)S(1)}, u32[]{:S(2)}, u32[]{:S(2)}) collective-permute-start(bf16[1,128,256]{2,1,0:T(8,128)(2,1)} %refs_0_.1), channel_id=1, source_target_pairs={{0,3},{1,2},{2,1},{3,0},{4,28},{5,29},{6,30},{7,31},{8,11},{9,10},... | collective-permute-start | bytes 196616 | tf_op jit(solution)/shard_map/ppermute | solution.py:371
  6.2 0.1 collective-permute-start.1
  6.3 3.6 %fetch.1 = (bf16[1,128,256]{2,1,0:T(8,128)(2,1)S(1)}, f32[16,1,256]{2,1,0:T(1,128)S(1)}, bf16[4096,512]{1,0:T(8,128)(2,1)S(1)}, bf16[4096,512]{1,0:T(8,128)(2,1)S(1)}) custom-call(bf16[1,128,256]{2,1,0:T(8,128)(2,1)} %refs_0_.1, f32[16,1,256]{2,1,0:T(1,128)} %bitcast.16, bf16[4096,512]{1,0:T(8,128)(2,1)} %bitcast.11, bf16[4096,512]{1,0:T(8,128)(2,1)} %bitcast.12), custom_call_target="tpu_custom_call" | custom-call | bytes 16941056 | tf_op jit(solution)/shard_map/fetch/pallas_call | solution.py:63
  9.9 0.1 collective-permute-done.2.refs_3_
  10.0 2.6 %collective-permute-done.1.refs_2_ = bf16[1,128,256]{2,1,0:T(8,128)(2,1)S(1)} collective-permute-done((bf16[1,128,256]{2,1,0:T(8,128)(2,1)}, bf16[1,128,256]{2,1,0:T(8,128)(2,1)S(1)}, u32[]{:S(2)}, u32[]{:S(2)}) %collective-permute-start.1) | collective-permute-done | bytes 65568 | tf_op jit(solution)/shard_map/ppermute | solution.py:371
  12.6 2.5 %collective-permute-start.5 = (bf16[4,128,256]{2,1,0:T(8,128)(2,1)S(1)}, bf16[4,128,256]{2,1,0:T(8,128)(2,1)S(1)}, u32[]{:S(2)}, u32[]{:S(2)}) collective-permute-start(bf16[4,128,256]{2,1,0:T(8,128)(2,1)S(1)} %join.1.refs_0_), channel_id=1, source_target_pairs={{0,24},{1,25},{2,26},{3,27},{4,7},{5,6},{6,5},{7,4},{8,16},{9,17},... | collective-permute-start | bytes 786440 | tf_op jit(solution)/shard_map/ppermute | solution.py:371
  15.1 0.5 %collective-permute-start.4 = (bf16[4,128,256]{2,1,0:T(8,128)(2,1)S(1)}, bf16[4,128,256]{2,1,0:T(8,128)(2,1)S(1)}, u32[]{:S(2)}, u32[]{:S(2)}) collective-permute-start(bf16[4,128,256]{2,1,0:T(8,128)(2,1)S(1)} %join.1.refs_0_), channel_id=1, source_target_pairs={{0,16},{1,17},{2,18},{3,19},{4,6},{5,7},{6,4},{7,5},{8,24},{9,25},... | collective-permute-start | bytes 786440 | tf_op jit(solution)/shard_map/ppermute | solution.py:371
  15.6 0.5 %collective-permute-start.3 = (bf16[4,128,256]{2,1,0:T(8,128)(2,1)S(1)}, bf16[4,128,256]{2,1,0:T(8,128)(2,1)S(1)}, u32[]{:S(2)}, u32[]{:S(2)}) collective-permute-start(bf16[4,128,256]{2,1,0:T(8,128)(2,1)S(1)} %join.1.refs_0_), channel_id=1, source_target_pairs={{0,8},{1,9},{2,10},{3,11},{4,5},{5,4},{6,7},{7,6},{8,0},{9,1},{10,... | collective-permute-start | bytes 786440 | tf_op jit(solution)/shard_map/ppermute | solution.py:371
  16.1 3.9 %collective-permute-done.5.refs_3_ = bf16[4,128,256]{2,1,0:T(8,128)(2,1)S(1)} collective-permute-done((bf16[4,128,256]{2,1,0:T(8,128)(2,1)S(1)}, bf16[4,128,256]{2,1,0:T(8,128)(2,1)S(1)}, u32[]{:S(2)}, u32[]{:S(2)}) %collective-permute-start.5) | collective-permute-done | bytes 262176 | tf_op jit(solution)/shard_map/ppermute | solution.py:371
  20.0 2.7 %collective-permute-done.4.refs_2_ = bf16[4,128,256]{2,1,0:T(8,128)(2,1)S(1)} collective-permute-done((bf16[4,128,256]{2,1,0:T(8,128)(2,1)S(1)}, bf16[4,128,256]{2,1,0:T(8,128)(2,1)S(1)}, u32[]{:S(2)}, u32[]{:S(2)}) %collective-permute-start.4) | collective-permute-done | bytes 262176 | tf_op jit(solution)/shard_map/ppermute | solution.py:371
  22.7 0.1 collective-permute-done.3.refs_1_
  22.8 3.0 %attend.1 = (bf16[4,256,256]{2,1,0:T(8,128)(2,1)S(1)}, bf16[4,256,256]{2,1,0:T(8,128)(2,1)S(1)}, bf16[128,512]{1,0:T(8,128)(2,1)S(1)}, bf16[128,512]{1,0:T(8,128...) custom-call(bf16[4,128,256]{2,1,0:T(8,128)(2,1)S(1)} %join.1.refs_0_, ...), custom_call_target="tpu_custom_call" | custom-call | flops 1342177280 | bytes 16777216 | tf_op jit(solution)/shard_map/attend/pallas_call | solution.py:169
  25.9 0.8 %project.6 = bf16[528,256]{1,0:T(8,128)(2,1)S(1)} custom-call(bf16[128,512]{1,0:T(8,128)(2,1)S(1)} %get-tuple-element.28.kg_ref, bf16[128,512]{1,0:T(8,128)(2,1)S(1)} %get-tuple-element.29.vg_ref, bf16[4096,512]{1,0:T(8,128)(2,1)S(1)} %get-tuple-element.26.refs_5_.wk_ref, bf16[4096,512]{1,0:T(8,128)(2,1)S(1)} %get-tuple-element.27.refs_6_.wv_ref, ...), custom_call_target="tpu_custom_call" | custom-call | flops 1 | bytes 1 | tf_op jit(solution)/shard_map/project/pallas_call | solution.py:234
  26.7 0.8 %project.5 = bf16[528,256]{1,0:T(8,128)(2,1)S(1)} custom-call(bf16[128,512]{1,0:T(8,128)(2,1)S(1)} %get-tuple-element.28.kg_ref, bf16[128,512]{1,0:T(8,128)(2,1)S(1)} %get-tuple-element.29.vg_ref, bf16[4096,512]{1,0:T(8,128)(2,1)S(1)} %get-tuple-element.26.refs_5_.wk_ref, bf16[4096,512]{1,0:T(8,128)(2,1)S(1)} %get-tuple-element.27.refs_6_.wv_ref, ...), custom_call_target="tpu_custom_call" | custom-call | flops 1 | bytes 1 | tf_op jit(solution)/shard_map/project/pallas_call | solution.py:234
  27.6 1.6 %collective-permute-start.6 = (bf16[528,256]{1,0:T(8,128)(2,1)S(1)}, bf16[528,256]{1,0:T(8,128)(2,1)S(1)}, u32[]{:S(2)}, u32[]{:S(2)}) collective-permute-start(bf16[528,256]{1,0:T(8,128)(2,1)S(1)} %project.5), channel_id=1, source_target_pairs={{0,8},{1,9},{2,10},{3,11},{4,7},{5,6},{6,5},{7,4},{8,0},{9,1},{10,... | collective-permute-start | bytes 811016 | tf_op jit(solution)/shard_map/ppermute | solution.py:371
  29.1 1.0 %collective-permute-start.7 = (bf16[528,256]{1,0:T(8,128)(2,1)S(1)}, bf16[528,256]{1,0:T(8,128)(2,1)S(1)}, u32[]{:S(2)}, u32[]{:S(2)}) collective-permute-start(bf16[528,256]{1,0:T(8,128)(2,1)S(1)} %project.6), channel_id=1, source_target_pairs={{0,16},{1,17},{2,18},{3,19},{4,6},{5,7},{6,4},{7,5},{8,24},{9,25},... | collective-permute-start | bytes 811016 | tf_op jit(solution)/shard_map/ppermute | solution.py:371
  30.1 0.8 %project.7 = bf16[528,256]{1,0:T(8,128)(2,1)S(1)} custom-call(bf16[128,512]{1,0:T(8,128)(2,1)S(1)} %get-tuple-element.28.kg_ref, bf16[128,512]{1,0:T(8,128)(2,1)S(1)} %get-tuple-element.29.vg_ref, bf16[4096,512]{1,0:T(8,128)(2,1)S(1)} %get-tuple-element.26.refs_5_.wk_ref, bf16[4096,512]{1,0:T(8,128)(2,1)S(1)} %get-tuple-element.27.refs_6_.wv_ref, ...), custom_call_target="tpu_custom_call" | custom-call | flops 1 | bytes 1 | tf_op jit(solution)/shard_map/project/pallas_call | solution.py:234
  30.9 1.1 %collective-permute-start.8 = (bf16[528,256]{1,0:T(8,128)(2,1)S(1)}, bf16[528,256]{1,0:T(8,128)(2,1)S(1)}, u32[]{:S(2)}, u32[]{:S(2)}) collective-permute-start(bf16[528,256]{1,0:T(8,128)(2,1)S(1)} %project.7), channel_id=1, source_target_pairs={{0,24},{1,25},{2,26},{3,27},{4,5},{5,4},{6,7},{7,6},{8,16},{9,17},... | collective-permute-start | bytes 811016 | tf_op jit(solution)/shard_map/ppermute | solution.py:371
  32.0 0.8 %project.4.refs_0_ = bf16[528,256]{1,0:T(8,128)(2,1)S(1)} custom-call(bf16[128,512]{1,0:T(8,128)(2,1)S(1)} %get-tuple-element.28.kg_ref, bf16[128,512]{1,0:T(8,128)(2,1)S(1)} %get-tuple-element.29.vg_ref, bf16[4096,512]{1,0:T(8,128)(2,1)S(1)} %get-tuple-element.26.refs_5_.wk_ref, bf16[4096,512]{1,0:T(8,128)(2,1)S(1)} %get-tuple-element.27.refs_6_.wv_ref, ...), custom_call_target="tpu_custom_call" | custom-call | flops 1 | bytes 1 | tf_op jit(solution)/shard_map/project/pallas_call | solution.py:234
  32.8 1.1 %mix.2 = bf16[256,512]{1,0:T(8,128)(2,1)} custom-call(bf16[4,256,256]{2,1,0:T(8,128)(2,1)S(1)} %get-tuple-element.31.shares_ref, bf16[128,512]{1,0:T(8,128)(2,1)S(1)} %get-tuple-element.32.weights_ref), custom_call_target="tpu_custom_call" | custom-call | flops 1 | bytes 1 | tf_op jit(solution)/shard_map/mix/pallas_call | solution.py:208
  33.8 1.1 %mix.3 = bf16[256,512]{1,0:T(8,128)(2,1)} custom-call(bf16[4,256,256]{2,1,0:T(8,128)(2,1)S(1)} %get-tuple-element.33.shares_ref, bf16[128,512]{1,0:T(8,128)(2,1)S(1)} %get-tuple-element.34.weights_ref), custom_call_target="tpu_custom_call" | custom-call | flops 1 | bytes 1 | tf_op jit(solution)/shard_map/mix/pallas_call | solution.py:208
  34.9 3.6 %collective-permute-done.7.refs_2_ = bf16[528,256]{1,0:T(8,128)(2,1)S(1)} collective-permute-done((bf16[528,256]{1,0:T(8,128)(2,1)S(1)}, bf16[528,256]{1,0:T(8,128)(2,1)S(1)}, u32[]{:S(2)}, u32[]{:S(2)}) %collective-permute-start.7) | collective-permute-done | bytes 270368 | tf_op jit(solution)/shard_map/ppermute | solution.py:371
  38.5 0.1 sum_chunks.1
  38.6 1.4 %collective-permute-start.9 = (bf16[144,256]{1,0:T(8,128)(2,1)S(1)}, bf16[144,256]{1,0:T(8,128)(2,1)S(1)}, u32[]{:S(2)}, u32[]{:S(2)}) collective-permute-start(bf16[144,256]{1,0:T(8,128)(2,1)S(1)} %get-tuple-element.41), channel_id=1, source_target_pairs={{0,3},{1,2},{2,1},{3,0},{4,12},{5,13},{6,14},{7,15},{8,11},{9,10},... | collective-permute-start | bytes 221192 | tf_op jit(solution)/shard_map/ppermute | solution.py:371
  40.0 3.1 %collective-permute-start.11 = (bf16[144,256]{1,0:T(8,128)(2,1)S(1)}, bf16[144,256]{1,0:T(8,128)(2,1)S(1)}, u32[]{:S(2)}, u32[]{:S(2)}) collective-permute-start(bf16[144,256]{1,0:T(8,128)(2,1)S(1)} %get-tuple-element.43), channel_id=1, source_target_pairs={{0,1},{1,0},{2,3},{3,2},{4,28},{5,29},{6,30},{7,31},{8,9},{9,8},{1... | collective-permute-start | bytes 221192 | tf_op jit(solution)/shard_map/ppermute | solution.py:371
  43.1 1.8 %collective-permute-done.9.refs_0_ = bf16[144,256]{1,0:T(8,128)(2,1)S(1)} collective-permute-done((bf16[144,256]{1,0:T(8,128)(2,1)S(1)}, bf16[144,256]{1,0:T(8,128)(2,1)S(1)}, u32[]{:S(2)}, u32[]{:S(2)}) %collective-permute-start.9) | collective-permute-done | bytes 73760 | tf_op jit(solution)/shard_map/ppermute | solution.py:371
  44.9 1.5 %collective-permute-done.10.refs_1_ = bf16[144,256]{1,0:T(8,128)(2,1)S(1)} collective-permute-done((bf16[144,256]{1,0:T(8,128)(2,1)S(1)}, bf16[144,256]{1,0:T(8,128)(2,1)S(1)}, u32[]{:S(2)}, u32[]{:S(2)}) %collective-permute-start.10) | collective-permute-done | bytes 73760 | tf_op jit(solution)/shard_map/ppermute | solution.py:371
  46.4 0.1 gain_part.1.mine_ref
  46.5 2.4 %collective-permute-start.12 = (f32[1,256]{1,0:T(1,128)S(1)}, f32[1,256]{1,0:T(1,128)S(1)}, u32[]{:S(2)}, u32[]{:S(2)}) collective-permute-start(f32[1,256]{1,0:T(1,128)S(1)} %gain_part.1.mine_ref), channel_id=1, source_target_pairs={{0,4},{4,0},{1,5},{5,1},{2,6},{6,2},{3,7},{7,3},{8,12},{12,8},{9,1... | collective-permute-start | bytes 3080 | tf_op jit(solution)/shard_map/ppermute | solution.py:447
  48.9 0.8 %finish.1 = f32[128,256]{1,0:T(8,128)} custom-call(bf16[1,128,256]{2,1,0:T(8,128)(2,1)S(1)} %get-tuple-element.24.refs_0_.hidden_ref, f32[16,1,256]{2,1,0:T(1,128)S(1)} %get-tuple-element.25.refs_4_.gain_ref, f32[128,128]{1,0:T(8,128)S(1)} %get-tuple-element.37.inverse_ref, f32[128,256]{1,0:T(8,128)S(1)} %get-tuple-element.39.own_ref, ...), custom_call_target="tpu_custom_call" | custom-call | bytes 65536 | tf_op jit(solution)/shard_map/finish/pallas_call | solution.py:335
  49.8 0.6 %add_gain.1 = f32[1,256]{1,0:T(1,128)} custom-call(f32[1,256]{1,0:T(1,128)S(1)} %gain_part.1.mine_ref, f32[1,256]{1,0:T(1,128)S(1)} %collective-permute-done.12.theirs_ref), custom_call_target="tpu_custom_call" | custom-call | tf_op jit(solution)/shard_map/add_gain/pallas_call | solution.py:350
  (11 shorter events, 0.0 us)
Async XLA Ops:
  0.6 9.3 %collective-permute-start = (bf16[1,128,256]{2,1,0:T(8,128)(2,1)}, bf16[1,128,256]{2,1,0:T(8,128)(2,1)S(1)}, u32[]{:S(2)}, u32[]{:S(2)}) collective-permute-start(bf16[1,128,256]{2,1,0:T(8,128)(2,1)} %refs_0_.1), channel_id=1, source_target_pairs={{0,1},{1,0},{2,3},{3,2},{4,12},{5,13},{6,14},{7,15},{8,9},{9,8},{1... | collective-permute-start | bytes 196616 | tf_op jit(solution)/shard_map/ppermute | solution.py:371
  3.7 6.3 %collective-permute-start.2 = (bf16[1,128,256]{2,1,0:T(8,128)(2,1)}, bf16[1,128,256]{2,1,0:T(8,128)(2,1)S(1)}, u32[]{:S(2)}, u32[]{:S(2)}) collective-permute-start(bf16[1,128,256]{2,1,0:T(8,128)(2,1)} %refs_0_.1), channel_id=1, source_target_pairs={{0,3},{1,2},{2,1},{3,0},{4,28},{5,29},{6,30},{7,31},{8,11},{9,10},... | collective-permute-start | bytes 196616 | tf_op jit(solution)/shard_map/ppermute | solution.py:371
  6.2 6.4 %collective-permute-start.1 = (bf16[1,128,256]{2,1,0:T(8,128)(2,1)}, bf16[1,128,256]{2,1,0:T(8,128)(2,1)S(1)}, u32[]{:S(2)}, u32[]{:S(2)}) collective-permute-start(bf16[1,128,256]{2,1,0:T(8,128)(2,1)} %refs_0_.1), channel_id=1, source_target_pairs={{0,2},{1,3},{2,0},{3,1},{4,20},{5,21},{6,22},{7,23},{8,10},{9,11},... | collective-permute-start | bytes 196616 | tf_op jit(solution)/shard_map/ppermute | solution.py:371
  6.3 16.5 %copy-start = (bf16[1,1,256,512]{3,2,1,0:T(8,128)(2,1)S(1)}, bf16[1,1,256,512]{3,2,1,0:T(8,128)(2,1)}, u32[]{:S(2)}) copy-start(bf16[1,1,256,512]{3,2,1,0:T(8,128)(2,1)} %param.10) | copy-start | bytes 786436
  6.3 16.5 %copy-start.1 = (bf16[1,1,256,512]{3,2,1,0:T(8,128)(2,1)S(1)}, bf16[1,1,256,512]{3,2,1,0:T(8,128)(2,1)}, u32[]{:S(2)}) copy-start(bf16[1,1,256,512]{3,2,1,0:T(8,128)(2,1)} %param.11) | copy-start | bytes 786436
  12.6 7.4 %collective-permute-start.5 = (bf16[4,128,256]{2,1,0:T(8,128)(2,1)S(1)}, bf16[4,128,256]{2,1,0:T(8,128)(2,1)S(1)}, u32[]{:S(2)}, u32[]{:S(2)}) collective-permute-start(bf16[4,128,256]{2,1,0:T(8,128)(2,1)S(1)} %join.1.refs_0_), channel_id=1, source_target_pairs={{0,24},{1,25},{2,26},{3,27},{4,7},{5,6},{6,5},{7,4},{8,16},{9,17},... | collective-permute-start | bytes 786440 | tf_op jit(solution)/shard_map/ppermute | solution.py:371
  15.1 7.6 %collective-permute-start.4 = (bf16[4,128,256]{2,1,0:T(8,128)(2,1)S(1)}, bf16[4,128,256]{2,1,0:T(8,128)(2,1)S(1)}, u32[]{:S(2)}, u32[]{:S(2)}) collective-permute-start(bf16[4,128,256]{2,1,0:T(8,128)(2,1)S(1)} %join.1.refs_0_), channel_id=1, source_target_pairs={{0,16},{1,17},{2,18},{3,19},{4,6},{5,7},{6,4},{7,5},{8,24},{9,25},... | collective-permute-start | bytes 786440 | tf_op jit(solution)/shard_map/ppermute | solution.py:371
  15.6 7.2 %collective-permute-start.3 = (bf16[4,128,256]{2,1,0:T(8,128)(2,1)S(1)}, bf16[4,128,256]{2,1,0:T(8,128)(2,1)S(1)}, u32[]{:S(2)}, u32[]{:S(2)}) collective-permute-start(bf16[4,128,256]{2,1,0:T(8,128)(2,1)S(1)} %join.1.refs_0_), channel_id=1, source_target_pairs={{0,8},{1,9},{2,10},{3,11},{4,5},{5,4},{6,7},{7,6},{8,0},{9,1},{10,... | collective-permute-start | bytes 786440 | tf_op jit(solution)/shard_map/ppermute | solution.py:371
  27.6 7.3 %collective-permute-start.6 = (bf16[528,256]{1,0:T(8,128)(2,1)S(1)}, bf16[528,256]{1,0:T(8,128)(2,1)S(1)}, u32[]{:S(2)}, u32[]{:S(2)}) collective-permute-start(bf16[528,256]{1,0:T(8,128)(2,1)S(1)} %project.5), channel_id=1, source_target_pairs={{0,8},{1,9},{2,10},{3,11},{4,7},{5,6},{6,5},{7,4},{8,0},{9,1},{10,... | collective-permute-start | bytes 811016 | tf_op jit(solution)/shard_map/ppermute | solution.py:371
  29.1 9.4 %collective-permute-start.7 = (bf16[528,256]{1,0:T(8,128)(2,1)S(1)}, bf16[528,256]{1,0:T(8,128)(2,1)S(1)}, u32[]{:S(2)}, u32[]{:S(2)}) collective-permute-start(bf16[528,256]{1,0:T(8,128)(2,1)S(1)} %project.6), channel_id=1, source_target_pairs={{0,16},{1,17},{2,18},{3,19},{4,6},{5,7},{6,4},{7,5},{8,24},{9,25},... | collective-permute-start | bytes 811016 | tf_op jit(solution)/shard_map/ppermute | solution.py:371
  30.9 7.5 %collective-permute-start.8 = (bf16[528,256]{1,0:T(8,128)(2,1)S(1)}, bf16[528,256]{1,0:T(8,128)(2,1)S(1)}, u32[]{:S(2)}, u32[]{:S(2)}) collective-permute-start(bf16[528,256]{1,0:T(8,128)(2,1)S(1)} %project.7), channel_id=1, source_target_pairs={{0,24},{1,25},{2,26},{3,27},{4,5},{5,4},{6,7},{7,6},{8,16},{9,17},... | collective-permute-start | bytes 811016 | tf_op jit(solution)/shard_map/ppermute | solution.py:371
  38.6 6.3 %collective-permute-start.9 = (bf16[144,256]{1,0:T(8,128)(2,1)S(1)}, bf16[144,256]{1,0:T(8,128)(2,1)S(1)}, u32[]{:S(2)}, u32[]{:S(2)}) collective-permute-start(bf16[144,256]{1,0:T(8,128)(2,1)S(1)} %get-tuple-element.41), channel_id=1, source_target_pairs={{0,3},{1,2},{2,1},{3,0},{4,12},{5,13},{6,14},{7,15},{8,11},{9,10},... | collective-permute-start | bytes 221192 | tf_op jit(solution)/shard_map/ppermute | solution.py:371
  40.0 6.4 %collective-permute-start.10 = (bf16[144,256]{1,0:T(8,128)(2,1)S(1)}, bf16[144,256]{1,0:T(8,128)(2,1)S(1)}, u32[]{:S(2)}, u32[]{:S(2)}) collective-permute-start(bf16[144,256]{1,0:T(8,128)(2,1)S(1)} %get-tuple-element.42), channel_id=1, source_target_pairs={{0,2},{1,3},{2,0},{3,1},{4,20},{5,21},{6,22},{7,23},{8,10},{9,11},... | collective-permute-start | bytes 221192 | tf_op jit(solution)/shard_map/ppermute | solution.py:371
  40.0 6.4 %collective-permute-start.11 = (bf16[144,256]{1,0:T(8,128)(2,1)S(1)}, bf16[144,256]{1,0:T(8,128)(2,1)S(1)}, u32[]{:S(2)}, u32[]{:S(2)}) collective-permute-start(bf16[144,256]{1,0:T(8,128)(2,1)S(1)} %get-tuple-element.43), channel_id=1, source_target_pairs={{0,1},{1,0},{2,3},{3,2},{4,28},{5,29},{6,30},{7,31},{8,9},{9,8},{1... | collective-permute-start | bytes 221192 | tf_op jit(solution)/shard_map/ppermute | solution.py:371
  46.5 3.3 %collective-permute-start.12 = (f32[1,256]{1,0:T(1,128)S(1)}, f32[1,256]{1,0:T(1,128)S(1)}, u32[]{:S(2)}, u32[]{:S(2)}) collective-permute-start(f32[1,256]{1,0:T(1,128)S(1)} %gain_part.1.mine_ref), channel_id=1, source_target_pairs={{0,4},{4,0},{1,5},{5,1},{2,6},{6,2},{3,7},{7,3},{8,12},{12,8},{9,1... | collective-permute-start | bytes 3080 | tf_op jit(solution)/shard_map/ppermute | solution.py:447

commit v4 on v3

--- a/solution.py
+++ b/solution.py
@@ -12,9 +12,7 @@
 BLOCK = 256
 EXTRA = 16
 EXTRA_WIDTH = 256
-TURN_GATHER = True
-TURN_SCATTER = True
-REORDER = True
+PAD = 32
 F32 = jnp.float32
 BF16 = jnp.bfloat16
 VMEM = pl.BlockSpec(memory_space=pltpu.VMEM)
@@ -47,14 +45,31 @@
     return pltpu.with_memory_space_constraint(array, pltpu.HBM)
 
 
-def fetch(*arrays):
-    count = len(arrays)
+def block_at(direct, j, i, slots):
+    if not direct:
+        return j * slots + i
+    section, mp, core = (lax.axis_index(name) for name in ("section", "mp", "dp"))
+    turn = lax.rem(core, 2) * (i - j)
+    return lax.bitwise_xor(section, j + turn) * slots + lax.bitwise_xor(mp, i - turn)
+
+
+def fetch(hidden, gain, wk, wv, sections, slots, direct):
+    width, columns = wk.shape
+    block = width // (sections * slots)
 
     def kernel(*refs):
-        sems = refs[-1]
-        copies = [
-            pltpu.make_async_copy(refs[n], refs[count + n], sems.at[n]) for n in range(count)
-        ]
+        ins, outs, few, many = refs[:4], refs[4:8], refs[8], refs[9]
+        copies = [pltpu.make_async_copy(ins[n], outs[n], few.at[n]) for n in range(2)]
+        for j in range(sections):
+            for i in range(slots):
+                row = pl.multiple_of(block_at(direct, j, i, slots) * block, block)
+                n = j * slots + i
+                copies += [
+                    pltpu.make_async_copy(
+                        ins[2 + w].at[pl.ds(row, block), :], outs[2 + w].at[n], many.at[w, n]
+                    )
+                    for w in range(2)
+                ]
         for copy in copies:
             copy.start()
         for copy in copies:
@@ -62,30 +77,21 @@
 
     return pl.pallas_call(
         kernel,
-        out_shape=tuple(pltpu.VMEM(array.shape, array.dtype) for array in arrays),
-        in_specs=[HBM] * count,
-        out_specs=(VMEM,) * count,
-        scratch_shapes=[pltpu.SemaphoreType.DMA((count,))],
+        out_shape=(
+            pltpu.VMEM(hidden.shape, BF16),
+            pltpu.VMEM(gain.shape, F32),
+            pltpu.VMEM((sections * slots, block, columns), BF16),
+            pltpu.VMEM((sections * slots, block, columns), BF16),
+        ),
+        in_specs=[HBM] * 4,
+        out_specs=(VMEM,) * 4,
+        scratch_shapes=[
+            pltpu.SemaphoreType.DMA((2,)), pltpu.SemaphoreType.DMA((2, sections * slots))
+        ],
         compiler_params=pltpu.CompilerParams(vmem_limit_bytes=1 << 20),
-        cost_estimate=cost(0, 2 * sum(a.size * a.dtype.itemsize for a in arrays)),
+        cost_estimate=cost(0, 8 * width * columns),
         name="fetch",
-    )(*map(in_hbm, arrays))
-
-
-def far_first(j):
-    return j ^ (j & 1) * 2
-
-
-def first_row(direct, j, i, slots, block, turned, reordered):
-    if direct:
-        section, mp, core = (lax.axis_index(name) for name in ("section", "mp", "dp"))
-        odd = lax.rem(core, 2) if turned else 0
-        label = far_first if reordered else lambda n: n
-        section = lax.bitwise_xor(section, j + odd * (i - j))
-        mp = lax.bitwise_xor(mp, label(i) + odd * (label(j) - label(i)))
-    else:
-        section, mp = j, i
-    return pl.multiple_of((section * slots + mp) * block, block)
+    )(*map(in_hbm, (hidden, gain, wk, wv)))
 
 
 def attend(x, gain, wk, wv, q, g, direct):
@@ -120,15 +126,11 @@
         values = jnp.zeros((rows, columns), F32)
         for j in range(sections):
             for i in range(slots):
-                row = first_row(direct, j, i, slots, block, TURN_GATHER, False)
-                memory = wide(j, i) * inverse * gain_ref[row // block]
-                memory_buf[pl.ds(row // block, 1)] = memory.astype(BF16)[None]
-        for j in range(sections):
-            blocks = [memory_buf[j * slots + i] for i in range(slots)]
-            memory = jnp.concatenate(blocks, axis=1)
-            span = slice(j * slots * block, (j + 1) * slots * block)
-            keys += dot(memory, wk_ref[span, :])
-            values += dot(memory, wv_ref[span, :])
+                memory = wide(j, i) * inverse * gain_ref[block_at(direct, j, i, slots)]
+                memory_buf[:, i * block:(i + 1) * block] = memory.astype(BF16)
+            span = slice(j * slots, (j + 1) * slots)
+            keys += dot(memory_buf[...], wk_ref[span].reshape(slots * block, columns))
+            values += dot(memory_buf[...], wv_ref[span].reshape(slots * block, columns))
         keys_ref[...] = keys.astype(BF16)
         values_ref[...] = values.astype(BF16)
 
@@ -180,7 +182,7 @@
         ),
         in_specs=[VMEM] * (len(flat) + 5),
         out_specs=(VMEM,) * 8,
-        scratch_shapes=[pltpu.VMEM((sections * slots, rows, block), BF16)],
+        scratch_shapes=[pltpu.VMEM((rows, slots * block), BF16)],
         compiler_params=pltpu.CompilerParams(vmem_limit_bytes=16 << 20),
         cost_estimate=pl.CostEstimate(
             flops=4 * rows * width * columns + 16 * length * rows * columns,
@@ -216,24 +218,26 @@
     )(in_vmem(shares), in_vmem(weights))
 
 
-def project(kg, vg, wk, wv, direct, j, slots, start, count, extra=None):
+def project(kg, vg, wk, wv, start, count, extra=None, size=0):
     rows, columns = kg.shape
-    block = BLOCK
+    block = wk.shape[1]
     tail = [] if extra is None else [in_vmem(extra)]
-    more = 0 if extra is None else extra.shape[0]
+    end = count * rows + EXTRA * len(tail)
+    size = max(size, end)
 
     def kernel(kg_ref, vg_ref, wk_ref, wv_ref, *refs):
         kg, vg, out_ref = kg_ref[...], vg_ref[...], refs[-1]
         for i in range(count):
-            span = pl.ds(first_row(direct, j, start + i, slots, block, TURN_SCATTER, REORDER), block)
-            part = dot(kg, wk_ref[span, :], NT) + dot(vg, wv_ref[span, :], NT)
+            part = dot(kg, wk_ref[start + i], NT) + dot(vg, wv_ref[start + i], NT)
             out_ref[i * rows:(i + 1) * rows, :] = part.astype(BF16)
         if tail:
-            out_ref[count * rows:, :] = refs[0][...]
-
-    return pl.pallas_call(
-        kernel,
-        out_shape=pltpu.VMEM((count * rows + more, block), BF16),
+            out_ref[count * rows:end, :] = refs[0][...]
+        if size > end:
+            out_ref[end:, :] = jnp.zeros((size - end, block), BF16)
+
+    return pl.pallas_call(
+        kernel,
+        out_shape=pltpu.VMEM((size, block), BF16),
         in_specs=[VMEM] * (4 + len(tail)),
         out_specs=VMEM,
         compiler_params=pltpu.CompilerParams(vmem_limit_bytes=4 << 20),
@@ -274,13 +278,12 @@
     return jnp.concatenate((high, low, blank), axis=0)
 
 
-def sum_chunks(chunks, rows, c_rows):
-    size, block = chunks[0].shape
-    count = (size - EXTRA) // rows
+def sum_chunks(chunks, count, rows, c_rows):
+    block = chunks[0].shape[1]
 
     def kernel(*refs):
         parts, outs = refs[:len(chunks)], refs[len(chunks):]
-        tail = c_tail(sum_c(total_of(parts, size - EXTRA, EXTRA), c_rows))
+        tail = c_tail(sum_c(total_of(parts, count * rows, EXTRA), c_rows))
         outs[-1][...] = tail
         outs[0][...] = total_of(parts, 0, rows)
         for i in range(1, count):
@@ -330,7 +333,7 @@
         total = own_ref[...] + total_of(part_refs, 0, rows)
         inverse = inverse_ref[:, 0:1]
         normed = hidden_ref[0].astype(F32) * inverse
-        out_ref[...] = inverse * (total * gain_ref[first_row(direct, 0, 0, slots, 1, False, False)] - normed * mean)
+        out_ref[...] = inverse * (total * gain_ref[block_at(direct, 0, 0, slots)] - normed * mean)
 
     return pl.pallas_call(
         kernel,
@@ -357,16 +360,16 @@
     )(in_vmem(mine), theirs)
 
 
-def exchange(array, step, j, turned, reordered):
+def exchange(array, step, j, direct):
     names = ("section", "dp", "mp")
     sizes = [lax.axis_size(name) for name in names]
     pairs = []
     for n in range(math.prod(sizes)):
         section, core, mp = n // (sizes[1] * sizes[2]), n // sizes[2] % sizes[1], n % sizes[2]
-        if (step == 2) != (turned and core % 2 == 1):
+        if (step == 2) != (direct and core % 2 == 1):
             section ^= j
         else:
-            mp ^= far_first(j) if reordered else j
+            mp ^= j
         pairs.append((n, (section * sizes[1] + core) * sizes[2] + mp))
     return lax.ppermute(array, names, pairs)
 
@@ -395,19 +398,17 @@
     c_rows = max(rows // own_columns, 1)
 
     slots = groups if direct else 4
-    longest = sorted(range(1, max(sections, groups)), key=lambda j: (-bin(j).count("1"), -j))
-    order = {1: [j for j in longest if j < groups], 2: [j for j in longest if j < sections]}
-
-    def swap(step, array_of, turned, reordered):
-        got = {j: exchange(array_of(j), step, j, direct and turned, direct and reordered) for j in order[step]}
-        return [got[j] for j in sorted(got)]
-
-    hidden, gain, wk, wv = fetch(
-        own[None], enc_gain.reshape(width // BLOCK, 1, BLOCK), wk, wv
-    )
-    x = join([hidden] + swap(1, lambda j: own[None], TURN_GATHER, False))
+
+    def swap(step, arrays):
+        got = [exchange(array, step, j, direct) for j, array in enumerate(arrays) if j]
+        return [arrays[0]] + got
+
+    gain = enc_gain.reshape(width // BLOCK, 1, BLOCK)
+    parts = width // (slots * BLOCK)
+    hidden, gain, wk, wv = fetch(own[None], gain, wk, wv, parts, slots, direct)
+    x = join([hidden] + swap(1, [own[None]] * groups)[1:])
     if direct:
-        x = [(x,)] + [(part,) for part in swap(2, lambda j: x, TURN_GATHER, False)]
+        x = [(part,) for part in swap(2, [x] * sections)]
     else:
         x = lax.all_gather(x, "section", axis=0)
         x = swapped(x, 1, mp).transpose(2, 0, 1, 3).reshape(rows, -1, slots, BLOCK)
@@ -418,13 +419,15 @@
 
     if direct:
         own_gain = gain
-        chunks = [
-            project(kg, vg, wk, wv, direct, j, slots, 0, slots, extra) for j in range(sections)
-        ]
+        size = {sections - 1: slots * rows + EXTRA + PAD}
+        chunks = {
+            j: project(kg, vg, wk, wv, j * slots, slots, extra, size.get(j, 0))
+            for j in (0, *range(sections - 1, 0, -1))
+        }
+        chunks = [chunks[j] for j in range(sections)]
     else:
         whole = [
-            project(kg, vg, wk, wv, direct, n // slots, slots, n % slots, 1)
-            for n in range(width // BLOCK)
+            project(kg, vg, wk, wv, n, 1) for n in range(width // BLOCK)
         ]
         whole = jnp.stack(whole).transpose(1, 0, 2)
         whole = whole.reshape(rows, sections, groups, own_columns).transpose(1, 2, 0, 3)
@@ -438,10 +441,10 @@
         ).reshape(1, 1, own_columns)
 
     attended, query_grad = mix(low, values), mix(grad_low, keys)
-    got = swap(2, lambda j: chunks[j], TURN_SCATTER, REORDER)
-    first, attended, query_grad = lax.optimization_barrier((chunks[0], attended, query_grad))
-    own_total, *parts, tail = sum_chunks([first] + got, rows, c_rows)
-    parts = swap(1, lambda j: parts[j - 1], TURN_SCATTER, REORDER)
+    first, *got = swap(2, chunks)
+    first, attended, query_grad = lax.optimization_barrier((first, attended, query_grad))
+    own_total, *parts, tail = sum_chunks([first] + got[::-1], groups, rows, c_rows)
+    parts = swap(1, [own_total] + parts)[:0:-1]
     gain_own = gain_part(own_total, parts, hidden, inverse)
     if replicas == 2:
         gain_other = lax.ppermute(gain_own, "dp", [(0, 1), (1, 0)])

time: 50.5 us -> 48.9 us (0.968)
  waiting for transfers between devices: 16.2 us -> 15.4 us
  starting transfers between devices: 19.7 us -> 19.1 us
    ppermute x12, waiting for transfers between devices: 16.2 us -> 15.4 us  [exchange(): return lax.ppermute(array, names, pairs)]
    ppermute x1, starting transfers between devices: 2.41 us -> 1.73 us  [per_device(): gain_other = lax.ppermute(gain_own, 'dp', [(0, 1), (1, 0)])]
  transfers between devices with their start and end apart: 13 -> 13, of which waited for: 8 -> 8; matrix products, arithmetic and copies ran while one was open for 0% -> 0% of each run, Pallas kernels for 16% -> 19%
where the time goes in v4:
time: 48.9 us; the launch traced here: 48.7 us
  starting transfers between devices  19.1 us (39%)
  waiting for transfers between devices  15.4 us (31%)
  Pallas kernels  13.5 us (28%)
  between operations  0.72 us (1%)
    ppermute x12, starting transfers between devices, exchange(): return lax.ppermute(array, names, pairs)  17.4 us
    ppermute x12, waiting for transfers between devices, exchange(): return lax.ppermute(array, names, pairs)  15.4 us
    pallas_call x1, Pallas kernels, fetch(): pl.pallas_call(kernel, out_shape=(pltpu.VMEM(hidden.shape, BF16), pltpu.V...  3.72 us
    pallas_call x4, Pallas kernels, project(): pl.pallas_call(kernel, out_shape=pltpu.VMEM((size, block), BF16), in_spec...  3.22 us
    pallas_call x1, Pallas kernels, attend(): pl.pallas_call(kernel, out_shape=(pltpu.VMEM((pairs, 2 * rows, length), B...  2.82 us
    pallas_call x2, Pallas kernels, mix(): pl.pallas_call(kernel, out_shape=jax.ShapeDtypeStruct((length, columns),...  2.1 us
    ppermute x1, starting transfers between devices, per_device(): gain_other = lax.ppermute(gain_own, 'dp', [(0, 1), (1, 0)])  1.73 us
  transfers between devices with their start and end apart: 13, of which 8 were waited for; matrix products, arithmetic and copies ran while one was open for 0% of the time, Pallas kernels for 19%

profile of v4, /device:TPU:0, one launch (start us, length us, event | category | flops | bytes accessed | tf_op | source)
XLA Modules:
  0.0 48.7 jit_solution(6212558025139675735)
XLA Ops:
  0.6 3.1 %collective-permute-start = (bf16[1,128,256]{2,1,0:T(8,128)(2,1)}, bf16[1,128,256]{2,1,0:T(8,128)(2,1)S(1)}, u32[]{:S(2)}, u32[]{:S(2)}) collective-permute-start(bf16[1,128,256]{2,1,0:T(8,128)(2,1)} %refs_0_.1), channel_id=1, source_target_pairs={{0,1},{1,0},{2,3},{3,2},{4,12},{5,13},{6,14},{7,15},{8,9},{9,8},{1... | collective-permute-start | bytes 196616 | tf_op jit(solution)/shard_map/ppermute | solution.py:374
  3.7 2.5 %collective-permute-start.2 = (bf16[1,128,256]{2,1,0:T(8,128)(2,1)}, bf16[1,128,256]{2,1,0:T(8,128)(2,1)S(1)}, u32[]{:S(2)}, u32[]{:S(2)}) collective-permute-start(bf16[1,128,256]{2,1,0:T(8,128)(2,1)} %refs_0_.1), channel_id=1, source_target_pairs={{0,3},{1,2},{2,1},{3,0},{4,28},{5,29},{6,30},{7,31},{8,11},{9,10},... | collective-permute-start | bytes 196616 | tf_op jit(solution)/shard_map/ppermute | solution.py:374
  6.2 0.1 collective-permute-start.1
  6.3 3.7 %fetch.1 = (bf16[1,128,256]{2,1,0:T(8,128)(2,1)S(1)}, f32[16,1,256]{2,1,0:T(1,128)S(1)}, bf16[16,256,512]{2,1,0:T(8,128)(2,1)S(1)}, bf16[16,256,512]{2,1,0:T(8,128)(2,1)S(1)}) custom-call(bf16[1,128,256]{2,1,0:T(8,128)(2,1)} %refs_0_.1, f32[16,1,256]{2,1,0:T(1,128)} %bitcast.16, bf16[4096,512]{1,0:T(8,128)(2,1)} %bitcast.11, bf16[4096,512]{1,0:T(8,128)(2,1)} %bitcast.12), custom_call_target="tpu_custom_call" | custom-call | bytes 16777216 | tf_op jit(solution)/shard_map/fetch/pallas_call | solution.py:78
  10.1 2.4 %collective-permute-done.1.refs_2_ = bf16[1,128,256]{2,1,0:T(8,128)(2,1)S(1)} collective-permute-done((bf16[1,128,256]{2,1,0:T(8,128)(2,1)}, bf16[1,128,256]{2,1,0:T(8,128)(2,1)S(1)}, u32[]{:S(2)}, u32[]{:S(2)}) %collective-permute-start.1) | collective-permute-done | bytes 65568 | tf_op jit(solution)/shard_map/ppermute | solution.py:374
  12.4 2.5 %collective-permute-start.5 = (bf16[4,128,256]{2,1,0:T(8,128)(2,1)S(1)}, bf16[4,128,256]{2,1,0:T(8,128)(2,1)S(1)}, u32[]{:S(2)}, u32[]{:S(2)}) collective-permute-start(bf16[4,128,256]{2,1,0:T(8,128)(2,1)S(1)} %join.1.refs_0_), channel_id=1, source_target_pairs={{0,24},{1,25},{2,26},{3,27},{4,7},{5,6},{6,5},{7,4},{8,16},{9,17},... | collective-permute-start | bytes 786440 | tf_op jit(solution)/shard_map/ppermute | solution.py:374
  15.0 0.5 %collective-permute-start.4 = (bf16[4,128,256]{2,1,0:T(8,128)(2,1)S(1)}, bf16[4,128,256]{2,1,0:T(8,128)(2,1)S(1)}, u32[]{:S(2)}, u32[]{:S(2)}) collective-permute-start(bf16[4,128,256]{2,1,0:T(8,128)(2,1)S(1)} %join.1.refs_0_), channel_id=1, source_target_pairs={{0,16},{1,17},{2,18},{3,19},{4,6},{5,7},{6,4},{7,5},{8,24},{9,25},... | collective-permute-start | bytes 786440 | tf_op jit(solution)/shard_map/ppermute | solution.py:374
  15.5 0.5 %collective-permute-start.3 = (bf16[4,128,256]{2,1,0:T(8,128)(2,1)S(1)}, bf16[4,128,256]{2,1,0:T(8,128)(2,1)S(1)}, u32[]{:S(2)}, u32[]{:S(2)}) collective-permute-start(bf16[4,128,256]{2,1,0:T(8,128)(2,1)S(1)} %join.1.refs_0_), channel_id=1, source_target_pairs={{0,8},{1,9},{2,10},{3,11},{4,5},{5,4},{6,7},{7,6},{8,0},{9,1},{10,... | collective-permute-start | bytes 786440 | tf_op jit(solution)/shard_map/ppermute | solution.py:374
  16.0 3.9 %collective-permute-done.5.refs_3_ = bf16[4,128,256]{2,1,0:T(8,128)(2,1)S(1)} collective-permute-done((bf16[4,128,256]{2,1,0:T(8,128)(2,1)S(1)}, bf16[4,128,256]{2,1,0:T(8,128)(2,1)S(1)}, u32[]{:S(2)}, u32[]{:S(2)}) %collective-permute-start.5) | collective-permute-done | bytes 262176 | tf_op jit(solution)/shard_map/ppermute | solution.py:374
  19.9 2.7 %collective-permute-done.4.refs_2_ = bf16[4,128,256]{2,1,0:T(8,128)(2,1)S(1)} collective-permute-done((bf16[4,128,256]{2,1,0:T(8,128)(2,1)S(1)}, bf16[4,128,256]{2,1,0:T(8,128)(2,1)S(1)}, u32[]{:S(2)}, u32[]{:S(2)}) %collective-permute-start.4) | collective-permute-done | bytes 262176 | tf_op jit(solution)/shard_map/ppermute | solution.py:374
  22.6 0.1 collective-permute-done.3.refs_1_
  22.7 2.8 %attend.1 = (bf16[4,256,256]{2,1,0:T(8,128)(2,1)S(1)}, bf16[4,256,256]{2,1,0:T(8,128)(2,1)S(1)}, bf16[128,512]{1,0:T(8,128)(2,1)S(1)}, bf16[128,512]{1,0:T(8,128...) custom-call(bf16[4,128,256]{2,1,0:T(8,128)(2,1)S(1)} %join.1.refs_0_, ...), custom_call_target="tpu_custom_call" | custom-call | flops 1342177280 | bytes 16777216 | tf_op jit(solution)/shard_map/attend/pallas_call | solution.py:171
  25.5 0.8 %project.5 = bf16[560,256]{1,0:T(8,128)(2,1)S(1)} custom-call(bf16[128,512]{1,0:T(8,128)(2,1)S(1)} %get-tuple-element.28.kg_ref, bf16[128,512]{1,0:T(8,128)(2,1)S(1)} %get-tuple-element.29.vg_ref, bf16[16,256,512]{2,1,0:T(8,128)(2,1)S(1)} %get-tuple-element.26.refs_5_.wk_ref, bf16[16,256,512]{2,1,0:T(8,128)(2,1)S(1)} %get-tuple-element.27.refs_6_.wv_ref, ...), custom_call_target="tpu_custom_call" | custom-call | flops 1 | bytes 1 | tf_op jit(solution)/shard_map/project/pallas_call | solution.py:238
  26.3 2.0 %collective-permute-start.6 = (bf16[560,256]{1,0:T(8,128)(2,1)S(1)}, bf16[560,256]{1,0:T(8,128)(2,1)S(1)}, u32[]{:S(2)}, u32[]{:S(2)}) collective-permute-start(bf16[560,256]{1,0:T(8,128)(2,1)S(1)} %project.5), channel_id=1, source_target_pairs={{0,24},{1,25},{2,26},{3,27},{4,7},{5,6},{6,5},{7,4},{8,16},{9,17},... | collective-permute-start | bytes 860168 | tf_op jit(solution)/shard_map/ppermute | solution.py:374
  28.3 0.8 %project.6 = bf16[528,256]{1,0:T(8,128)(2,1)S(1)} custom-call(bf16[128,512]{1,0:T(8,128)(2,1)S(1)} %get-tuple-element.28.kg_ref, bf16[128,512]{1,0:T(8,128)(2,1)S(1)} %get-tuple-element.29.vg_ref, bf16[16,256,512]{2,1,0:T(8,128)(2,1)S(1)} %get-tuple-element.26.refs_5_.wk_ref, bf16[16,256,512]{2,1,0:T(8,128)(2,1)S(1)} %get-tuple-element.27.refs_6_.wv_ref, ...), custom_call_target="tpu_custom_call" | custom-call | flops 1 | bytes 1 | tf_op jit(solution)/shard_map/project/pallas_call | solution.py:238
  29.2 1.1 %collective-permute-start.7 = (bf16[528,256]{1,0:T(8,128)(2,1)S(1)}, bf16[528,256]{1,0:T(8,128)(2,1)S(1)}, u32[]{:S(2)}, u32[]{:S(2)}) collective-permute-start(bf16[528,256]{1,0:T(8,128)(2,1)S(1)} %project.6), channel_id=1, source_target_pairs={{0,16},{1,17},{2,18},{3,19},{4,6},{5,7},{6,4},{7,5},{8,24},{9,25},... | collective-permute-start | bytes 811016 | tf_op jit(solution)/shard_map/ppermute | solution.py:374
  30.2 0.8 %project.7 = bf16[528,256]{1,0:T(8,128)(2,1)S(1)} custom-call(bf16[128,512]{1,0:T(8,128)(2,1)S(1)} %get-tuple-element.28.kg_ref, bf16[128,512]{1,0:T(8,128)(2,1)S(1)} %get-tuple-element.29.vg_ref, bf16[16,256,512]{2,1,0:T(8,128)(2,1)S(1)} %get-tuple-element.26.refs_5_.wk_ref, bf16[16,256,512]{2,1,0:T(8,128)(2,1)S(1)} %get-tuple-element.27.refs_6_.wv_ref, ...), custom_call_target="tpu_custom_call" | custom-call | flops 1 | bytes 1 | tf_op jit(solution)/shard_map/project/pallas_call | solution.py:238
  31.0 0.6 %collective-permute-start.8 = (bf16[528,256]{1,0:T(8,128)(2,1)S(1)}, bf16[528,256]{1,0:T(8,128)(2,1)S(1)}, u32[]{:S(2)}, u32[]{:S(2)}) collective-permute-start(bf16[528,256]{1,0:T(8,128)(2,1)S(1)} %project.7), channel_id=1, source_target_pairs={{0,8},{1,9},{2,10},{3,11},{4,5},{5,4},{6,7},{7,6},{8,0},{9,1},{10,... | collective-permute-start | bytes 811016 | tf_op jit(solution)/shard_map/ppermute | solution.py:374
  31.6 0.8 %project.4.refs_0_ = bf16[528,256]{1,0:T(8,128)(2,1)S(1)} custom-call(bf16[128,512]{1,0:T(8,128)(2,1)S(1)} %get-tuple-element.28.kg_ref, bf16[128,512]{1,0:T(8,128)(2,1)S(1)} %get-tuple-element.29.vg_ref, bf16[16,256,512]{2,1,0:T(8,128)(2,1)S(1)} %get-tuple-element.26.refs_5_.wk_ref, bf16[16,256,512]{2,1,0:T(8,128)(2,1)S(1)} %get-tuple-element.27.refs_6_.wv_ref, ...), custom_call_target="tpu_custom_call" | custom-call | flops 1 | bytes 1 | tf_op jit(solution)/shard_map/project/pallas_call | solution.py:238
  32.5 1.1 %mix.2 = bf16[256,512]{1,0:T(8,128)(2,1)} custom-call(bf16[4,256,256]{2,1,0:T(8,128)(2,1)S(1)} %get-tuple-element.31.shares_ref, bf16[128,512]{1,0:T(8,128)(2,1)S(1)} %get-tuple-element.32.weights_ref), custom_call_target="tpu_custom_call" | custom-call | flops 1 | bytes 1 | tf_op jit(solution)/shard_map/mix/pallas_call | solution.py:210
  33.5 1.1 %mix.3 = bf16[256,512]{1,0:T(8,128)(2,1)} custom-call(bf16[4,256,256]{2,1,0:T(8,128)(2,1)S(1)} %get-tuple-element.33.shares_ref, bf16[128,512]{1,0:T(8,128)(2,1)S(1)} %get-tuple-element.34.weights_ref), custom_call_target="tpu_custom_call" | custom-call | flops 1 | bytes 1 | tf_op jit(solution)/shard_map/mix/pallas_call | solution.py:210
  34.6 2.3 %collective-permute-done.7.refs_2_ = bf16[528,256]{1,0:T(8,128)(2,1)S(1)} collective-permute-done((bf16[528,256]{1,0:T(8,128)(2,1)S(1)}, bf16[528,256]{1,0:T(8,128)(2,1)S(1)}, u32[]{:S(2)}, u32[]{:S(2)}) %collective-permute-start.7) | collective-permute-done | bytes 270368 | tf_op jit(solution)/shard_map/ppermute | solution.py:374
  36.8 0.7 %collective-permute-done.8.refs_3_ = bf16[528,256]{1,0:T(8,128)(2,1)S(1)} collective-permute-done((bf16[528,256]{1,0:T(8,128)(2,1)S(1)}, bf16[528,256]{1,0:T(8,128)(2,1)S(1)}, u32[]{:S(2)}, u32[]{:S(2)}) %collective-permute-start.8) | collective-permute-done | bytes 270368 | tf_op jit(solution)/shard_map/ppermute | solution.py:374
  37.6 0.1 sum_chunks.1
  37.7 1.5 %collective-permute-start.9 = (bf16[144,256]{1,0:T(8,128)(2,1)S(1)}, bf16[144,256]{1,0:T(8,128)(2,1)S(1)}, u32[]{:S(2)}, u32[]{:S(2)}) collective-permute-start(bf16[144,256]{1,0:T(8,128)(2,1)S(1)} %get-tuple-element.41), channel_id=1, source_target_pairs={{0,3},{1,2},{2,1},{3,0},{4,28},{5,29},{6,30},{7,31},{8,11},{9,10},... | collective-permute-start | bytes 221192 | tf_op jit(solution)/shard_map/ppermute | solution.py:374
  39.2 2.9 %collective-permute-start.11 = (bf16[144,256]{1,0:T(8,128)(2,1)S(1)}, bf16[144,256]{1,0:T(8,128)(2,1)S(1)}, u32[]{:S(2)}, u32[]{:S(2)}) collective-permute-start(bf16[144,256]{1,0:T(8,128)(2,1)S(1)} %get-tuple-element.43), channel_id=1, source_target_pairs={{0,1},{1,0},{2,3},{3,2},{4,12},{5,13},{6,14},{7,15},{8,9},{9,8},{1... | collective-permute-start | bytes 221192 | tf_op jit(solution)/shard_map/ppermute | solution.py:374
  42.2 1.8 %collective-permute-done.9.refs_0_ = bf16[144,256]{1,0:T(8,128)(2,1)S(1)} collective-permute-done((bf16[144,256]{1,0:T(8,128)(2,1)S(1)}, bf16[144,256]{1,0:T(8,128)(2,1)S(1)}, u32[]{:S(2)}, u32[]{:S(2)}) %collective-permute-start.9) | collective-permute-done | bytes 73760 | tf_op jit(solution)/shard_map/ppermute | solution.py:374
  44.0 1.5 %collective-permute-done.10.refs_1_ = bf16[144,256]{1,0:T(8,128)(2,1)S(1)} collective-permute-done((bf16[144,256]{1,0:T(8,128)(2,1)S(1)}, bf16[144,256]{1,0:T(8,128)(2,1)S(1)}, u32[]{:S(2)}, u32[]{:S(2)}) %collective-permute-start.10) | collective-permute-done | bytes 73760 | tf_op jit(solution)/shard_map/ppermute | solution.py:374
  45.5 0.1 gain_part.1.mine_ref
  45.6 1.7 %collective-permute-start.12 = (f32[1,256]{1,0:T(1,128)S(1)}, f32[1,256]{1,0:T(1,128)S(1)}, u32[]{:S(2)}, u32[]{:S(2)}) collective-permute-start(f32[1,256]{1,0:T(1,128)S(1)} %gain_part.1.mine_ref), channel_id=1, source_target_pairs={{0,4},{4,0},{1,5},{5,1},{2,6},{6,2},{3,7},{7,3},{8,12},{12,8},{9,1... | collective-permute-start | bytes 3080 | tf_op jit(solution)/shard_map/ppermute | solution.py:450
  47.3 0.8 %finish.1 = f32[128,256]{1,0:T(8,128)} custom-call(bf16[1,128,256]{2,1,0:T(8,128)(2,1)S(1)} %get-tuple-element.24.refs_0_.hidden_ref, f32[16,1,256]{2,1,0:T(1,128)S(1)} %get-tuple-element.25.refs_4_.gain_ref, f32[128,128]{1,0:T(8,128)S(1)} %get-tuple-element.37.inverse_ref, f32[128,256]{1,0:T(8,128)S(1)} %get-tuple-element.39.own_ref, ...), custom_call_target="tpu_custom_call" | custom-call | bytes 65536 | tf_op jit(solution)/shard_map/finish/pallas_call | solution.py:338
  48.2 0.6 %add_gain.1 = f32[1,256]{1,0:T(1,128)} custom-call(f32[1,256]{1,0:T(1,128)S(1)} %gain_part.1.mine_ref, f32[1,256]{1,0:T(1,128)S(1)} %collective-permute-done.12.theirs_ref), custom_call_target="tpu_custom_call" | custom-call | tf_op jit(solution)/shard_map/add_gain/pallas_call | solution.py:353
  (11 shorter events, 0.0 us)
Async XLA Ops:
  0.6 9.4 %collective-permute-start = (bf16[1,128,256]{2,1,0:T(8,128)(2,1)}, bf16[1,128,256]{2,1,0:T(8,128)(2,1)S(1)}, u32[]{:S(2)}, u32[]{:S(2)}) collective-permute-start(bf16[1,128,256]{2,1,0:T(8,128)(2,1)} %refs_0_.1), channel_id=1, source_target_pairs={{0,1},{1,0},{2,3},{3,2},{4,12},{5,13},{6,14},{7,15},{8,9},{9,8},{1... | collective-permute-start | bytes 196616 | tf_op jit(solution)/shard_map/ppermute | solution.py:374
  3.7 6.3 %collective-permute-start.2 = (bf16[1,128,256]{2,1,0:T(8,128)(2,1)}, bf16[1,128,256]{2,1,0:T(8,128)(2,1)S(1)}, u32[]{:S(2)}, u32[]{:S(2)}) collective-permute-start(bf16[1,128,256]{2,1,0:T(8,128)(2,1)} %refs_0_.1), channel_id=1, source_target_pairs={{0,3},{1,2},{2,1},{3,0},{4,28},{5,29},{6,30},{7,31},{8,11},{9,10},... | collective-permute-start | bytes 196616 | tf_op jit(solution)/shard_map/ppermute | solution.py:374
  6.2 6.2 %collective-permute-start.1 = (bf16[1,128,256]{2,1,0:T(8,128)(2,1)}, bf16[1,128,256]{2,1,0:T(8,128)(2,1)S(1)}, u32[]{:S(2)}, u32[]{:S(2)}) collective-permute-start(bf16[1,128,256]{2,1,0:T(8,128)(2,1)} %refs_0_.1), channel_id=1, source_target_pairs={{0,2},{1,3},{2,0},{3,1},{4,20},{5,21},{6,22},{7,23},{8,10},{9,11},... | collective-permute-start | bytes 196616 | tf_op jit(solution)/shard_map/ppermute | solution.py:374
  6.3 16.4 %copy-start = (bf16[1,1,256,512]{3,2,1,0:T(8,128)(2,1)S(1)}, bf16[1,1,256,512]{3,2,1,0:T(8,128)(2,1)}, u32[]{:S(2)}) copy-start(bf16[1,1,256,512]{3,2,1,0:T(8,128)(2,1)} %param.10) | copy-start | bytes 786436
  6.3 16.4 %copy-start.1 = (bf16[1,1,256,512]{3,2,1,0:T(8,128)(2,1)S(1)}, bf16[1,1,256,512]{3,2,1,0:T(8,128)(2,1)}, u32[]{:S(2)}) copy-start(bf16[1,1,256,512]{3,2,1,0:T(8,128)(2,1)} %param.11) | copy-start | bytes 786436
  12.4 7.4 %collective-permute-start.5 = (bf16[4,128,256]{2,1,0:T(8,128)(2,1)S(1)}, bf16[4,128,256]{2,1,0:T(8,128)(2,1)S(1)}, u32[]{:S(2)}, u32[]{:S(2)}) collective-permute-start(bf16[4,128,256]{2,1,0:T(8,128)(2,1)S(1)} %join.1.refs_0_), channel_id=1, source_target_pairs={{0,24},{1,25},{2,26},{3,27},{4,7},{5,6},{6,5},{7,4},{8,16},{9,17},... | collective-permute-start | bytes 786440 | tf_op jit(solution)/shard_map/ppermute | solution.py:374
  15.0 7.6 %collective-permute-start.4 = (bf16[4,128,256]{2,1,0:T(8,128)(2,1)S(1)}, bf16[4,128,256]{2,1,0:T(8,128)(2,1)S(1)}, u32[]{:S(2)}, u32[]{:S(2)}) collective-permute-start(bf16[4,128,256]{2,1,0:T(8,128)(2,1)S(1)} %join.1.refs_0_), channel_id=1, source_target_pairs={{0,16},{1,17},{2,18},{3,19},{4,6},{5,7},{6,4},{7,5},{8,24},{9,25},... | collective-permute-start | bytes 786440 | tf_op jit(solution)/shard_map/ppermute | solution.py:374
  15.5 7.2 %collective-permute-start.3 = (bf16[4,128,256]{2,1,0:T(8,128)(2,1)S(1)}, bf16[4,128,256]{2,1,0:T(8,128)(2,1)S(1)}, u32[]{:S(2)}, u32[]{:S(2)}) collective-permute-start(bf16[4,128,256]{2,1,0:T(8,128)(2,1)S(1)} %join.1.refs_0_), channel_id=1, source_target_pairs={{0,8},{1,9},{2,10},{3,11},{4,5},{5,4},{6,7},{7,6},{8,0},{9,1},{10,... | collective-permute-start | bytes 786440 | tf_op jit(solution)/shard_map/ppermute | solution.py:374
  26.3 11.2 %collective-permute-start.6 = (bf16[560,256]{1,0:T(8,128)(2,1)S(1)}, bf16[560,256]{1,0:T(8,128)(2,1)S(1)}, u32[]{:S(2)}, u32[]{:S(2)}) collective-permute-start(bf16[560,256]{1,0:T(8,128)(2,1)S(1)} %project.5), channel_id=1, source_target_pairs={{0,24},{1,25},{2,26},{3,27},{4,7},{5,6},{6,5},{7,4},{8,16},{9,17},... | collective-permute-start | bytes 860168 | tf_op jit(solution)/shard_map/ppermute | solution.py:374
  29.2 7.7 %collective-permute-start.7 = (bf16[528,256]{1,0:T(8,128)(2,1)S(1)}, bf16[528,256]{1,0:T(8,128)(2,1)S(1)}, u32[]{:S(2)}, u32[]{:S(2)}) collective-permute-start(bf16[528,256]{1,0:T(8,128)(2,1)S(1)} %project.6), channel_id=1, source_target_pairs={{0,16},{1,17},{2,18},{3,19},{4,6},{5,7},{6,4},{7,5},{8,24},{9,25},... | collective-permute-start | bytes 811016 | tf_op jit(solution)/shard_map/ppermute | solution.py:374
  31.0 6.5 %collective-permute-start.8 = (bf16[528,256]{1,0:T(8,128)(2,1)S(1)}, bf16[528,256]{1,0:T(8,128)(2,1)S(1)}, u32[]{:S(2)}, u32[]{:S(2)}) collective-permute-start(bf16[528,256]{1,0:T(8,128)(2,1)S(1)} %project.7), channel_id=1, source_target_pairs={{0,8},{1,9},{2,10},{3,11},{4,5},{5,4},{6,7},{7,6},{8,0},{9,1},{10,... | collective-permute-start | bytes 811016 | tf_op jit(solution)/shard_map/ppermute | solution.py:374
  37.7 6.3 %collective-permute-start.9 = (bf16[144,256]{1,0:T(8,128)(2,1)S(1)}, bf16[144,256]{1,0:T(8,128)(2,1)S(1)}, u32[]{:S(2)}, u32[]{:S(2)}) collective-permute-start(bf16[144,256]{1,0:T(8,128)(2,1)S(1)} %get-tuple-element.41), channel_id=1, source_target_pairs={{0,3},{1,2},{2,1},{3,0},{4,28},{5,29},{6,30},{7,31},{8,11},{9,10},... | collective-permute-start | bytes 221192 | tf_op jit(solution)/shard_map/ppermute | solution.py:374
  39.2 6.3 %collective-permute-start.10 = (bf16[144,256]{1,0:T(8,128)(2,1)S(1)}, bf16[144,256]{1,0:T(8,128)(2,1)S(1)}, u32[]{:S(2)}, u32[]{:S(2)}) collective-permute-start(bf16[144,256]{1,0:T(8,128)(2,1)S(1)} %get-tuple-element.42), channel_id=1, source_target_pairs={{0,2},{1,3},{2,0},{3,1},{4,20},{5,21},{6,22},{7,23},{8,10},{9,11},... | collective-permute-start | bytes 221192 | tf_op jit(solution)/shard_map/ppermute | solution.py:374
  39.2 6.3 %collective-permute-start.11 = (bf16[144,256]{1,0:T(8,128)(2,1)S(1)}, bf16[144,256]{1,0:T(8,128)(2,1)S(1)}, u32[]{:S(2)}, u32[]{:S(2)}) collective-permute-start(bf16[144,256]{1,0:T(8,128)(2,1)S(1)} %get-tuple-element.43), channel_id=1, source_target_pairs={{0,1},{1,0},{2,3},{3,2},{4,12},{5,13},{6,14},{7,15},{8,9},{9,8},{1... | collective-permute-start | bytes 221192 | tf_op jit(solution)/shard_map/ppermute | solution.py:374
  45.6 2.6 %collective-permute-start.12 = (f32[1,256]{1,0:T(1,128)S(1)}, f32[1,256]{1,0:T(1,128)S(1)}, u32[]{:S(2)}, u32[]{:S(2)}) collective-permute-start(f32[1,256]{1,0:T(1,128)S(1)} %gain_part.1.mine_ref), channel_id=1, source_target_pairs={{0,4},{4,0},{1,5},{5,1},{2,6},{6,2},{3,7},{7,3},{8,12},{12,8},{9,1... | collective-permute-start | bytes 3080 | tf_op jit(solution)/shard_map/ppermute | solution.py:450

commit v5 on v4

--- a/solution.py
+++ b/solution.py
@@ -12,7 +12,7 @@
 BLOCK = 256
 EXTRA = 16
 EXTRA_WIDTH = 256
-PAD = 32
+PAD = 16
 F32 = jnp.float32
 BF16 = jnp.bfloat16
 VMEM = pl.BlockSpec(memory_space=pltpu.VMEM)
@@ -53,22 +53,23 @@
     return lax.bitwise_xor(section, j + turn) * slots + lax.bitwise_xor(mp, i - turn)
 
 
-def fetch(hidden, gain, wk, wv, sections, slots, direct):
-    width, columns = wk.shape
+def fetch(arrays, weights, sections, slots, direct):
+    width, columns = weights[0].shape
     block = width // (sections * slots)
+    few, many = len(arrays), len(weights)
 
     def kernel(*refs):
-        ins, outs, few, many = refs[:4], refs[4:8], refs[8], refs[9]
-        copies = [pltpu.make_async_copy(ins[n], outs[n], few.at[n]) for n in range(2)]
+        ins, outs, sems = refs[:few + many], refs[few + many:-1], refs[-1]
+        copies = [pltpu.make_async_copy(ins[n], outs[n], sems.at[many, n]) for n in range(few)]
         for j in range(sections):
             for i in range(slots):
                 row = pl.multiple_of(block_at(direct, j, i, slots) * block, block)
                 n = j * slots + i
                 copies += [
                     pltpu.make_async_copy(
-                        ins[2 + w].at[pl.ds(row, block), :], outs[2 + w].at[n], many.at[w, n]
+                        ins[few + w].at[pl.ds(row, block), :], outs[few + w].at[n], sems.at[w, n]
                     )
-                    for w in range(2)
+                    for w in range(many)
                 ]
         for copy in copies:
             copy.start()
@@ -77,21 +78,15 @@
 
     return pl.pallas_call(
         kernel,
-        out_shape=(
-            pltpu.VMEM(hidden.shape, BF16),
-            pltpu.VMEM(gain.shape, F32),
-            pltpu.VMEM((sections * slots, block, columns), BF16),
-            pltpu.VMEM((sections * slots, block, columns), BF16),
-        ),
-        in_specs=[HBM] * 4,
-        out_specs=(VMEM,) * 4,
-        scratch_shapes=[
-            pltpu.SemaphoreType.DMA((2,)), pltpu.SemaphoreType.DMA((2, sections * slots))
-        ],
+        out_shape=tuple(pltpu.VMEM(array.shape, array.dtype) for array in arrays)
+        + (pltpu.VMEM((sections * slots, block, columns), BF16),) * many,
+        in_specs=[HBM] * (few + many),
+        out_specs=(VMEM,) * (few + many),
+        scratch_shapes=[pltpu.SemaphoreType.DMA((many + 1, sections * slots))],
         compiler_params=pltpu.CompilerParams(vmem_limit_bytes=1 << 20),
-        cost_estimate=cost(0, 8 * width * columns),
+        cost_estimate=cost(0, 4 * many * width * columns),
         name="fetch",
-    )(*map(in_hbm, (hidden, gain, wk, wv)))
+    )(*map(in_hbm, (*arrays, *weights)))
 
 
 def attend(x, gain, wk, wv, q, g, direct):
@@ -246,9 +241,9 @@
     )(in_vmem(kg), in_vmem(vg), in_vmem(wk), in_vmem(wv), *tail)
 
 
-def join(parts):
+def join(parts, order):
     def kernel(*refs):
-        for n, ref in enumerate(refs[:-1]):
+        for n, ref in zip(order, refs[:-1]):
             refs[-1][n] = ref[0]
 
     return pl.pallas_call(
@@ -405,8 +400,11 @@
 
     gain = enc_gain.reshape(width // BLOCK, 1, BLOCK)
     parts = width // (slots * BLOCK)
-    hidden, gain, wk, wv = fetch(own[None], gain, wk, wv, parts, slots, direct)
-    x = join([hidden] + swap(1, [own[None]] * groups)[1:])
+    hidden, gain, wk = fetch((own[None], gain), (wk,), parts, slots, direct)
+    (wv,) = fetch((), (wv,), parts, slots, direct)
+    column = [hidden] + swap(1, [own[None]] * groups)[1:]
+    order = sorted(range(groups), key=lambda j: (j > 0, j != 3, j))
+    x = join([column[j] for j in order], order)
     if direct:
         x = [(part,) for part in swap(2, [x] * sections)]
     else:

time: 48.9 us -> 47 us (0.961)
  waiting for transfers between devices: 15.4 us -> 13.2 us
  Pallas kernels: 13.5 us -> 14.7 us
  starting transfers between devices: 19.1 us -> 18.3 us
    ppermute x12, waiting for transfers between devices: 15.4 us -> 13.2 us  [exchange(): return lax.ppermute(array, names, pairs)]
    pallas_call x1 -> x2, Pallas kernels: 3.72 us -> 4.94 us  [fetch(): pl.pallas_call(kernel, out_shape=tuple((pltpu.VMEM(array.shape, array.dty...]
    ppermute x1, starting transfers between devices: 1.73 us -> 0.82 us  [per_device(): gain_other = lax.ppermute(gain_own, 'dp', [(0, 1), (1, 0)])]
  transfers between devices with their start and end apart: 13 -> 13, of which waited for: 8 -> 8; matrix products, arithmetic and copies ran while one was open for 0% -> 0% of each run, Pallas kernels for 19% -> 22%
where the time goes in v5:
time: 47 us; the launch traced here: 46.9 us
  starting transfers between devices  18.3 us (39%)
  Pallas kernels  14.7 us (31%)
  waiting for transfers between devices  13.2 us (28%)
  between operations  0.72 us (2%)
    ppermute x12, starting transfers between devices, exchange(): return lax.ppermute(array, names, pairs)  17.4 us
    ppermute x12, waiting for transfers between devices, exchange(): return lax.ppermute(array, names, pairs)  13.2 us
    pallas_call x2, Pallas kernels, fetch(): pl.pallas_call(kernel, out_shape=tuple((pltpu.VMEM(array.shape, array.dty...  4.94 us
    pallas_call x4, Pallas kernels, project(): pl.pallas_call(kernel, out_shape=pltpu.VMEM((size, block), BF16), in_spec...  3.21 us
    pallas_call x1, Pallas kernels, attend(): pl.pallas_call(kernel, out_shape=(pltpu.VMEM((pairs, 2 * rows, length), B...  2.82 us
    pallas_call x2, Pallas kernels, mix(): pl.pallas_call(kernel, out_shape=jax.ShapeDtypeStruct((length, columns),...  2.1 us
  transfers between devices with their start and end apart: 13, of which 8 were waited for; matrix products, arithmetic and copies ran while one was open for 0% of the time, Pallas kernels for 22%

profile of v5, /device:TPU:0, one launch (start us, length us, event | category | flops | bytes accessed | tf_op | source)
XLA Modules:
  0.0 46.9 jit_solution(10596908353077811559)
XLA Ops:
  0.6 5.1 %collective-permute-start = (bf16[1,128,256]{2,1,0:T(8,128)(2,1)}, bf16[1,128,256]{2,1,0:T(8,128)(2,1)S(1)}, u32[]{:S(2)}, u32[]{:S(2)}) collective-permute-start(bf16[1,128,256]{2,1,0:T(8,128)(2,1)} %refs_0_.1), channel_id=1, source_target_pairs={{0,3},{1,2},{2,1},{3,0},{4,28},{5,29},{6,30},{7,31},{8,11},{9,10},... | collective-permute-start | bytes 196616 | tf_op jit(solution)/shard_map/ppermute | solution.py:369
  5.7 0.6 %collective-permute-start.1 = (bf16[1,128,256]{2,1,0:T(8,128)(2,1)}, bf16[1,128,256]{2,1,0:T(8,128)(2,1)S(1)}, u32[]{:S(2)}, u32[]{:S(2)}) collective-permute-start(bf16[1,128,256]{2,1,0:T(8,128)(2,1)} %refs_0_.1), channel_id=1, source_target_pairs={{0,1},{1,0},{2,3},{3,2},{4,12},{5,13},{6,14},{7,15},{8,9},{9,8},{1... | collective-permute-start | bytes 196616 | tf_op jit(solution)/shard_map/ppermute | solution.py:369
  6.4 2.5 %fetch.2 = (bf16[1,128,256]{2,1,0:T(8,128)(2,1)S(1)}, f32[16,1,256]{2,1,0:T(1,128)S(1)}, bf16[16,256,512]{2,1,0:T(8,128)(2,1)S(1)}) custom-call(bf16[1,128,256]{2,1,0:T(8,128)(2,1)} %refs_0_.1, f32[16,1,256]{2,1,0:T(1,128)} %bitcast.16, bf16[4096,512]{1,0:T(8,128)(2,1)} %bitcast.11), custom_call_target="tpu_custom_call" | custom-call | bytes 8388608 | tf_op jit(solution)/shard_map/fetch/pallas_call | solution.py:79
  8.9 2.2 %collective-permute-done.2.refs_3_ = bf16[1,128,256]{2,1,0:T(8,128)(2,1)S(1)} collective-permute-done((bf16[1,128,256]{2,1,0:T(8,128)(2,1)}, bf16[1,128,256]{2,1,0:T(8,128)(2,1)S(1)}, u32[]{:S(2)}, u32[]{:S(2)}) %collective-permute-start.2) | collective-permute-done | bytes 65568 | tf_op jit(solution)/shard_map/ppermute | solution.py:369
  11.1 2.9 %collective-permute-start.5 = (bf16[4,128,256]{2,1,0:T(8,128)(2,1)S(1)}, bf16[4,128,256]{2,1,0:T(8,128)(2,1)S(1)}, u32[]{:S(2)}, u32[]{:S(2)}) collective-permute-start(bf16[4,128,256]{2,1,0:T(8,128)(2,1)S(1)} %join.1.refs_0_), channel_id=1, source_target_pairs={{0,24},{1,25},{2,26},{3,27},{4,7},{5,6},{6,5},{7,4},{8,16},{9,17},... | collective-permute-start | bytes 786440 | tf_op jit(solution)/shard_map/ppermute | solution.py:369
  14.0 0.5 %collective-permute-start.4 = (bf16[4,128,256]{2,1,0:T(8,128)(2,1)S(1)}, bf16[4,128,256]{2,1,0:T(8,128)(2,1)S(1)}, u32[]{:S(2)}, u32[]{:S(2)}) collective-permute-start(bf16[4,128,256]{2,1,0:T(8,128)(2,1)S(1)} %join.1.refs_0_), channel_id=1, source_target_pairs={{0,16},{1,17},{2,18},{3,19},{4,6},{5,7},{6,4},{7,5},{8,24},{9,25},... | collective-permute-start | bytes 786440 | tf_op jit(solution)/shard_map/ppermute | solution.py:369
  14.5 0.2 collective-permute-start.3
  14.7 2.5 %fetch.3.refs_6_.wv_ref = bf16[16,256,512]{2,1,0:T(8,128)(2,1)S(1)} custom-call(bf16[4096,512]{1,0:T(8,128)(2,1)} %bitcast.12), custom_call_target="tpu_custom_call" | custom-call | bytes 8388608 | tf_op jit(solution)/shard_map/fetch/pallas_call | solution.py:79
  17.2 1.4 %collective-permute-done.5.refs_3_ = bf16[4,128,256]{2,1,0:T(8,128)(2,1)S(1)} collective-permute-done((bf16[4,128,256]{2,1,0:T(8,128)(2,1)S(1)}, bf16[4,128,256]{2,1,0:T(8,128)(2,1)S(1)}, u32[]{:S(2)}, u32[]{:S(2)}) %collective-permute-start.5) | collective-permute-done | bytes 262176 | tf_op jit(solution)/shard_map/ppermute | solution.py:369
  18.6 2.7 %collective-permute-done.4.refs_2_ = bf16[4,128,256]{2,1,0:T(8,128)(2,1)S(1)} collective-permute-done((bf16[4,128,256]{2,1,0:T(8,128)(2,1)S(1)}, bf16[4,128,256]{2,1,0:T(8,128)(2,1)S(1)}, u32[]{:S(2)}, u32[]{:S(2)}) %collective-permute-start.4) | collective-permute-done | bytes 262176 | tf_op jit(solution)/shard_map/ppermute | solution.py:369
  21.4 2.8 %attend.1 = (bf16[4,256,256]{2,1,0:T(8,128)(2,1)S(1)}, bf16[4,256,256]{2,1,0:T(8,128)(2,1)S(1)}, bf16[128,512]{1,0:T(8,128)(2,1)S(1)}, bf16[128,512]{1,0:T(8,128...) custom-call(bf16[4,128,256]{2,1,0:T(8,128)(2,1)S(1)} %join.1.refs_0_, ...), custom_call_target="tpu_custom_call" | custom-call | flops 1342177280 | bytes 16777216 | tf_op jit(solution)/shard_map/attend/pallas_call | solution.py:166
  24.2 0.8 %project.5 = bf16[544,256]{1,0:T(8,128)(2,1)S(1)} custom-call(bf16[128,512]{1,0:T(8,128)(2,1)S(1)} %get-tuple-element.26.kg_ref, bf16[128,512]{1,0:T(8,128)(2,1)S(1)} %get-tuple-element.27.vg_ref, bf16[16,256,512]{2,1,0:T(8,128)(2,1)S(1)} %get-tuple-element.25.refs_5_.wk_ref, bf16[16,256,512]{2,1,0:T(8,128)(2,1)S(1)} %fetch.3.refs_6_.wv_ref, ...), custom_call_target="tpu_custom_call" | custom-call | flops 1 | bytes 1 | tf_op jit(solution)/shard_map/project/pallas_call | solution.py:233
  25.0 2.0 %collective-permute-start.6 = (bf16[544,256]{1,0:T(8,128)(2,1)S(1)}, bf16[544,256]{1,0:T(8,128)(2,1)S(1)}, u32[]{:S(2)}, u32[]{:S(2)}) collective-permute-start(bf16[544,256]{1,0:T(8,128)(2,1)S(1)} %project.5), channel_id=1, source_target_pairs={{0,24},{1,25},{2,26},{3,27},{4,7},{5,6},{6,5},{7,4},{8,16},{9,17},... | collective-permute-start | bytes 835592 | tf_op jit(solution)/shard_map/ppermute | solution.py:369
  27.0 0.8 %project.6 = bf16[528,256]{1,0:T(8,128)(2,1)S(1)} custom-call(bf16[128,512]{1,0:T(8,128)(2,1)S(1)} %get-tuple-element.26.kg_ref, bf16[128,512]{1,0:T(8,128)(2,1)S(1)} %get-tuple-element.27.vg_ref, bf16[16,256,512]{2,1,0:T(8,128)(2,1)S(1)} %get-tuple-element.25.refs_5_.wk_ref, bf16[16,256,512]{2,1,0:T(8,128)(2,1)S(1)} %fetch.3.refs_6_.wv_ref, ...), custom_call_target="tpu_custom_call" | custom-call | flops 1 | bytes 1 | tf_op jit(solution)/shard_map/project/pallas_call | solution.py:233
  27.9 1.4 %collective-permute-start.7 = (bf16[528,256]{1,0:T(8,128)(2,1)S(1)}, bf16[528,256]{1,0:T(8,128)(2,1)S(1)}, u32[]{:S(2)}, u32[]{:S(2)}) collective-permute-start(bf16[528,256]{1,0:T(8,128)(2,1)S(1)} %project.6), channel_id=1, source_target_pairs={{0,16},{1,17},{2,18},{3,19},{4,6},{5,7},{6,4},{7,5},{8,24},{9,25},... | collective-permute-start | bytes 811016 | tf_op jit(solution)/shard_map/ppermute | solution.py:369
  29.3 0.8 %project.7 = bf16[528,256]{1,0:T(8,128)(2,1)S(1)} custom-call(bf16[128,512]{1,0:T(8,128)(2,1)S(1)} %get-tuple-element.26.kg_ref, bf16[128,512]{1,0:T(8,128)(2,1)S(1)} %get-tuple-element.27.vg_ref, bf16[16,256,512]{2,1,0:T(8,128)(2,1)S(1)} %get-tuple-element.25.refs_5_.wk_ref, bf16[16,256,512]{2,1,0:T(8,128)(2,1)S(1)} %fetch.3.refs_6_.wv_ref, ...), custom_call_target="tpu_custom_call" | custom-call | flops 1 | bytes 1 | tf_op jit(solution)/shard_map/project/pallas_call | solution.py:233
  30.1 0.2 collective-permute-start.8
  30.3 0.8 %project.4.refs_0_ = bf16[528,256]{1,0:T(8,128)(2,1)S(1)} custom-call(bf16[128,512]{1,0:T(8,128)(2,1)S(1)} %get-tuple-element.26.kg_ref, bf16[128,512]{1,0:T(8,128)(2,1)S(1)} %get-tuple-element.27.vg_ref, bf16[16,256,512]{2,1,0:T(8,128)(2,1)S(1)} %get-tuple-element.25.refs_5_.wk_ref, bf16[16,256,512]{2,1,0:T(8,128)(2,1)S(1)} %fetch.3.refs_6_.wv_ref, ...), custom_call_target="tpu_custom_call" | custom-call | flops 1 | bytes 1 | tf_op jit(solution)/shard_map/project/pallas_call | solution.py:233
  31.1 1.1 %mix.2 = bf16[256,512]{1,0:T(8,128)(2,1)} custom-call(bf16[4,256,256]{2,1,0:T(8,128)(2,1)S(1)} %get-tuple-element.29.shares_ref, bf16[128,512]{1,0:T(8,128)(2,1)S(1)} %get-tuple-element.30.weights_ref), custom_call_target="tpu_custom_call" | custom-call | flops 1 | bytes 1 | tf_op jit(solution)/shard_map/mix/pallas_call | solution.py:205
  32.2 1.1 %mix.3 = bf16[256,512]{1,0:T(8,128)(2,1)} custom-call(bf16[4,256,256]{2,1,0:T(8,128)(2,1)S(1)} %get-tuple-element.31.shares_ref, bf16[128,512]{1,0:T(8,128)(2,1)S(1)} %get-tuple-element.32.weights_ref), custom_call_target="tpu_custom_call" | custom-call | flops 1 | bytes 1 | tf_op jit(solution)/shard_map/mix/pallas_call | solution.py:205
  33.2 2.2 %collective-permute-done.7.refs_2_ = bf16[528,256]{1,0:T(8,128)(2,1)S(1)} collective-permute-done((bf16[528,256]{1,0:T(8,128)(2,1)S(1)}, bf16[528,256]{1,0:T(8,128)(2,1)S(1)}, u32[]{:S(2)}, u32[]{:S(2)}) %collective-permute-start.7) | collective-permute-done | bytes 270368 | tf_op jit(solution)/shard_map/ppermute | solution.py:369
  35.5 1.2 %collective-permute-done.8.refs_3_ = bf16[528,256]{1,0:T(8,128)(2,1)S(1)} collective-permute-done((bf16[528,256]{1,0:T(8,128)(2,1)S(1)}, bf16[528,256]{1,0:T(8,128)(2,1)S(1)}, u32[]{:S(2)}, u32[]{:S(2)}) %collective-permute-start.8) | collective-permute-done | bytes 270368 | tf_op jit(solution)/shard_map/ppermute | solution.py:369
  36.6 0.1 sum_chunks.1
  36.8 1.5 %collective-permute-start.9 = (bf16[144,256]{1,0:T(8,128)(2,1)S(1)}, bf16[144,256]{1,0:T(8,128)(2,1)S(1)}, u32[]{:S(2)}, u32[]{:S(2)}) collective-permute-start(bf16[144,256]{1,0:T(8,128)(2,1)S(1)} %get-tuple-element.39), channel_id=1, source_target_pairs={{0,3},{1,2},{2,1},{3,0},{4,28},{5,29},{6,30},{7,31},{8,11},{9,10},... | collective-permute-start | bytes 221192 | tf_op jit(solution)/shard_map/ppermute | solution.py:369
  38.3 1.0 %collective-permute-start.10 = (bf16[144,256]{1,0:T(8,128)(2,1)S(1)}, bf16[144,256]{1,0:T(8,128)(2,1)S(1)}, u32[]{:S(2)}, u32[]{:S(2)}) collective-permute-start(bf16[144,256]{1,0:T(8,128)(2,1)S(1)} %get-tuple-element.40), channel_id=1, source_target_pairs={{0,2},{1,3},{2,0},{3,1},{4,20},{5,21},{6,22},{7,23},{8,10},{9,11},... | collective-permute-start | bytes 221192 | tf_op jit(solution)/shard_map/ppermute | solution.py:369
  39.3 1.9 %collective-permute-start.11 = (bf16[144,256]{1,0:T(8,128)(2,1)S(1)}, bf16[144,256]{1,0:T(8,128)(2,1)S(1)}, u32[]{:S(2)}, u32[]{:S(2)}) collective-permute-start(bf16[144,256]{1,0:T(8,128)(2,1)S(1)} %get-tuple-element.41), channel_id=1, source_target_pairs={{0,1},{1,0},{2,3},{3,2},{4,12},{5,13},{6,14},{7,15},{8,9},{9,8},{1... | collective-permute-start | bytes 221192 | tf_op jit(solution)/shard_map/ppermute | solution.py:369
  41.2 1.8 %collective-permute-done.9.refs_0_ = bf16[144,256]{1,0:T(8,128)(2,1)S(1)} collective-permute-done((bf16[144,256]{1,0:T(8,128)(2,1)S(1)}, bf16[144,256]{1,0:T(8,128)(2,1)S(1)}, u32[]{:S(2)}, u32[]{:S(2)}) %collective-permute-start.9) | collective-permute-done | bytes 73760 | tf_op jit(solution)/shard_map/ppermute | solution.py:369
  43.0 1.5 %collective-permute-done.10.refs_1_ = bf16[144,256]{1,0:T(8,128)(2,1)S(1)} collective-permute-done((bf16[144,256]{1,0:T(8,128)(2,1)S(1)}, bf16[144,256]{1,0:T(8,128)(2,1)S(1)}, u32[]{:S(2)}, u32[]{:S(2)}) %collective-permute-start.10) | collective-permute-done | bytes 73760 | tf_op jit(solution)/shard_map/ppermute | solution.py:369
  44.6 0.1 gain_part.1.mine_ref
  44.7 0.8 %collective-permute-start.12 = (f32[1,256]{1,0:T(1,128)S(1)}, f32[1,256]{1,0:T(1,128)S(1)}, u32[]{:S(2)}, u32[]{:S(2)}) collective-permute-start(f32[1,256]{1,0:T(1,128)S(1)} %gain_part.1.mine_ref), channel_id=1, source_target_pairs={{0,4},{4,0},{1,5},{5,1},{2,6},{6,2},{3,7},{7,3},{8,12},{12,8},{9,1... | collective-permute-start | bytes 3080 | tf_op jit(solution)/shard_map/ppermute | solution.py:448
  45.5 0.8 %finish.1 = f32[128,256]{1,0:T(8,128)} custom-call(bf16[1,128,256]{2,1,0:T(8,128)(2,1)S(1)} %get-tuple-element.23.refs_0_.hidden_ref, f32[16,1,256]{2,1,0:T(1,128)S(1)} %get-tuple-element.24.refs_4_.gain_ref, f32[128,128]{1,0:T(8,128)S(1)} %get-tuple-element.35.inverse_ref, f32[128,256]{1,0:T(8,128)S(1)} %get-tuple-element.37.own_ref, ...), custom_call_target="tpu_custom_call" | custom-call | bytes 65536 | tf_op jit(solution)/shard_map/finish/pallas_call | solution.py:333
  46.3 0.6 %add_gain.1 = f32[1,256]{1,0:T(1,128)} custom-call(f32[1,256]{1,0:T(1,128)S(1)} %gain_part.1.mine_ref, f32[1,256]{1,0:T(1,128)S(1)} %collective-permute-done.12.theirs_ref), custom_call_target="tpu_custom_call" | custom-call | tf_op jit(solution)/shard_map/add_gain/pallas_call | solution.py:348
  (12 shorter events, 0.1 us)
Async XLA Ops:
  0.6 8.2 %collective-permute-start = (bf16[1,128,256]{2,1,0:T(8,128)(2,1)}, bf16[1,128,256]{2,1,0:T(8,128)(2,1)S(1)}, u32[]{:S(2)}, u32[]{:S(2)}) collective-permute-start(bf16[1,128,256]{2,1,0:T(8,128)(2,1)} %refs_0_.1), channel_id=1, source_target_pairs={{0,3},{1,2},{2,1},{3,0},{4,28},{5,29},{6,30},{7,31},{8,11},{9,10},... | collective-permute-start | bytes 196616 | tf_op jit(solution)/shard_map/ppermute | solution.py:369
  5.7 5.4 %collective-permute-start.2 = (bf16[1,128,256]{2,1,0:T(8,128)(2,1)}, bf16[1,128,256]{2,1,0:T(8,128)(2,1)S(1)}, u32[]{:S(2)}, u32[]{:S(2)}) collective-permute-start(bf16[1,128,256]{2,1,0:T(8,128)(2,1)} %refs_0_.1), channel_id=1, source_target_pairs={{0,2},{1,3},{2,0},{3,1},{4,20},{5,21},{6,22},{7,23},{8,10},{9,11},... | collective-permute-start | bytes 196616 | tf_op jit(solution)/shard_map/ppermute | solution.py:369
  5.7 5.4 %collective-permute-start.1 = (bf16[1,128,256]{2,1,0:T(8,128)(2,1)}, bf16[1,128,256]{2,1,0:T(8,128)(2,1)S(1)}, u32[]{:S(2)}, u32[]{:S(2)}) collective-permute-start(bf16[1,128,256]{2,1,0:T(8,128)(2,1)} %refs_0_.1), channel_id=1, source_target_pairs={{0,1},{1,0},{2,3},{3,2},{4,12},{5,13},{6,14},{7,15},{8,9},{9,8},{1... | collective-permute-start | bytes 196616 | tf_op jit(solution)/shard_map/ppermute | solution.py:369
  11.1 7.4 %collective-permute-start.5 = (bf16[4,128,256]{2,1,0:T(8,128)(2,1)S(1)}, bf16[4,128,256]{2,1,0:T(8,128)(2,1)S(1)}, u32[]{:S(2)}, u32[]{:S(2)}) collective-permute-start(bf16[4,128,256]{2,1,0:T(8,128)(2,1)S(1)} %join.1.refs_0_), channel_id=1, source_target_pairs={{0,24},{1,25},{2,26},{3,27},{4,7},{5,6},{6,5},{7,4},{8,16},{9,17},... | collective-permute-start | bytes 786440 | tf_op jit(solution)/shard_map/ppermute | solution.py:369
  14.0 7.3 %collective-permute-start.4 = (bf16[4,128,256]{2,1,0:T(8,128)(2,1)S(1)}, bf16[4,128,256]{2,1,0:T(8,128)(2,1)S(1)}, u32[]{:S(2)}, u32[]{:S(2)}) collective-permute-start(bf16[4,128,256]{2,1,0:T(8,128)(2,1)S(1)} %join.1.refs_0_), channel_id=1, source_target_pairs={{0,16},{1,17},{2,18},{3,19},{4,6},{5,7},{6,4},{7,5},{8,24},{9,25},... | collective-permute-start | bytes 786440 | tf_op jit(solution)/shard_map/ppermute | solution.py:369
  14.5 6.9 %collective-permute-start.3 = (bf16[4,128,256]{2,1,0:T(8,128)(2,1)S(1)}, bf16[4,128,256]{2,1,0:T(8,128)(2,1)S(1)}, u32[]{:S(2)}, u32[]{:S(2)}) collective-permute-start(bf16[4,128,256]{2,1,0:T(8,128)(2,1)S(1)} %join.1.refs_0_), channel_id=1, source_target_pairs={{0,8},{1,9},{2,10},{3,11},{4,5},{5,4},{6,7},{7,6},{8,0},{9,1},{10,... | collective-permute-start | bytes 786440 | tf_op jit(solution)/shard_map/ppermute | solution.py:369
  14.7 6.7 %copy-start = (bf16[1,1,256,512]{3,2,1,0:T(8,128)(2,1)S(1)}, bf16[1,1,256,512]{3,2,1,0:T(8,128)(2,1)}, u32[]{:S(2)}) copy-start(bf16[1,1,256,512]{3,2,1,0:T(8,128)(2,1)} %param.10) | copy-start | bytes 786436
  14.7 6.7 %copy-start.1 = (bf16[1,1,256,512]{3,2,1,0:T(8,128)(2,1)S(1)}, bf16[1,1,256,512]{3,2,1,0:T(8,128)(2,1)}, u32[]{:S(2)}) copy-start(bf16[1,1,256,512]{3,2,1,0:T(8,128)(2,1)} %param.11) | copy-start | bytes 786436
  25.0 11.6 %collective-permute-start.6 = (bf16[544,256]{1,0:T(8,128)(2,1)S(1)}, bf16[544,256]{1,0:T(8,128)(2,1)S(1)}, u32[]{:S(2)}, u32[]{:S(2)}) collective-permute-start(bf16[544,256]{1,0:T(8,128)(2,1)S(1)} %project.5), channel_id=1, source_target_pairs={{0,24},{1,25},{2,26},{3,27},{4,7},{5,6},{6,5},{7,4},{8,16},{9,17},... | collective-permute-start | bytes 835592 | tf_op jit(solution)/shard_map/ppermute | solution.py:369
  27.9 7.6 %collective-permute-start.7 = (bf16[528,256]{1,0:T(8,128)(2,1)S(1)}, bf16[528,256]{1,0:T(8,128)(2,1)S(1)}, u32[]{:S(2)}, u32[]{:S(2)}) collective-permute-start(bf16[528,256]{1,0:T(8,128)(2,1)S(1)} %project.6), channel_id=1, source_target_pairs={{0,16},{1,17},{2,18},{3,19},{4,6},{5,7},{6,4},{7,5},{8,24},{9,25},... | collective-permute-start | bytes 811016 | tf_op jit(solution)/shard_map/ppermute | solution.py:369
  30.1 6.5 %collective-permute-start.8 = (bf16[528,256]{1,0:T(8,128)(2,1)S(1)}, bf16[528,256]{1,0:T(8,128)(2,1)S(1)}, u32[]{:S(2)}, u32[]{:S(2)}) collective-permute-start(bf16[528,256]{1,0:T(8,128)(2,1)S(1)} %project.7), channel_id=1, source_target_pairs={{0,8},{1,9},{2,10},{3,11},{4,5},{5,4},{6,7},{7,6},{8,0},{9,1},{10,... | collective-permute-start | bytes 811016 | tf_op jit(solution)/shard_map/ppermute | solution.py:369
  36.8 6.2 %collective-permute-start.9 = (bf16[144,256]{1,0:T(8,128)(2,1)S(1)}, bf16[144,256]{1,0:T(8,128)(2,1)S(1)}, u32[]{:S(2)}, u32[]{:S(2)}) collective-permute-start(bf16[144,256]{1,0:T(8,128)(2,1)S(1)} %get-tuple-element.39), channel_id=1, source_target_pairs={{0,3},{1,2},{2,1},{3,0},{4,28},{5,29},{6,30},{7,31},{8,11},{9,10},... | collective-permute-start | bytes 221192 | tf_op jit(solution)/shard_map/ppermute | solution.py:369
  38.3 6.3 %collective-permute-start.10 = (bf16[144,256]{1,0:T(8,128)(2,1)S(1)}, bf16[144,256]{1,0:T(8,128)(2,1)S(1)}, u32[]{:S(2)}, u32[]{:S(2)}) collective-permute-start(bf16[144,256]{1,0:T(8,128)(2,1)S(1)} %get-tuple-element.40), channel_id=1, source_target_pairs={{0,2},{1,3},{2,0},{3,1},{4,20},{5,21},{6,22},{7,23},{8,10},{9,11},... | collective-permute-start | bytes 221192 | tf_op jit(solution)/shard_map/ppermute | solution.py:369
  39.3 5.3 %collective-permute-start.11 = (bf16[144,256]{1,0:T(8,128)(2,1)S(1)}, bf16[144,256]{1,0:T(8,128)(2,1)S(1)}, u32[]{:S(2)}, u32[]{:S(2)}) collective-permute-start(bf16[144,256]{1,0:T(8,128)(2,1)S(1)} %get-tuple-element.41), channel_id=1, source_target_pairs={{0,1},{1,0},{2,3},{3,2},{4,12},{5,13},{6,14},{7,15},{8,9},{9,8},{1... | collective-permute-start | bytes 221192 | tf_op jit(solution)/shard_map/ppermute | solution.py:369
  44.7 1.7 %collective-permute-start.12 = (f32[1,256]{1,0:T(1,128)S(1)}, f32[1,256]{1,0:T(1,128)S(1)}, u32[]{:S(2)}, u32[]{:S(2)}) collective-permute-start(f32[1,256]{1,0:T(1,128)S(1)} %gain_part.1.mine_ref), channel_id=1, source_target_pairs={{0,4},{4,0},{1,5},{5,1},{2,6},{6,2},{3,7},{7,3},{8,12},{12,8},{9,1... | collective-permute-start | bytes 3080 | tf_op jit(solution)/shard_map/ppermute | solution.py:448

commit v6 on v5

--- a/solution.py
+++ b/solution.py
@@ -438,10 +438,13 @@
             enc_gain, (section * groups + mp) * own_columns, own_columns, 0
         ).reshape(1, 1, own_columns)
 
-    attended, query_grad = mix(low, values), mix(grad_low, keys)
+    attended = mix(low, values)
     first, *got = swap(2, chunks)
-    first, attended, query_grad = lax.optimization_barrier((first, attended, query_grad))
+    first, attended = lax.optimization_barrier((first, attended))
     own_total, *parts, tail = sum_chunks([first] + got[::-1], groups, rows, c_rows)
+    own_total, grad_low = lax.optimization_barrier((own_total, grad_low))
+    query_grad = mix(grad_low, keys)
+    own_total, query_grad = lax.optimization_barrier((own_total, query_grad))
     parts = swap(1, [own_total] + parts)[:0:-1]
     gain_own = gain_part(own_total, parts, hidden, inverse)
     if replicas == 2:

time: 47 us -> 47 us (level)
  no operation moved by 1% of the time
where the time goes in v6:
time: 47 us; the launch traced here: 46.9 us
  starting transfers between devices  18.3 us (39%)
  Pallas kernels  14.7 us (31%)
  waiting for transfers between devices  13.2 us (28%)
  between operations  0.72 us (2%)
    ppermute x12, starting transfers between devices, exchange(): return lax.ppermute(array, names, pairs)  17.4 us
    ppermute x12, waiting for transfers between devices, exchange(): return lax.ppermute(array, names, pairs)  13.2 us
    pallas_call x2, Pallas kernels, fetch(): pl.pallas_call(kernel, out_shape=tuple((pltpu.VMEM(array.shape, array.dty...  4.94 us
    pallas_call x4, Pallas kernels, project(): pl.pallas_call(kernel, out_shape=pltpu.VMEM((size, block), BF16), in_spec...  3.21 us
    pallas_call x1, Pallas kernels, attend(): pl.pallas_call(kernel, out_shape=(pltpu.VMEM((pairs, 2 * rows, length), B...  2.82 us
    pallas_call x2, Pallas kernels, mix(): pl.pallas_call(kernel, out_shape=jax.ShapeDtypeStruct((length, columns),...  2.1 us
  transfers between devices with their start and end apart: 13, of which 8 were waited for; matrix products, arithmetic and copies ran while one was open for 0% of the time, Pallas kernels for 22%

profile of v6, /device:TPU:0, one launch (start us, length us, event | category | flops | bytes accessed | tf_op | source)
XLA Modules:
  0.0 46.9 jit_solution(2303219001736404304)
XLA Ops:
  0.6 5.1 %collective-permute-start = (bf16[1,128,256]{2,1,0:T(8,128)(2,1)}, bf16[1,128,256]{2,1,0:T(8,128)(2,1)S(1)}, u32[]{:S(2)}, u32[]{:S(2)}) collective-permute-start(bf16[1,128,256]{2,1,0:T(8,128)(2,1)} %refs_0_.1), channel_id=1, source_target_pairs={{0,3},{1,2},{2,1},{3,0},{4,28},{5,29},{6,30},{7,31},{8,11},{9,10},... | collective-permute-start | bytes 196616 | tf_op jit(solution)/shard_map/ppermute | solution.py:369
  5.7 0.6 %collective-permute-start.1 = (bf16[1,128,256]{2,1,0:T(8,128)(2,1)}, bf16[1,128,256]{2,1,0:T(8,128)(2,1)S(1)}, u32[]{:S(2)}, u32[]{:S(2)}) collective-permute-start(bf16[1,128,256]{2,1,0:T(8,128)(2,1)} %refs_0_.1), channel_id=1, source_target_pairs={{0,1},{1,0},{2,3},{3,2},{4,12},{5,13},{6,14},{7,15},{8,9},{9,8},{1... | collective-permute-start | bytes 196616 | tf_op jit(solution)/shard_map/ppermute | solution.py:369
  6.4 2.5 %fetch.2 = (bf16[1,128,256]{2,1,0:T(8,128)(2,1)S(1)}, f32[16,1,256]{2,1,0:T(1,128)S(1)}, bf16[16,256,512]{2,1,0:T(8,128)(2,1)S(1)}) custom-call(bf16[1,128,256]{2,1,0:T(8,128)(2,1)} %refs_0_.1, f32[16,1,256]{2,1,0:T(1,128)} %bitcast.16, bf16[4096,512]{1,0:T(8,128)(2,1)} %bitcast.11), custom_call_target="tpu_custom_call" | custom-call | bytes 8388608 | tf_op jit(solution)/shard_map/fetch/pallas_call | solution.py:79
  8.9 2.2 %collective-permute-done.2.refs_3_ = bf16[1,128,256]{2,1,0:T(8,128)(2,1)S(1)} collective-permute-done((bf16[1,128,256]{2,1,0:T(8,128)(2,1)}, bf16[1,128,256]{2,1,0:T(8,128)(2,1)S(1)}, u32[]{:S(2)}, u32[]{:S(2)}) %collective-permute-start.2) | collective-permute-done | bytes 65568 | tf_op jit(solution)/shard_map/ppermute | solution.py:369
  11.1 2.9 %collective-permute-start.5 = (bf16[4,128,256]{2,1,0:T(8,128)(2,1)S(1)}, bf16[4,128,256]{2,1,0:T(8,128)(2,1)S(1)}, u32[]{:S(2)}, u32[]{:S(2)}) collective-permute-start(bf16[4,128,256]{2,1,0:T(8,128)(2,1)S(1)} %join.1.refs_0_), channel_id=1, source_target_pairs={{0,24},{1,25},{2,26},{3,27},{4,7},{5,6},{6,5},{7,4},{8,16},{9,17},... | collective-permute-start | bytes 786440 | tf_op jit(solution)/shard_map/ppermute | solution.py:369
  14.0 0.5 %collective-permute-start.4 = (bf16[4,128,256]{2,1,0:T(8,128)(2,1)S(1)}, bf16[4,128,256]{2,1,0:T(8,128)(2,1)S(1)}, u32[]{:S(2)}, u32[]{:S(2)}) collective-permute-start(bf16[4,128,256]{2,1,0:T(8,128)(2,1)S(1)} %join.1.refs_0_), channel_id=1, source_target_pairs={{0,16},{1,17},{2,18},{3,19},{4,6},{5,7},{6,4},{7,5},{8,24},{9,25},... | collective-permute-start | bytes 786440 | tf_op jit(solution)/shard_map/ppermute | solution.py:369
  14.5 0.2 collective-permute-start.3
  14.7 2.5 %fetch.3.refs_6_.wv_ref = bf16[16,256,512]{2,1,0:T(8,128)(2,1)S(1)} custom-call(bf16[4096,512]{1,0:T(8,128)(2,1)} %bitcast.12), custom_call_target="tpu_custom_call" | custom-call | bytes 8388608 | tf_op jit(solution)/shard_map/fetch/pallas_call | solution.py:79
  17.2 1.4 %collective-permute-done.5.refs_3_ = bf16[4,128,256]{2,1,0:T(8,128)(2,1)S(1)} collective-permute-done((bf16[4,128,256]{2,1,0:T(8,128)(2,1)S(1)}, bf16[4,128,256]{2,1,0:T(8,128)(2,1)S(1)}, u32[]{:S(2)}, u32[]{:S(2)}) %collective-permute-start.5) | collective-permute-done | bytes 262176 | tf_op jit(solution)/shard_map/ppermute | solution.py:369
  18.6 2.7 %collective-permute-done.4.refs_2_ = bf16[4,128,256]{2,1,0:T(8,128)(2,1)S(1)} collective-permute-done((bf16[4,128,256]{2,1,0:T(8,128)(2,1)S(1)}, bf16[4,128,256]{2,1,0:T(8,128)(2,1)S(1)}, u32[]{:S(2)}, u32[]{:S(2)}) %collective-permute-start.4) | collective-permute-done | bytes 262176 | tf_op jit(solution)/shard_map/ppermute | solution.py:369
  21.4 2.8 %attend.1 = (bf16[4,256,256]{2,1,0:T(8,128)(2,1)S(1)}, bf16[4,256,256]{2,1,0:T(8,128)(2,1)S(1)}, bf16[128,512]{1,0:T(8,128)(2,1)S(1)}, bf16[128,512]{1,0:T(8,128...) custom-call(bf16[4,128,256]{2,1,0:T(8,128)(2,1)S(1)} %join.1.refs_0_, ...), custom_call_target="tpu_custom_call" | custom-call | flops 1342177280 | bytes 16777216 | tf_op jit(solution)/shard_map/attend/pallas_call | solution.py:166
  24.2 0.8 %project.5 = bf16[544,256]{1,0:T(8,128)(2,1)S(1)} custom-call(bf16[128,512]{1,0:T(8,128)(2,1)S(1)} %get-tuple-element.29.kg_ref, bf16[128,512]{1,0:T(8,128)(2,1)S(1)} %get-tuple-element.30.vg_ref, bf16[16,256,512]{2,1,0:T(8,128)(2,1)S(1)} %get-tuple-element.28.refs_5_.wk_ref, bf16[16,256,512]{2,1,0:T(8,128)(2,1)S(1)} %fetch.3.refs_6_.wv_ref, ...), custom_call_target="tpu_custom_call" | custom-call | flops 1 | bytes 1 | tf_op jit(solution)/shard_map/project/pallas_call | solution.py:233
  25.0 2.0 %collective-permute-start.6 = (bf16[544,256]{1,0:T(8,128)(2,1)S(1)}, bf16[544,256]{1,0:T(8,128)(2,1)S(1)}, u32[]{:S(2)}, u32[]{:S(2)}) collective-permute-start(bf16[544,256]{1,0:T(8,128)(2,1)S(1)} %project.5), channel_id=1, source_target_pairs={{0,24},{1,25},{2,26},{3,27},{4,7},{5,6},{6,5},{7,4},{8,16},{9,17},... | collective-permute-start | bytes 835592 | tf_op jit(solution)/shard_map/ppermute | solution.py:369
  27.0 0.8 %project.6 = bf16[528,256]{1,0:T(8,128)(2,1)S(1)} custom-call(bf16[128,512]{1,0:T(8,128)(2,1)S(1)} %get-tuple-element.29.kg_ref, bf16[128,512]{1,0:T(8,128)(2,1)S(1)} %get-tuple-element.30.vg_ref, bf16[16,256,512]{2,1,0:T(8,128)(2,1)S(1)} %get-tuple-element.28.refs_5_.wk_ref, bf16[16,256,512]{2,1,0:T(8,128)(2,1)S(1)} %fetch.3.refs_6_.wv_ref, ...), custom_call_target="tpu_custom_call" | custom-call | flops 1 | bytes 1 | tf_op jit(solution)/shard_map/project/pallas_call | solution.py:233
  27.9 1.4 %collective-permute-start.7 = (bf16[528,256]{1,0:T(8,128)(2,1)S(1)}, bf16[528,256]{1,0:T(8,128)(2,1)S(1)}, u32[]{:S(2)}, u32[]{:S(2)}) collective-permute-start(bf16[528,256]{1,0:T(8,128)(2,1)S(1)} %project.6), channel_id=1, source_target_pairs={{0,16},{1,17},{2,18},{3,19},{4,6},{5,7},{6,4},{7,5},{8,24},{9,25},... | collective-permute-start | bytes 811016 | tf_op jit(solution)/shard_map/ppermute | solution.py:369
  29.3 0.8 %project.7 = bf16[528,256]{1,0:T(8,128)(2,1)S(1)} custom-call(bf16[128,512]{1,0:T(8,128)(2,1)S(1)} %get-tuple-element.29.kg_ref, bf16[128,512]{1,0:T(8,128)(2,1)S(1)} %get-tuple-element.30.vg_ref, bf16[16,256,512]{2,1,0:T(8,128)(2,1)S(1)} %get-tuple-element.28.refs_5_.wk_ref, bf16[16,256,512]{2,1,0:T(8,128)(2,1)S(1)} %fetch.3.refs_6_.wv_ref, ...), custom_call_target="tpu_custom_call" | custom-call | flops 1 | bytes 1 | tf_op jit(solution)/shard_map/project/pallas_call | solution.py:233
  30.1 0.2 collective-permute-start.8
  30.3 0.8 %project.4.refs_0_ = bf16[528,256]{1,0:T(8,128)(2,1)S(1)} custom-call(bf16[128,512]{1,0:T(8,128)(2,1)S(1)} %get-tuple-element.29.kg_ref, bf16[128,512]{1,0:T(8,128)(2,1)S(1)} %get-tuple-element.30.vg_ref, bf16[16,256,512]{2,1,0:T(8,128)(2,1)S(1)} %get-tuple-element.28.refs_5_.wk_ref, bf16[16,256,512]{2,1,0:T(8,128)(2,1)S(1)} %fetch.3.refs_6_.wv_ref, ...), custom_call_target="tpu_custom_call" | custom-call | flops 1 | bytes 1 | tf_op jit(solution)/shard_map/project/pallas_call | solution.py:233
  31.1 1.1 %mix.2 = bf16[256,512]{1,0:T(8,128)(2,1)} custom-call(bf16[4,256,256]{2,1,0:T(8,128)(2,1)S(1)} %get-tuple-element.32.shares_ref, bf16[128,512]{1,0:T(8,128)(2,1)S(1)} %get-tuple-element.33.weights_ref), custom_call_target="tpu_custom_call" | custom-call | flops 1 | bytes 1 | tf_op jit(solution)/shard_map/mix/pallas_call | solution.py:205
  32.2 3.3 %collective-permute-done.7.refs_2_ = bf16[528,256]{1,0:T(8,128)(2,1)S(1)} collective-permute-done((bf16[528,256]{1,0:T(8,128)(2,1)S(1)}, bf16[528,256]{1,0:T(8,128)(2,1)S(1)}, u32[]{:S(2)}, u32[]{:S(2)}) %collective-permute-start.7) | collective-permute-done | bytes 270368 | tf_op jit(solution)/shard_map/ppermute | solution.py:369
  35.5 1.2 %collective-permute-done.8.refs_3_ = bf16[528,256]{1,0:T(8,128)(2,1)S(1)} collective-permute-done((bf16[528,256]{1,0:T(8,128)(2,1)S(1)}, bf16[528,256]{1,0:T(8,128)(2,1)S(1)}, u32[]{:S(2)}, u32[]{:S(2)}) %collective-permute-start.8) | collective-permute-done | bytes 270368 | tf_op jit(solution)/shard_map/ppermute | solution.py:369
  36.6 0.1 sum_chunks.1
  36.8 1.5 %collective-permute-start.9 = (bf16[144,256]{1,0:T(8,128)(2,1)S(1)}, bf16[144,256]{1,0:T(8,128)(2,1)S(1)}, u32[]{:S(2)}, u32[]{:S(2)}) collective-permute-start(bf16[144,256]{1,0:T(8,128)(2,1)S(1)} %get-tuple-element.45), channel_id=1, source_target_pairs={{0,3},{1,2},{2,1},{3,0},{4,28},{5,29},{6,30},{7,31},{8,11},{9,10},... | collective-permute-start | bytes 221192 | tf_op jit(solution)/shard_map/ppermute | solution.py:369
  38.3 1.0 %collective-permute-start.10 = (bf16[144,256]{1,0:T(8,128)(2,1)S(1)}, bf16[144,256]{1,0:T(8,128)(2,1)S(1)}, u32[]{:S(2)}, u32[]{:S(2)}) collective-permute-start(bf16[144,256]{1,0:T(8,128)(2,1)S(1)} %get-tuple-element.46), channel_id=1, source_target_pairs={{0,2},{1,3},{2,0},{3,1},{4,20},{5,21},{6,22},{7,23},{8,10},{9,11},... | collective-permute-start | bytes 221192 | tf_op jit(solution)/shard_map/ppermute | solution.py:369
  39.3 1.9 %collective-permute-start.11 = (bf16[144,256]{1,0:T(8,128)(2,1)S(1)}, bf16[144,256]{1,0:T(8,128)(2,1)S(1)}, u32[]{:S(2)}, u32[]{:S(2)}) collective-permute-start(bf16[144,256]{1,0:T(8,128)(2,1)S(1)} %get-tuple-element.47), channel_id=1, source_target_pairs={{0,1},{1,0},{2,3},{3,2},{4,12},{5,13},{6,14},{7,15},{8,9},{9,8},{1... | collective-permute-start | bytes 221192 | tf_op jit(solution)/shard_map/ppermute | solution.py:369
  41.2 1.1 %mix.3 = bf16[256,512]{1,0:T(8,128)(2,1)} custom-call(bf16[4,256,256]{2,1,0:T(8,128)(2,1)S(1)} %get-tuple-element.39.shares_ref, bf16[128,512]{1,0:T(8,128)(2,1)S(1)} %get-tuple-element.40.weights_ref), custom_call_target="tpu_custom_call" | custom-call | flops 1 | bytes 1 | tf_op jit(solution)/shard_map/mix/pallas_call | solution.py:205
  42.3 0.7 %collective-permute-done.9.refs_0_ = bf16[144,256]{1,0:T(8,128)(2,1)S(1)} collective-permute-done((bf16[144,256]{1,0:T(8,128)(2,1)S(1)}, bf16[144,256]{1,0:T(8,128)(2,1)S(1)}, u32[]{:S(2)}, u32[]{:S(2)}) %collective-permute-start.9) | collective-permute-done | bytes 73760 | tf_op jit(solution)/shard_map/ppermute | solution.py:369
  43.0 1.5 %collective-permute-done.10.refs_1_ = bf16[144,256]{1,0:T(8,128)(2,1)S(1)} collective-permute-done((bf16[144,256]{1,0:T(8,128)(2,1)S(1)}, bf16[144,256]{1,0:T(8,128)(2,1)S(1)}, u32[]{:S(2)}, u32[]{:S(2)}) %collective-permute-start.10) | collective-permute-done | bytes 73760 | tf_op jit(solution)/shard_map/ppermute | solution.py:369
  44.6 0.1 gain_part.1.mine_ref
  44.7 0.8 %collective-permute-start.12 = (f32[1,256]{1,0:T(1,128)S(1)}, f32[1,256]{1,0:T(1,128)S(1)}, u32[]{:S(2)}, u32[]{:S(2)}) collective-permute-start(f32[1,256]{1,0:T(1,128)S(1)} %gain_part.1.mine_ref), channel_id=1, source_target_pairs={{0,4},{4,0},{1,5},{5,1},{2,6},{6,2},{3,7},{7,3},{8,12},{12,8},{9,1... | collective-permute-start | bytes 3080 | tf_op jit(solution)/shard_map/ppermute | solution.py:451
  45.5 0.8 %finish.1 = f32[128,256]{1,0:T(8,128)} custom-call(bf16[1,128,256]{2,1,0:T(8,128)(2,1)S(1)} %get-tuple-element.26.refs_0_.hidden_ref, f32[16,1,256]{2,1,0:T(1,128)S(1)} %get-tuple-element.27.refs_4_.gain_ref, f32[128,128]{1,0:T(8,128)S(1)} %get-tuple-element.42.inverse_ref, f32[128,256]{1,0:T(8,128)S(1)} %get-tuple-element.43.own_ref, ...), custom_call_target="tpu_custom_call" | custom-call | bytes 65536 | tf_op jit(solution)/shard_map/finish/pallas_call | solution.py:333
  46.3 0.6 %add_gain.1 = f32[1,256]{1,0:T(1,128)} custom-call(f32[1,256]{1,0:T(1,128)S(1)} %gain_part.1.mine_ref, f32[1,256]{1,0:T(1,128)S(1)} %collective-permute-done.12.theirs_ref), custom_call_target="tpu_custom_call" | custom-call | tf_op jit(solution)/shard_map/add_gain/pallas_call | solution.py:348
  (12 shorter events, 0.1 us)
Async XLA Ops:
  0.6 8.2 %collective-permute-start = (bf16[1,128,256]{2,1,0:T(8,128)(2,1)}, bf16[1,128,256]{2,1,0:T(8,128)(2,1)S(1)}, u32[]{:S(2)}, u32[]{:S(2)}) collective-permute-start(bf16[1,128,256]{2,1,0:T(8,128)(2,1)} %refs_0_.1), channel_id=1, source_target_pairs={{0,3},{1,2},{2,1},{3,0},{4,28},{5,29},{6,30},{7,31},{8,11},{9,10},... | collective-permute-start | bytes 196616 | tf_op jit(solution)/shard_map/ppermute | solution.py:369
  5.7 5.4 %collective-permute-start.2 = (bf16[1,128,256]{2,1,0:T(8,128)(2,1)}, bf16[1,128,256]{2,1,0:T(8,128)(2,1)S(1)}, u32[]{:S(2)}, u32[]{:S(2)}) collective-permute-start(bf16[1,128,256]{2,1,0:T(8,128)(2,1)} %refs_0_.1), channel_id=1, source_target_pairs={{0,2},{1,3},{2,0},{3,1},{4,20},{5,21},{6,22},{7,23},{8,10},{9,11},... | collective-permute-start | bytes 196616 | tf_op jit(solution)/shard_map/ppermute | solution.py:369
  5.7 5.4 %collective-permute-start.1 = (bf16[1,128,256]{2,1,0:T(8,128)(2,1)}, bf16[1,128,256]{2,1,0:T(8,128)(2,1)S(1)}, u32[]{:S(2)}, u32[]{:S(2)}) collective-permute-start(bf16[1,128,256]{2,1,0:T(8,128)(2,1)} %refs_0_.1), channel_id=1, source_target_pairs={{0,1},{1,0},{2,3},{3,2},{4,12},{5,13},{6,14},{7,15},{8,9},{9,8},{1... | collective-permute-start | bytes 196616 | tf_op jit(solution)/shard_map/ppermute | solution.py:369
  11.1 7.4 %collective-permute-start.5 = (bf16[4,128,256]{2,1,0:T(8,128)(2,1)S(1)}, bf16[4,128,256]{2,1,0:T(8,128)(2,1)S(1)}, u32[]{:S(2)}, u32[]{:S(2)}) collective-permute-start(bf16[4,128,256]{2,1,0:T(8,128)(2,1)S(1)} %join.1.refs_0_), channel_id=1, source_target_pairs={{0,24},{1,25},{2,26},{3,27},{4,7},{5,6},{6,5},{7,4},{8,16},{9,17},... | collective-permute-start | bytes 786440 | tf_op jit(solution)/shard_map/ppermute | solution.py:369
  14.0 7.3 %collective-permute-start.4 = (bf16[4,128,256]{2,1,0:T(8,128)(2,1)S(1)}, bf16[4,128,256]{2,1,0:T(8,128)(2,1)S(1)}, u32[]{:S(2)}, u32[]{:S(2)}) collective-permute-start(bf16[4,128,256]{2,1,0:T(8,128)(2,1)S(1)} %join.1.refs_0_), channel_id=1, source_target_pairs={{0,16},{1,17},{2,18},{3,19},{4,6},{5,7},{6,4},{7,5},{8,24},{9,25},... | collective-permute-start | bytes 786440 | tf_op jit(solution)/shard_map/ppermute | solution.py:369
  14.5 6.9 %collective-permute-start.3 = (bf16[4,128,256]{2,1,0:T(8,128)(2,1)S(1)}, bf16[4,128,256]{2,1,0:T(8,128)(2,1)S(1)}, u32[]{:S(2)}, u32[]{:S(2)}) collective-permute-start(bf16[4,128,256]{2,1,0:T(8,128)(2,1)S(1)} %join.1.refs_0_), channel_id=1, source_target_pairs={{0,8},{1,9},{2,10},{3,11},{4,5},{5,4},{6,7},{7,6},{8,0},{9,1},{10,... | collective-permute-start | bytes 786440 | tf_op jit(solution)/shard_map/ppermute | solution.py:369
  14.7 6.7 %copy-start = (bf16[1,1,256,512]{3,2,1,0:T(8,128)(2,1)S(1)}, bf16[1,1,256,512]{3,2,1,0:T(8,128)(2,1)}, u32[]{:S(2)}) copy-start(bf16[1,1,256,512]{3,2,1,0:T(8,128)(2,1)} %param.10) | copy-start | bytes 786436
  14.7 6.7 %copy-start.1 = (bf16[1,1,256,512]{3,2,1,0:T(8,128)(2,1)S(1)}, bf16[1,1,256,512]{3,2,1,0:T(8,128)(2,1)}, u32[]{:S(2)}) copy-start(bf16[1,1,256,512]{3,2,1,0:T(8,128)(2,1)} %param.11) | copy-start | bytes 786436
  25.0 11.6 %collective-permute-start.6 = (bf16[544,256]{1,0:T(8,128)(2,1)S(1)}, bf16[544,256]{1,0:T(8,128)(2,1)S(1)}, u32[]{:S(2)}, u32[]{:S(2)}) collective-permute-start(bf16[544,256]{1,0:T(8,128)(2,1)S(1)} %project.5), channel_id=1, source_target_pairs={{0,24},{1,25},{2,26},{3,27},{4,7},{5,6},{6,5},{7,4},{8,16},{9,17},... | collective-permute-start | bytes 835592 | tf_op jit(solution)/shard_map/ppermute | solution.py:369
  27.9 7.6 %collective-permute-start.7 = (bf16[528,256]{1,0:T(8,128)(2,1)S(1)}, bf16[528,256]{1,0:T(8,128)(2,1)S(1)}, u32[]{:S(2)}, u32[]{:S(2)}) collective-permute-start(bf16[528,256]{1,0:T(8,128)(2,1)S(1)} %project.6), channel_id=1, source_target_pairs={{0,16},{1,17},{2,18},{3,19},{4,6},{5,7},{6,4},{7,5},{8,24},{9,25},... | collective-permute-start | bytes 811016 | tf_op jit(solution)/shard_map/ppermute | solution.py:369
  30.1 6.5 %collective-permute-start.8 = (bf16[528,256]{1,0:T(8,128)(2,1)S(1)}, bf16[528,256]{1,0:T(8,128)(2,1)S(1)}, u32[]{:S(2)}, u32[]{:S(2)}) collective-permute-start(bf16[528,256]{1,0:T(8,128)(2,1)S(1)} %project.7), channel_id=1, source_target_pairs={{0,8},{1,9},{2,10},{3,11},{4,5},{5,4},{6,7},{7,6},{8,0},{9,1},{10,... | collective-permute-start | bytes 811016 | tf_op jit(solution)/shard_map/ppermute | solution.py:369
  36.8 6.2 %collective-permute-start.9 = (bf16[144,256]{1,0:T(8,128)(2,1)S(1)}, bf16[144,256]{1,0:T(8,128)(2,1)S(1)}, u32[]{:S(2)}, u32[]{:S(2)}) collective-permute-start(bf16[144,256]{1,0:T(8,128)(2,1)S(1)} %get-tuple-element.45), channel_id=1, source_target_pairs={{0,3},{1,2},{2,1},{3,0},{4,28},{5,29},{6,30},{7,31},{8,11},{9,10},... | collective-permute-start | bytes 221192 | tf_op jit(solution)/shard_map/ppermute | solution.py:369
  38.3 6.3 %collective-permute-start.10 = (bf16[144,256]{1,0:T(8,128)(2,1)S(1)}, bf16[144,256]{1,0:T(8,128)(2,1)S(1)}, u32[]{:S(2)}, u32[]{:S(2)}) collective-permute-start(bf16[144,256]{1,0:T(8,128)(2,1)S(1)} %get-tuple-element.46), channel_id=1, source_target_pairs={{0,2},{1,3},{2,0},{3,1},{4,20},{5,21},{6,22},{7,23},{8,10},{9,11},... | collective-permute-start | bytes 221192 | tf_op jit(solution)/shard_map/ppermute | solution.py:369
  39.3 5.3 %collective-permute-start.11 = (bf16[144,256]{1,0:T(8,128)(2,1)S(1)}, bf16[144,256]{1,0:T(8,128)(2,1)S(1)}, u32[]{:S(2)}, u32[]{:S(2)}) collective-permute-start(bf16[144,256]{1,0:T(8,128)(2,1)S(1)} %get-tuple-element.47), channel_id=1, source_target_pairs={{0,1},{1,0},{2,3},{3,2},{4,12},{5,13},{6,14},{7,15},{8,9},{9,8},{1... | collective-permute-start | bytes 221192 | tf_op jit(solution)/shard_map/ppermute | solution.py:369
  44.7 1.7 %collective-permute-start.12 = (f32[1,256]{1,0:T(1,128)S(1)}, f32[1,256]{1,0:T(1,128)S(1)}, u32[]{:S(2)}, u32[]{:S(2)}) collective-permute-start(f32[1,256]{1,0:T(1,128)S(1)} %gain_part.1.mine_ref), channel_id=1, source_target_pairs={{0,4},{4,0},{1,5},{5,1},{2,6},{6,2},{3,7},{7,3},{8,12},{12,8},{9,1... | collective-permute-start | bytes 3080 | tf_op jit(solution)/shard_map/ppermute | solution.py:451
